TPU v7x, 128 devices: a whole 4x4x4 slice. The times are simulated.
128 devices in a mesh: img: 16 (over y, x), own: 8 (over z, core).
Axes of the slice: x: 4, y: 4, z: 4, core: 2. Of those that a mesh axis runs over, the one named last changes fastest.
Arguments:
- patches: bfloat16 [25088, 4608], P(('img', 'own')), may hold values from -6 to 6
- grads: bfloat16 [25088, 512], P(('img', 'own')), may hold values from -0.8984375 to 0.8984375
- basis_g: bfloat16 [512, 512], replicated, may hold values from -0.25 to 0.25
- basis_slots: bfloat16 [4608, 9216], P(None, 'own'), may hold values from -0.09375 to 0.09375
- col_counts: int32 [8], replicated, may hold values from 1 to 1152, 4608 in all
Outputs:
- corrections: float32 [4608, 512], P(('img', 'own'))
Inputs may be any that keep to these rules, and one draw needn't show every extreme that they name: `col_counts`: the counts sum to 4608; one owner has exactly 1152.
All inputs are finite; a program needn't handle non-finite values.
Results may differ from a plain program's by a relative error of at most 0.00049.
Values may be sent and summed in bfloat16 or wider, within the bound.
No kernel may reach another device: no remote copies, remote signals or barrier semaphores. Data moves between devices by JAX's collectives and lax.ppermute only.
A program may use at most 128 MiB of HBM per device.

v0:
```python
import jax
import jax.numpy as jnp
from jax import lax
from jax.sharding import PartitionSpec as P

POS = 49


def shards(patches, grads, basis_g, basis_slots, col_counts):
    groups = lax.axis_size("img")
    owner_id = lax.axis_index("own")
    slots = basis_slots.shape[1]
    kin = basis_slots.shape[0]
    gout = basis_g.shape[1]
    proj_local = jnp.dot(grads, basis_g, preferred_element_type=jnp.float32).astype(jnp.bfloat16)
    proj_g = lax.all_gather(proj_local, "own", axis=0, tiled=True)
    proj_a = jnp.dot(
        lax.all_gather(patches, "own", axis=0, tiled=True),
        basis_slots,
        preferred_element_type=jnp.float32,
    ).astype(jnp.bfloat16)
    images_here = proj_a.shape[0] // POS
    coef = jnp.einsum(
        "nps,npg->nsg",
        proj_a.reshape(images_here, POS, slots),
        proj_g.reshape(images_here, POS, gout),
        preferred_element_type=jnp.float32,
    )
    total_images = images_here * groups
    slot_corr = jnp.sum(coef * coef, axis=0) / jnp.float32(total_images)
    starts = jnp.cumsum(col_counts) - col_counts
    my_count = lax.dynamic_index_in_dim(col_counts, owner_id, keepdims=False)
    my_start = lax.dynamic_index_in_dim(starts, owner_id, keepdims=False)
    slot_index = jnp.arange(slots, dtype=jnp.int32)
    masked = jnp.where((slot_index < my_count)[:, None], slot_corr, jnp.float32(0.0))
    laid = lax.dynamic_update_slice(
        jnp.zeros((kin + slots, gout), jnp.float32), masked, (my_start, jnp.int32(0))
    )[:kin]
    return lax.psum_scatter(laid, ("img", "own"), scatter_dimension=0, tiled=True)


def solution(mesh):
    in_specs = (P(("img", "own"), None), P(("img", "own"), None), P(), P(None, "own"), P())
    out_specs = P(("img", "own"), None)
    return jax.shard_map(shards, mesh=mesh, in_specs=in_specs, out_specs=out_specs, check_vma=False)
```

profile of v0, /device:TPU:12, one launch (start us, length us, event | category | flops | bytes accessed | tf_op | source)
XLA Modules:
  0.0 612.0 jit_solution(12443474549382979716)
XLA Ops:
  16.1 20.4 %all-gather.7.cloned.1.call-done = bf16[8,196,512]{2,1,0:T(8,128)(2,1)} async-done(((bf16[1,196,512]{2,1,0:T(8,128)(2,1)}), bf16[8,196,512]{2,1,0:T(8,128)(2,1)}) %all-gather.7.cloned.1.call-update) | async-done | bytes 1605648 | tf_op jit(solution)/shard_map/all_gather | solution.py:16
  36.5 2.4 reshape.37
  38.9 76.0 %all-gather.5.cloned.1.call-done = bf16[8,196,4608]{2,1,0:T(8,128)(2,1)} async-done(((bf16[1,196,4608]{2,1,0:T(8,128)(2,1)}), bf16[8,196,4608]{2,1,0:T(8,128)(2,1)}) %all-gather.5.cloned.1.call-update) | async-done | bytes 14450704 | tf_op jit(solution)/shard_map/all_gather | solution.py:18
  115.0 11.2 %reshape.41 = bf16[1568,4608]{1,0:T(8,128)(2,1)} reshape(bf16[8,196,4608]{2,1,0:T(8,128)(2,1)} %all-gather.5.cloned.1.call-done) | data formatting | bytes 28901376
  126.2 25.3 %convolution_convert_fusion = bf16[1568,1152]{1,0:T(8,128)(2,1)} fusion(bf16[1568,4608]{1,0:T(8,128)(2,1)} %reshape.41, bf16[4608,1152]{1,0:T(8,128)(2,1)} %param.8), kind=kOutput, calls=%fused_computation.1 | convolution fusion | flops 16648998912 | bytes 28680192 | tf_op jit(solution)/shard_map/dot_general | solution.py:17
  151.5 5.0 reshape.36
  156.5 12.9 %multiply_reduce_fusion = f32[1152,512]{1,0:T(8,128)S(1)} fusion(bf16[32,49,1152]{2,1,0:T(8,128)(2,1)} %reshape.36, bf16[32,49,512]{2,1,0:T(8,128)(2,1)S(1)} %reshape.37), kind=kOutput, calls=%fused_computation | convolution fusion | flops 1886846976 | bytes 7577600 | tf_op jit(solution)/shard_map/nps,npg->nsg/dot_general | solution.py:23
  169.8 5.9 broadcast_in_dim.16
  175.6 7.0 %dynamic_update_slice.3 = f32[5760,512]{1,0:T(8,128)} dynamic-update-slice(f32[5760,512]{1,0:T(8,128)} %broadcast_in_dim.16, f32[1152,512]{1,0:T(8,128)S(1)} %multiply_select_fusion, s32[]{:T(128)S(6)} %select_n.14, s32[]{:T(128)} %constant.20.clone.1) | dynamic-update-slice | bytes 4718596 | tf_op jit(solution)/shard_map/dynamic_update_slice | solution.py:36
  182.7 8.4 %slice.4 = f32[4608,512]{1,0:T(8,128)} slice(f32[5760,512]{1,0:T(8,128)} %dynamic_update_slice.3), slice={[0:4608], [0:512]} | slice | bytes 18874368 | tf_op jit(solution)/shard_map/slice | solution.py:36
  191.0 277.9 %fusion = f32[40,512]{1,0:T(8,128)S(1)} fusion(f32[4608,512]{1,0:T(8,128)} %slice.4), kind=kCustom, calls=%all-reduce-scatter | all-reduce-scatter fusion | flops 2621441 | bytes 9519104
  469.0 4.6 collective-permute-start
  473.6 8.9 %collective-permute-start.1 = (f32[40,512]{1,0:T(8,128)S(1)}, f32[40,512]{1,0:T(8,128)S(1)}, u32[]{:S(2)}, u32[]{:S(2)}) collective-permute-start(f32[40,512]{1,0:T(8,128)S(1)} %fusion), channel_id=1, source_target_pairs={{0,2},{1,3},{2,4},{3,5},{4,6},{5,7},{6,8},{7,9},{8,10},{9,11},{10,... | collective-permute-start | bytes 245768
  482.5 44.6 %collective-permute-start.12 = (f32[28,512]{1,0:T(8,128)S(1)}, f32[28,512]{1,0:T(8,128)S(1)}, u32[]{:S(2)}, u32[]{:S(2)}) collective-permute-start(f32[28,512]{1,0:T(8,128)S(1)} %slice.5), channel_id=1, source_target_pairs={{0,13},{1,14},{2,15},{3,16},{4,17},{5,18},{6,19},{7,20},{8,21},{9,... | collective-permute-start | bytes 172040
  527.1 1.9 collective-permute-start.10
  529.0 1.9 collective-permute-start.11
  531.0 1.9 collective-permute-start.2
  532.9 2.2 collective-permute-start.3
  535.1 11.7 %collective-permute-start.4 = (f32[40,512]{1,0:T(8,128)S(1)}, f32[40,512]{1,0:T(8,128)S(1)}, u32[]{:S(2)}, u32[]{:S(2)}) collective-permute-start(f32[40,512]{1,0:T(8,128)S(1)} %fusion), channel_id=1, source_target_pairs={{0,5},{1,6},{2,7},{3,8},{4,9},{5,10},{6,11},{7,12},{8,13},{9,14},{... | collective-permute-start | bytes 245768
  546.9 1.9 collective-permute-start.5
  548.8 2.5 collective-permute-start.6
  551.3 15.8 %collective-permute-start.7 = (f32[40,512]{1,0:T(8,128)S(1)}, f32[40,512]{1,0:T(8,128)S(1)}, u32[]{:S(2)}, u32[]{:S(2)}) collective-permute-start(f32[40,512]{1,0:T(8,128)S(1)} %fusion), channel_id=1, source_target_pairs={{0,8},{1,9},{2,10},{3,11},{4,12},{5,13},{6,14},{7,15},{8,16},{9,17... | collective-permute-start | bytes 245768
  567.1 25.6 %collective-permute-start.8 = (f32[40,512]{1,0:T(8,128)S(1)}, f32[40,512]{1,0:T(8,128)S(1)}, u32[]{:S(2)}, u32[]{:S(2)}) collective-permute-start(f32[40,512]{1,0:T(8,128)S(1)} %fusion), channel_id=1, source_target_pairs={{0,9},{1,10},{2,11},{3,12},{4,13},{5,14},{6,15},{7,16},{8,17},{9,1... | collective-permute-start | bytes 245768
  594.8 7.9 %collective-permute-done.9 = f32[40,512]{1,0:T(8,128)S(1)} collective-permute-done((f32[40,512]{1,0:T(8,128)S(1)}, f32[40,512]{1,0:T(8,128)S(1)}, u32[]{:S(2)}, u32[]{:S(2)}) %collective-permute-start.9) | collective-permute-done | bytes 81952
  (31 shorter events, 12.6 us)
Async XLA Ops:
  6.5 1.0 copy-start
  6.5 30.0 %all-gather.7.cloned.1.call-start = ((), (), s32[]{:S(2)}) async-start(), calls=%async_computation.1 | async-start | bytes 1843200 | tf_op jit(solution)/shard_map/all_gather | solution.py:16
  9.5 105.5 %all-gather.5.cloned.1.call-start = ((), (), s32[]{:S(2)}) async-start(), calls=%async_computation | async-start | bytes 16588800 | tf_op jit(solution)/shard_map/all_gather | solution.py:18
  182.7 422.5 %copy-start.1 = (bf16[512,512]{1,0:T(8,128)(2,1)S(1)}, bf16[512,512]{1,0:T(8,128)(2,1)}, u32[]{:S(2)}) copy-start(bf16[512,512]{1,0:T(8,128)(2,1)} %param.7) | copy-start | bytes 1572868
  469.0 63.9 %collective-permute-start = (f32[40,512]{1,0:T(8,128)S(1)}, f32[40,512]{1,0:T(8,128)S(1)}, u32[]{:S(2)}, u32[]{:S(2)}) collective-permute-start(f32[40,512]{1,0:T(8,128)S(1)} %fusion), channel_id=1, source_target_pairs={{0,1},{1,2},{2,3},{3,4},{4,5},{5,6},{6,7},{7,8},{8,9},{9,10},{10,1... | collective-permute-start | bytes 245768
  473.6 61.6 %collective-permute-start.1 = (f32[40,512]{1,0:T(8,128)S(1)}, f32[40,512]{1,0:T(8,128)S(1)}, u32[]{:S(2)}, u32[]{:S(2)}) collective-permute-start(f32[40,512]{1,0:T(8,128)S(1)} %fusion), channel_id=1, source_target_pairs={{0,2},{1,3},{2,4},{3,5},{4,6},{5,7},{6,8},{7,9},{8,10},{9,11},{10,... | collective-permute-start | bytes 245768
  482.5 48.5 %collective-permute-start.12 = (f32[28,512]{1,0:T(8,128)S(1)}, f32[28,512]{1,0:T(8,128)S(1)}, u32[]{:S(2)}, u32[]{:S(2)}) collective-permute-start(f32[28,512]{1,0:T(8,128)S(1)} %slice.5), channel_id=1, source_target_pairs={{0,13},{1,14},{2,15},{3,16},{4,17},{5,18},{6,19},{7,20},{8,21},{9,... | collective-permute-start | bytes 172040
  527.1 19.8 %collective-permute-start.10 = (f32[40,512]{1,0:T(8,128)S(1)}, f32[40,512]{1,0:T(8,128)S(1)}, u32[]{:S(2)}, u32[]{:S(2)}) collective-permute-start(f32[40,512]{1,0:T(8,128)S(1)} %fusion), channel_id=1, source_target_pairs={{0,11},{1,12},{2,13},{3,14},{4,15},{5,16},{6,17},{7,18},{8,19},{9,... | collective-permute-start | bytes 245768
  529.0 19.8 %collective-permute-start.11 = (f32[40,512]{1,0:T(8,128)S(1)}, f32[40,512]{1,0:T(8,128)S(1)}, u32[]{:S(2)}, u32[]{:S(2)}) collective-permute-start(f32[40,512]{1,0:T(8,128)S(1)} %fusion), channel_id=1, source_target_pairs={{0,12},{1,13},{2,14},{3,15},{4,16},{5,17},{6,18},{7,19},{8,20},{9,... | collective-permute-start | bytes 245768
  531.0 20.3 %collective-permute-start.2 = (f32[40,512]{1,0:T(8,128)S(1)}, f32[40,512]{1,0:T(8,128)S(1)}, u32[]{:S(2)}, u32[]{:S(2)}) collective-permute-start(f32[40,512]{1,0:T(8,128)S(1)} %fusion), channel_id=1, source_target_pairs={{0,3},{1,4},{2,5},{3,6},{4,7},{5,8},{6,9},{7,10},{8,11},{9,12},{10... | collective-permute-start | bytes 245768
  532.9 34.2 %collective-permute-start.3 = (f32[40,512]{1,0:T(8,128)S(1)}, f32[40,512]{1,0:T(8,128)S(1)}, u32[]{:S(2)}, u32[]{:S(2)}) collective-permute-start(f32[40,512]{1,0:T(8,128)S(1)} %fusion), channel_id=1, source_target_pairs={{0,4},{1,5},{2,6},{3,7},{4,8},{5,9},{6,10},{7,11},{8,12},{9,13},{1... | collective-permute-start | bytes 245768
  535.1 57.6 %collective-permute-start.4 = (f32[40,512]{1,0:T(8,128)S(1)}, f32[40,512]{1,0:T(8,128)S(1)}, u32[]{:S(2)}, u32[]{:S(2)}) collective-permute-start(f32[40,512]{1,0:T(8,128)S(1)} %fusion), channel_id=1, source_target_pairs={{0,5},{1,6},{2,7},{3,8},{4,9},{5,10},{6,11},{7,12},{8,13},{9,14},{... | collective-permute-start | bytes 245768
  546.9 47.8 %collective-permute-start.5 = (f32[40,512]{1,0:T(8,128)S(1)}, f32[40,512]{1,0:T(8,128)S(1)}, u32[]{:S(2)}, u32[]{:S(2)}) collective-permute-start(f32[40,512]{1,0:T(8,128)S(1)} %fusion), channel_id=1, source_target_pairs={{0,6},{1,7},{2,8},{3,9},{4,10},{5,11},{6,12},{7,13},{8,14},{9,15},... | collective-permute-start | bytes 245768
  548.8 45.8 %collective-permute-start.6 = (f32[40,512]{1,0:T(8,128)S(1)}, f32[40,512]{1,0:T(8,128)S(1)}, u32[]{:S(2)}, u32[]{:S(2)}) collective-permute-start(f32[40,512]{1,0:T(8,128)S(1)} %fusion), channel_id=1, source_target_pairs={{0,7},{1,8},{2,9},{3,10},{4,11},{5,12},{6,13},{7,14},{8,15},{9,16}... | collective-permute-start | bytes 245768
  551.3 43.4 %collective-permute-start.7 = (f32[40,512]{1,0:T(8,128)S(1)}, f32[40,512]{1,0:T(8,128)S(1)}, u32[]{:S(2)}, u32[]{:S(2)}) collective-permute-start(f32[40,512]{1,0:T(8,128)S(1)} %fusion), channel_id=1, source_target_pairs={{0,8},{1,9},{2,10},{3,11},{4,12},{5,13},{6,14},{7,15},{8,16},{9,17... | collective-permute-start | bytes 245768
  567.1 27.6 %collective-permute-start.8 = (f32[40,512]{1,0:T(8,128)S(1)}, f32[40,512]{1,0:T(8,128)S(1)}, u32[]{:S(2)}, u32[]{:S(2)}) collective-permute-start(f32[40,512]{1,0:T(8,128)S(1)} %fusion), channel_id=1, source_target_pairs={{0,9},{1,10},{2,11},{3,12},{4,13},{5,14},{6,15},{7,16},{8,17},{9,1... | collective-permute-start | bytes 245768
  592.7 9.9 %collective-permute-start.9 = (f32[40,512]{1,0:T(8,128)S(1)}, f32[40,512]{1,0:T(8,128)S(1)}, u32[]{:S(2)}, u32[]{:S(2)}) collective-permute-start(f32[40,512]{1,0:T(8,128)S(1)} %fusion), channel_id=1, source_target_pairs={{0,10},{1,11},{2,12},{3,13},{4,14},{5,15},{6,16},{7,17},{8,18},{9,... | collective-permute-start | bytes 245768
Sparse Core Ops, SparseCore 0:
  9.6 26.8 all-gather.6
  38.2 76.7 all-gather.4
where the time goes:
time: 613 us; the launch traced here: 612 us
  blocking collectives  278 us (45%)
  starting transfers between devices  126 us (21%)
  waiting for transfers between devices  105 us (17%)
  local copies, waits for them, and re-layouts  45.2 us (7%)
  matrix products  40.2 us (7%)
  between operations  15.5 us (3%)
    unnamed x1, blocking collectives  278 us
    unnamed x13, starting transfers between devices  125 us
    all_gather x1, waiting for transfers between devices, shards(): lax.all_gather(patches, 'own', axis=0, tiled=True)  76 us
    dot_general x1, matrix products, shards(): jnp.dot(lax.all_gather(patches, 'own', axis=0, tiled=True), basis_slots,...  25.3 us
    all_gather x1, waiting for transfers between devices, shards(): proj_g = lax.all_gather(proj_local, 'own', axis=0, tiled=True)  20.4 us
    unnamed x8, local copies, waits for them, and re-layouts  14.7 us
    dot_general x1, matrix products, shards(): jnp.einsum('nps,npg->nsg', proj_a.reshape(images_here, POS, slots), proj_...  12.9 us
  transfers between devices with their start and end apart: 15, of which 4 were waited for; matrix products, arithmetic and copies ran while one was open for 1% of the time, Pallas kernels for 0%

commit v1 on v0

v1 whole, which is shorter than its diff:
```python
import jax
import jax.numpy as jnp
from jax import lax
from jax.sharding import PartitionSpec as P

POS = 49


def shards(patches, grads, basis_g, basis_slots, col_counts):
    groups = lax.axis_size("img")
    owners = lax.axis_size("own")
    img = lax.axis_index("img")
    own = lax.axis_index("own")
    f32, bf16, i32 = jnp.float32, jnp.bfloat16, jnp.int32
    rows = patches.shape[0]
    kin, cap = basis_slots.shape
    gout = basis_g.shape[1]
    blk = kin // (groups * owners)
    stripe = blk * owners
    ring = -(-cap // stripe) * stripe
    per = ring // owners
    cols = blk * groups
    depth = kin // groups
    starts = jnp.cumsum(col_counts) - col_counts
    my_count = col_counts[own]
    my_start = starts[own]

    proj = jnp.dot(grads, basis_g, preferred_element_type=f32).astype(bf16)
    everything = lax.all_gather(jnp.concatenate([patches, proj], axis=1), "own", axis=0)

    piece = lax.dynamic_slice(basis_slots, (img * depth, jnp.int32(0)), (depth, cap))
    slot = jnp.arange(cap, dtype=i32)
    place = (my_start + slot) % ring
    place = (place % stripe) // blk * per + place // stripe * blk + place % blk
    send = (jnp.arange(ring, dtype=i32)[:, None] == place[None, :]) & (slot < my_count)[None, :]
    outgoing = lax.dot_general(
        send.astype(bf16), piece, (((1,), (1,)), ((), ())), preferred_element_type=f32
    ).astype(bf16)
    incoming = lax.all_to_all(outgoing.reshape(owners, per, depth), "own", 0, 0, tiled=True)
    spot = jnp.arange(per, dtype=i32)
    at = spot // blk * stripe + own * blk + spot % blk
    offset = (at[None, :] - starts[:, None]) % ring
    column = starts[:, None] + offset
    target = jnp.where(offset < col_counts[:, None], column // stripe * blk + column % blk, -1)
    keep = target.reshape(ring)[:, None] == jnp.arange(cols, dtype=i32)[None, :]
    mine = lax.dot_general(
        incoming.reshape(ring, depth), keep.astype(bf16), (((0,), (0,)), ((), ())), preferred_element_type=f32
    ).astype(bf16)
    basis = lax.all_gather(mine, "img", axis=0, tiled=True)

    proj_a = jnp.einsum("drk,kc->drc", everything[:, :, :kin], basis, preferred_element_type=f32).astype(bf16)
    images = owners * rows // POS
    coef = jnp.einsum(
        "nps,npg->nsg",
        proj_a.reshape(images, POS, cols),
        everything[:, :, kin:].reshape(images, POS, gout),
        preferred_element_type=f32,
    )
    total = jnp.sum(coef * coef, axis=0)
    parts = lax.all_to_all(total.reshape(groups, blk, gout), "img", 0, 0, tiled=True)
    return jnp.sum(parts, axis=0) / f32(images * groups)


def solution(mesh):
    in_specs = (P(("img", "own"), None), P(("img", "own"), None), P(), P(None, "own"), P())
    out_specs = P(("img", "own"), None)
    return jax.shard_map(shards, mesh=mesh, in_specs=in_specs, out_specs=out_specs, check_vma=False)
```

time: 613 us -> 230 us (0.38)
  the two profiles are of different devices: /device:TPU:12 before, /device:TPU:0 now
where the time goes in v1:
time: 230 us; the launch traced here: 229 us
  waiting for transfers between devices  138 us (60%)
  matrix products  30.9 us (13%)
  blocking collectives  25 us (11%)
  between operations  13.5 us (6%)
  local copies, waits for them, and re-layouts  10.9 us (5%)
  starting transfers between devices  5.44 us (2%)
  other arithmetic  5.33 us (2%)
    all_gather x1, waiting for transfers between devices, shards(): basis = lax.all_gather(mine, 'img', axis=0, tiled=True)  58.1 us
    all_gather x1, waiting for transfers between devices, shards(): lax.all_gather(jnp.concatenate([patches, proj], axis=1), 'own', axis=0)  57.9 us
    all_to_all x1, blocking collectives, shards(): lax.all_to_all(total.reshape(groups, blk, gout), 'img', 0, 0, tiled=True)  25 us
    all_to_all x1, waiting for transfers between devices, shards(): lax.all_to_all(outgoing.reshape(owners, per, depth), 'own', 0, 0, tiled=T...  21.9 us
    dot_general x1, matrix products, shards(): jnp.einsum('drk,kc->drc', everything[:, :, :kin], basis, preferred_elemen...  17.6 us
    dot_general x1, matrix products, shards(): jnp.einsum('nps,npg->nsg', proj_a.reshape(images, POS, cols), everything[...  7.89 us
    all_to_all x1, starting transfers between devices, shards(): lax.all_to_all(outgoing.reshape(owners, per, depth), 'own', 0, 0, tiled=T...  5.4 us
  transfers between devices with their start and end apart: 3, of which 3 were waited for; matrix products, arithmetic and copies ran while one was open for 4% of the time, Pallas kernels for 0%

profile of v1, /device:TPU:0, one launch (start us, length us, event | category | flops | bytes accessed | tf_op | source)
XLA Modules:
  0.0 229.0 jit_solution(298658799918011712)
XLA Ops:
  6.5 1.0 copy-done
  7.6 1.2 convolution_convert_fusion
  8.8 3.1 %maximum_bitcast_fusion = bf16[1,196,5120]{2,1,0:T(8,128)(2,1)} fusion(bf16[196,512]{1,0:T(8,128)(2,1)S(1)} %convolution_convert_fusion, bf16[196,4608]{1,0:T(8,128)(2,1)} %param.5), kind=kLoop, calls=%fused_computation.12 | loop fusion | flops 4014080 | bytes 4014080
  11.9 0.6 dynamic_slice.10
  12.5 0.2 reduce-window.9
  12.7 0.6 dynamic_slice.9
  13.3 0.6 iota_compare_fusion.5
  13.9 0.7 fusion.22
  14.6 2.6 %fusion.9 = bf16[1152,288]{0,1:T(8,128)(2,1)S(1)} fusion(s32[1152]{0:T(1024)S(1)} %fusion.22, pred[1152]{0:T(1024)(128)(4,1)S(1)} %iota_compare_fusion.5, bf16[4608,1152]{1,0:T(8,128)(2,1)} %param.8, s32[]{:T(128)S(6)} %select_n.110), kind=kOutput, calls=%fused_computation.11 | convolution fusion | flops 767397888 | bytes 1332868 | tf_op jit(solution)/shard_map/dot_general | solution.py:36
  17.2 1.2 copy.7
  18.4 5.4 %all-to-all-start = ((bf16[8,144,288]{2,1,0:T(8,128)(2,1)}), bf16[8,144,288]{2,1,0:T(8,128)(2,1)S(1)}, u32[]{:S(2)}, u32[]{:S(2)}) async-start(bf16[8,144,288]{2,1,0:T(8,128)(2,1)} %bitcast.5), calls=%async_computation | async-start | bytes 1769472 | tf_op jit(solution)/shard_map/all_to_all | solution.py:39
  24.3 21.9 %all-to-all-done = bf16[8,144,288]{2,1,0:T(8,128)(2,1)S(1)} async-done(((bf16[8,144,288]{2,1,0:T(8,128)(2,1)}), bf16[8,144,288]{2,1,0:T(8,128)(2,1)S(1)}, u32[]{:S(2)}, u32[]{:S(2)}) %all-to-all-start) | async-done | bytes 663584 | tf_op jit(solution)/shard_map/all_to_all | solution.py:39
  46.2 1.6 fusion.18
  47.8 57.9 %all-gather.7.cloned.1.call-done = bf16[8,196,5120]{2,1,0:T(8,128)(2,1)} async-done(((bf16[1,196,5120]{2,1,0:T(8,128)(2,1)}), bf16[8,196,5120]{2,1,0:T(8,128)(2,1)}) %all-gather.7.cloned.1.call-update) | async-done | bytes 16056336 | tf_op jit(solution)/shard_map/all_gather | solution.py:29
  105.7 1.4 slice-done
  107.1 1.5 reshape.162
  108.6 58.1 %all-gather.5.cloned.1.call-done = bf16[4608,576]{1,0:T(8,128)(2,1)} async-done(((bf16[288,576]{1,0:T(8,128)(2,1)}), bf16[4608,576]{1,0:T(8,128)(2,1)}) %all-gather.5.cloned.1.call-update) | async-done | bytes 5308432 | tf_op jit(solution)/shard_map/all_gather | solution.py:49
  166.7 17.6 %fusion.12 = bf16[8,196,576]{2,1,0:T(8,128)(2,1)} fusion(bf16[4608,576]{1,0:T(8,128)(2,1)} %all-gather.5.cloned.1.call-done, bf16[8,196,5120]{2,1,0:T(8,128)(2,1)} %all-gather.7.cloned.1.call-done), kind=kOutput, calls=%fused_computation.13 | convolution fusion | flops 8324499456 | bytes 22450176 | tf_op jit(solution)/shard_map/drk,kc->drc/dot_general | solution.py:51
  184.3 2.8 %reshape.161 = bf16[32,49,576]{2,1,0:T(8,128)(2,1)S(1)} reshape(bf16[8,196,576]{2,1,0:T(8,128)(2,1)} %fusion.12) | data formatting | bytes 3612672 | tf_op jit(solution)/shard_map/reshape | solution.py:55
  187.1 7.9 %multiply_reduce_fusion = f32[576,512]{1,0:T(8,128)} fusion(bf16[32,49,576]{2,1,0:T(8,128)(2,1)S(1)} %reshape.161, bf16[32,49,512]{2,1,0:T(8,128)(2,1)} %reshape.162), kind=kOutput, calls=%fused_computation | convolution fusion | flops 943423488 | bytes 4591616 | tf_op jit(solution)/shard_map/nps,npg->nsg/dot_general | solution.py:53
  195.0 1.4 reshape.163
  196.4 25.0 %all_to_all.10 = f32[16,36,512]{2,1,0:T(8,128)S(1)} all-to-all(f32[16,36,512]{2,1,0:T(8,128)S(1)} %reshape.163), channel_id=1, replica_groups=mesh['img'=16,'own'=8] {'img'}, dimensions={0} | all-to-all | bytes 2359296 | tf_op jit(solution)/shard_map/all_to_all | solution.py:60
  221.5 0.1 reduce_sum.19
  221.6 0.6 broadcast_multiply_fusion
  (17 shorter events, 0.5 us)
Async XLA Ops:
  6.5 1.0 copy-start
  6.5 99.2 %all-gather.7.cloned.1.call-start = ((), (), s32[]{:S(2)}) async-start(), calls=%async_computation.3 | async-start | bytes 18432000 | tf_op jit(solution)/shard_map/all_gather | solution.py:29
  8.8 3.1 %copy-start.1 = (s32[8]{0:T(128)S(1)}, s32[8]{0:T(128)}, u32[]{:S(2)}) copy-start(s32[8]{0:T(128)} %param.9) | copy-start | bytes 100
  18.4 27.8 %all-to-all-start = ((bf16[8,144,288]{2,1,0:T(8,128)(2,1)}), bf16[8,144,288]{2,1,0:T(8,128)(2,1)S(1)}, u32[]{:S(2)}, u32[]{:S(2)}) async-start(bf16[8,144,288]{2,1,0:T(8,128)(2,1)} %bitcast.5), calls=%async_computation | async-start | bytes 1769472 | tf_op jit(solution)/shard_map/all_to_all | solution.py:39
  23.8 142.9 %all-gather.5.cloned.1.call-start = ((), (), s32[]{:S(2)}) async-start(), calls=%async_computation.2 | async-start | bytes 6266880 | tf_op jit(solution)/shard_map/all_gather | solution.py:49
  105.7 1.4 slice-start
Sparse Core Ops, SparseCore 0:
  12.0 93.6 all-gather.6
  107.8 58.8 all-gather.4

commit v2 on v0

v2 whole, which is shorter than its diff:
```python
import functools

import jax
import jax.numpy as jnp
from jax import lax
from jax.experimental import pallas as pl
from jax.experimental.pallas import tpu as pltpu
from jax.sharding import PartitionSpec as P

POS = 49
CHIPS = 4
CORES = 2
F32, BF16, I32 = jnp.float32, jnp.bfloat16, jnp.int32


def accumulate(n, chunk, *refs):
    lows, highs = refs[:n], refs[n : 2 * n]
    basis, *before, total, low, high, held, flip, sems = refs[2 * n :]
    rows, half = low.shape[1:]
    kin, cols = held.shape
    rest = kin - half
    gout = half - rest
    first = pltpu.make_async_copy(basis.at[pl.ds(0, half)], held.at[pl.ds(0, half)], sems.at[0])
    second = pltpu.make_async_copy(basis.at[pl.ds(half, rest)], held.at[pl.ds(half, rest)], sems.at[1])
    lefts = [pltpu.make_async_copy(lows[k], low.at[k], sems.at[2 + 2 * k]) for k in range(n)]
    rights = [pltpu.make_async_copy(highs[k], high.at[k], sems.at[3 + 2 * k]) for k in range(n)]
    first.start()
    lefts[0].start()
    second.start()
    rights[0].start()
    image = lax.broadcasted_iota(I32, (rows, gout), 0) // POS
    for k in range(n):
        lefts[k].wait()
        if k == 0:
            first.wait()
        if k + 1 < n:
            lefts[k + 1].start()
            rights[k + 1].start()
        proj = jnp.dot(low[k], held[:half], preferred_element_type=F32)
        rights[k].wait()
        if k == 0:
            second.wait()
        proj += jnp.dot(high[k, :, :rest], held[half:], preferred_element_type=F32)
        flip[...] = proj.astype(BF16).T
        grads = high[k, :, rest:]
        apart = [jnp.where(image == m, grads, jnp.zeros_like(grads)) for m in range(rows // POS)]
        for s in range(0, cols, chunk):
            left = flip[s : s + chunk]
            source = (total if k else before[0] if before else None)
            squares = jnp.zeros((chunk, gout), F32) if source is None else source[s : s + chunk]
            for one in apart:
                coef = jnp.dot(left, one, preferred_element_type=F32)
                squares += coef * coef
            total[s : s + chunk] = squares


def added(lows, highs, basis, *before):
    n = len(lows)
    rows, half = lows[0].shape
    kin, cols = basis.shape
    gout = 2 * half - kin
    anywhere = pl.BlockSpec(memory_space=pl.ANY)
    return pl.pallas_call(
        functools.partial(accumulate, n, 80),
        out_shape=jax.ShapeDtypeStruct((cols, gout), F32),
        in_specs=[anywhere] * (2 * n + 1) + [pl.BlockSpec(memory_space=pltpu.VMEM)] * len(before),
        out_specs=pl.BlockSpec(memory_space=pltpu.VMEM),
        scratch_shapes=[
            pltpu.VMEM((n, rows, half), BF16),
            pltpu.VMEM((n, rows, half), BF16),
            pltpu.VMEM((kin, cols), BF16),
            pltpu.VMEM((cols, rows), BF16),
            pltpu.SemaphoreType.DMA((2 * n + 2,)),
        ],
        compiler_params=pltpu.CompilerParams(vmem_limit_bytes=60 << 20),
        cost_estimate=pl.CostEstimate(
            flops=2 * n * rows * kin * cols, bytes_accessed=4 * n * rows * half + 2 * kin * cols, transcendentals=0
        ),
    )(*lows, *highs, basis, *before)


def up(a, step):
    pairs = [(z * CORES + c, (z + step) % CHIPS * CORES + c) for z in range(CHIPS) for c in range(CORES)]
    return lax.ppermute(a, "own", pairs)


def swap(a):
    return lax.ppermute(a, "own", [(o, o ^ 1) for o in range(CHIPS * CORES)])


def balanced_basis(basis_slots, col_counts, img, own, groups, blk, wide):
    owners = CHIPS * CORES
    kin, cap = basis_slots.shape
    stripe = blk * owners
    ring = -(-cap // stripe) * stripe
    per = ring // owners
    depth = kin // groups
    starts = jnp.cumsum(col_counts) - col_counts
    z, c = own // CORES, own % CORES
    piece = lax.dynamic_slice(basis_slots, (img * depth, jnp.int32(0)), (depth, cap))
    slot = jnp.arange(cap, dtype=I32)
    place = (starts[own] + slot) % ring
    goal = place % stripe // blk
    hop = (goal // CORES - z) % CHIPS + CHIPS * ((goal % CORES) ^ c)
    place = jnp.where(slot < col_counts[own], hop * per + place // stripe * blk + place % blk, -1)
    send = jnp.arange(ring, dtype=I32)[:, None] == place[None, :]
    outgoing = lax.dot_general(send.astype(BF16), piece, (((1,), (1,)), ((), ())), preferred_element_type=F32)
    outgoing = outgoing.astype(BF16).reshape(CORES, CHIPS, per, depth)
    both = jnp.stack([outgoing[0], swap(outgoing[1])], axis=1)
    incoming = jnp.stack([both[0], up(both[1], 1), up(both[2], 2), up(both[3], -1)])
    source = ((z - jnp.arange(CHIPS, dtype=I32)) % CHIPS * CORES)[:, None] + (jnp.arange(CORES, dtype=I32) ^ c)[None, :]
    source = source.reshape(owners)
    begin, count = starts[source], col_counts[source]
    spot = jnp.arange(per, dtype=I32)
    at = spot // blk * stripe + own * blk + spot % blk
    offset = (at[None, :] - begin[:, None]) % ring
    column = begin[:, None] + offset
    target = jnp.where(offset < count[:, None], column // stripe * wide + column % blk, -1)
    keep = target.reshape(ring)[:, None] == jnp.arange(groups * wide, dtype=I32)[None, :]
    mine = lax.dot_general(
        incoming.reshape(ring, depth), keep.astype(BF16), (((0,), (0,)), ((), ())), preferred_element_type=F32
    )
    return lax.all_gather(mine.astype(BF16), "img", axis=0, tiled=True)


def gathered(low, high):
    low_down, high_up = up(low, 1), up(high, -1)
    low, high, low_down, high_up = lax.optimization_barrier((low, high, low_down, high_up))
    high_down, low_up = up(high, 1), up(low, -1)
    low_down, high_up, high_down, low_up = lax.optimization_barrier((low_down, high_up, high_down, low_up))
    low_far, high_far = up(low_down, 1), up(high_up, -1)
    lows, highs = [low, low_down, low_up, low_far], [high, high_down, high_up, high_far]
    lows = [b for a in lows for b in (a, swap(a))]
    highs = [b for a in highs for b in (a, swap(a))]
    return lows, highs


def shards(patches, grads, basis_g, basis_slots, col_counts):
    groups = lax.axis_size("img")
    owners = CHIPS * CORES
    img, own = lax.axis_index("img"), lax.axis_index("own")
    rows, kin = patches.shape
    gout = basis_g.shape[1]
    blk = kin // (groups * owners)
    proj = jnp.dot(grads, basis_g, preferred_element_type=F32).astype(BF16)
    half = (kin + gout) // 2
    low, high = patches[:, :half], jnp.concatenate([patches[:, half:], proj], axis=1)
    lows, highs = gathered(low, high)
    wide = -(-blk // 8) * 8
    basis = balanced_basis(basis_slots, col_counts, img, own, groups, blk, wide)
    near = len(lows) - CORES
    total = added(lows[:near], highs[:near], basis)
    total = added(lows[near:], highs[near:], basis, total)
    parts = lax.all_to_all(total.reshape(groups, wide, gout), "img", 0, 0, tiled=True)
    return jnp.sum(parts[:, :blk], axis=0) / F32(owners * rows // POS * groups)


def solution(mesh):
    in_specs = (P(("img", "own"), None), P(("img", "own"), None), P(), P(None, "own"), P())
    out_specs = P(("img", "own"), None)
    return jax.shard_map(shards, mesh=mesh, in_specs=in_specs, out_specs=out_specs, check_vma=False)
```

time: 613 us -> 188 us (0.31)
  the two profiles are of different devices: /device:TPU:12 before, /device:TPU:0 now
where the time goes in v2:
time: 188 us; the launch traced here: 187 us
  waiting for transfers between devices  78.1 us (42%)
  Pallas kernels  35 us (19%)
  blocking collectives  27.3 us (15%)
  starting transfers between devices  17.4 us (9%)
  between operations  13.8 us (7%)
  local copies, waits for them, and re-layouts  7.15 us (4%)
  matrix products  4.26 us (2%)
  other arithmetic  4.25 us (2%)
    ppermute x9, waiting for transfers between devices, up(): return lax.ppermute(a, 'own', pairs)  78.1 us
    pallas_call x2, Pallas kernels, added(): pl.pallas_call(functools.partial(accumulate, n, 80), out_shape=jax.ShapeD...  35 us
    all_to_all x1, blocking collectives, shards(): lax.all_to_all(total.reshape(groups, wide, gout), 'img', 0, 0, tiled=True)  27.3 us
    ppermute x9, starting transfers between devices, up(): return lax.ppermute(a, 'own', pairs)  15.4 us
  transfers between devices with their start and end apart: 19, of which 6 were waited for; matrix products, arithmetic and copies ran while one was open for 1% of the time, Pallas kernels for 12%

profile of v2, /device:TPU:0, one launch (start us, length us, event | category | flops | bytes accessed | tf_op | source)
XLA Modules:
  0.0 187.2 jit_solution(17775517856950301735)
XLA Ops:
  6.5 0.9 reduce-window.9
  8.1 1.3 dynamic_slice.9
  10.0 1.4 fusion.20
  11.3 2.3 %fusion.3 = bf16[1152,288]{0,1:T(8,128)(2,1)S(1)} fusion(s32[1152]{0:T(1024)S(1)} %fusion.20, bf16[4608,1152]{1,0:T(8,128)(2,1)} %param.8, s32[]{:T(128)S(6)} %select_n.178), kind=kOutput, calls=%fused_computation.7 | convolution fusion | flops 766070784 | bytes 1331716 | tf_op jit(solution)/shard_map/dot_general | solution.py:107
  16.6 4.0 %collective-permute-start.10 = (bf16[2,144,288]{2,1,0:T(8,128)(2,1)S(1)}, bf16[2,144,288]{2,1,0:T(8,128)(2,1)S(1)}, u32[]{:S(2)}, u32[]{:S(2)}) collective-permute-start(bf16[2,144,288]{2,1,0:T(8,128)(2,1)S(1)} %get-tuple-element.24), channel_id=1, source_target_pairs={{0,4},{1,5},{2,6},{3,7},{4,0},{5,1},{6,2},{7,3},{8,12},{9,13},{10,... | collective-permute-start | bytes 497672 | tf_op jit(solution)/shard_map/ppermute | solution.py:84
  20.6 0.7 collective-permute-start.11
  21.3 1.3 collective-permute-start.9
  22.7 4.2 %collective-permute-done.10 = bf16[2,144,288]{2,1,0:T(8,128)(2,1)S(1)} collective-permute-done((bf16[2,144,288]{2,1,0:T(8,128)(2,1)S(1)}, bf16[2,144,288]{2,1,0:T(8,128)(2,1)S(1)}, u32[]{:S(2)}, u32[]{:S(2)}) %collective-permute-start.10) | collective-permute-done | bytes 165920 | tf_op jit(solution)/shard_map/ppermute | solution.py:84
  26.9 5.3 %collective-permute-done.11 = bf16[2,144,288]{2,1,0:T(8,128)(2,1)S(1)} collective-permute-done((bf16[2,144,288]{2,1,0:T(8,128)(2,1)S(1)}, bf16[2,144,288]{2,1,0:T(8,128)(2,1)S(1)}, u32[]{:S(2)}, u32[]{:S(2)}) %collective-permute-start.11) | collective-permute-done | bytes 165920 | tf_op jit(solution)/shard_map/ppermute | solution.py:84
  32.4 1.7 fusion.5
  34.4 0.8 slice-done
  35.3 2.7 %collective-permute-start.1 = (bf16[196,2560]{1,0:T(8,128)(2,1)S(1)}, bf16[196,2560]{1,0:T(8,128)(2,1)S(1)}, u32[]{:S(2)}, u32[]{:S(2)}) collective-permute-start(bf16[196,2560]{1,0:T(8,128)(2,1)S(1)} %pad_maximum_fusion.refs_6_), channel_id=1, source_target_pairs={{0,6},{1,7},{2,0},{3,1},{4,2},{5,3},{6,4},{7,5},{8,14},{9,15},{10,... | collective-permute-start | bytes 3010568 | tf_op jit(solution)/shard_map/ppermute | solution.py:84
  38.2 21.8 %collective-permute-done.1.refs_10_ = bf16[196,2560]{1,0:T(8,128)(2,1)S(1)} collective-permute-done((bf16[196,2560]{1,0:T(8,128)(2,1)S(1)}, bf16[196,2560]{1,0:T(8,128)(2,1)S(1)}, u32[]{:S(2)}, u32[]{:S(2)}) %collective-permute-start.1) | collective-permute-done | bytes 1003552 | tf_op jit(solution)/shard_map/ppermute | solution.py:84
  60.1 3.6 %collective-permute-done.refs_2_ = bf16[196,2560]{1,0:T(8,128)(2,1)S(1)} collective-permute-done((bf16[196,2560]{1,0:T(8,128)(2,1)S(1)}, bf16[196,2560]{1,0:T(8,128)(2,1)S(1)}, u32[]{:S(2)}, u32[]{:S(2)}) %collective-permute-start) | collective-permute-done | bytes 1003552 | tf_op jit(solution)/shard_map/ppermute | solution.py:84
  63.6 3.2 %collective-permute-start.3 = (bf16[196,2560]{1,0:T(8,128)(2,1)S(1)}, bf16[196,2560]{1,0:T(8,128)(2,1)S(1)}, u32[]{:S(2)}, u32[]{:S(2)}) collective-permute-start(bf16[196,2560]{1,0:T(8,128)(2,1)S(1)} %slice.29.refs_0_), channel_id=1, source_target_pairs={{0,6},{1,7},{2,0},{3,1},{4,2},{5,3},{6,4},{7,5},{8,14},{9,15},{10,... | collective-permute-start | bytes 3010568 | tf_op jit(solution)/shard_map/ppermute | solution.py:84
  67.4 20.8 %collective-permute-done.2.refs_8_ = bf16[196,2560]{1,0:T(8,128)(2,1)S(1)} collective-permute-done((bf16[196,2560]{1,0:T(8,128)(2,1)S(1)}, bf16[196,2560]{1,0:T(8,128)(2,1)S(1)}, u32[]{:S(2)}, u32[]{:S(2)}) %collective-permute-start.2) | collective-permute-done | bytes 1003552 | tf_op jit(solution)/shard_map/ppermute | solution.py:84
  88.3 3.2 %collective-permute-start.6 = (bf16[196,2560]{1,0:T(8,128)(2,1)S(1)}, bf16[196,2560]{1,0:T(8,128)(2,1)S(1)}, u32[]{:S(2)}, u32[]{:S(2)}) collective-permute-start(bf16[196,2560]{1,0:T(8,128)(2,1)S(1)} %collective-permute-done.1.refs_10_), channel_id=1, source_target_pairs={{0,6},{1,7},{2,0},{3,1},{4,2},{5,3},{6,4},{7,5},{8,14},{9,15},{10,... | collective-permute-start | bytes 3010568 | tf_op jit(solution)/shard_map/ppermute | solution.py:84
  92.2 22.3 %collective-permute-done.4.refs_0_ = bf16[196,2560]{1,0:T(8,128)(2,1)S(1)} collective-permute-done((bf16[196,2560]{1,0:T(8,128)(2,1)S(1)}, bf16[196,2560]{1,0:T(8,128)(2,1)S(1)}, u32[]{:S(2)}, u32[]{:S(2)}) %collective-permute-start.4) | collective-permute-done | bytes 1003552 | tf_op jit(solution)/shard_map/ppermute | solution.py:84
  114.5 0.7 collective-permute-start.7
  115.4 0.9 copy-done.15
  116.3 1.0 copy-done.16
  117.3 23.2 %shard_map.55.refs_5_ = f32[640,512]{1,0:T(8,128)} custom-call(bf16[196,2560]{1,0:T(8,128)(2,1)} %copy-done.6, bf16[196,2560]{1,0:T(8,128)(2,1)} %copy-done.12, bf16[196,2560]{1,0:T(8,128)(2,1)} %copy-done.9, bf16[196,2560]{1,0:T(8,128)(2,1)} %copy-done.14, bf16[196,2560]{1,0:T(8,128)(2,1)} %copy-done.11, bf16[196,2560]{1,0:T(8,128)(2,1)} %copy-done.16, ...), custom_call_target="tpu_custom_call" | custom-call | flops 6936330240 | bytes 17940480 | tf_op jit(solution)/shard_map/pallas_call | solution.py:63
  140.6 11.7 %shard_map.56 = f32[640,512]{1,0:T(8,128)} custom-call(bf16[196,2560]{1,0:T(8,128)(2,1)} %copy-done.3, bf16[196,2560]{1,0:T(8,128)(2,1)} %collective-permute-done.5.refs_1_, bf16[196,2560]{1,0:T(8,128)(2,1)} %copy-done.4, bf16[196,2560]{1,0:T(8,128)(2,1)} %collective-permute-done.7.refs_3_, bf16[4608,640]{1,0:T(8,128)(2,1)} %all-gather.2.cloned.1.call-done.refs_12_.refs_4_, ...), custom_call_target="tpu_custom_call" | custom-call | flops 2312110080 | bytes 9912320 | tf_op jit(solution)/shard_map/pallas_call | solution.py:63
  152.3 27.3 %all_to_all.5 = f32[16,40,512]{2,1,0:T(8,128)S(1)} all-to-all(f32[16,40,512]{2,1,0:T(8,128)} %bitcast.29), channel_id=1, replica_groups=mesh['img'=16,'own'=8] {'img'}, dimensions={0} | all-to-all | bytes 2621440 | tf_op jit(solution)/shard_map/all_to_all | solution.py:154
  (87 shorter events, 6.9 us)
Async XLA Ops:
  6.5 27.6 %copy-start = (bf16[512,512]{1,0:T(8,128)(2,1)S(1)}, bf16[512,512]{1,0:T(8,128)(2,1)}, u32[]{:S(2)}) copy-start(bf16[512,512]{1,0:T(8,128)(2,1)} %param.7) | copy-start | bytes 1572868
  6.5 110.7 %all-gather.2.cloned.1.call-start = ((), (), s32[]{:S(2)}) async-start(), calls=%async_computation.1 | async-start | bytes 6266880 | tf_op jit(solution)/shard_map/all_gather | solution.py:123
  14.1 2.3 %collective-permute-start.8 = (bf16[4,144,288]{2,1,0:T(8,128)(2,1)S(1)}, bf16[4,144,288]{2,1,0:T(8,128)(2,1)S(1)}, u32[]{:S(2)}, u32[]{:S(2)}) collective-permute-start(bf16[4,144,288]{2,1,0:T(8,128)(2,1)S(1)} %bitcast.33), channel_id=1, source_target_pairs={{0,1},{1,0},{2,3},{3,2},{4,5},{5,4},{6,7},{7,6},{8,9},{9,8},{10,11... | collective-permute-start | bytes 995336 | tf_op jit(solution)/shard_map/ppermute | solution.py:88
  16.6 10.3 %collective-permute-start.10 = (bf16[2,144,288]{2,1,0:T(8,128)(2,1)S(1)}, bf16[2,144,288]{2,1,0:T(8,128)(2,1)S(1)}, u32[]{:S(2)}, u32[]{:S(2)}) collective-permute-start(bf16[2,144,288]{2,1,0:T(8,128)(2,1)S(1)} %get-tuple-element.24), channel_id=1, source_target_pairs={{0,4},{1,5},{2,6},{3,7},{4,0},{5,1},{6,2},{7,3},{8,12},{9,13},{10,... | collective-permute-start | bytes 497672 | tf_op jit(solution)/shard_map/ppermute | solution.py:84
  20.6 11.6 %collective-permute-start.11 = (bf16[2,144,288]{2,1,0:T(8,128)(2,1)S(1)}, bf16[2,144,288]{2,1,0:T(8,128)(2,1)S(1)}, u32[]{:S(2)}, u32[]{:S(2)}) collective-permute-start(bf16[2,144,288]{2,1,0:T(8,128)(2,1)S(1)} %get-tuple-element.23), channel_id=1, source_target_pairs={{0,6},{1,7},{2,0},{3,1},{4,2},{5,3},{6,4},{7,5},{8,14},{9,15},{10,... | collective-permute-start | bytes 497672 | tf_op jit(solution)/shard_map/ppermute | solution.py:84
  21.3 10.9 %collective-permute-start.9 = (bf16[2,144,288]{2,1,0:T(8,128)(2,1)S(1)}, bf16[2,144,288]{2,1,0:T(8,128)(2,1)S(1)}, u32[]{:S(2)}, u32[]{:S(2)}) collective-permute-start(bf16[2,144,288]{2,1,0:T(8,128)(2,1)S(1)} %get-tuple-element.22), channel_id=1, source_target_pairs={{0,2},{1,3},{2,4},{3,5},{4,6},{5,7},{6,0},{7,1},{8,10},{9,11},{10,... | collective-permute-start | bytes 497672 | tf_op jit(solution)/shard_map/ppermute | solution.py:84
  35.3 79.2 %copy-start.5 = (bf16[196,2560]{1,0:T(8,128)(2,1)}, bf16[196,2560]{1,0:T(8,128)(2,1)S(1)}, u32[]{:S(2)}) copy-start(bf16[196,2560]{1,0:T(8,128)(2,1)S(1)} %pad_maximum_fusion.refs_6_) | copy-start | bytes 3010564
  35.3 24.7 %collective-permute-start.1 = (bf16[196,2560]{1,0:T(8,128)(2,1)S(1)}, bf16[196,2560]{1,0:T(8,128)(2,1)S(1)}, u32[]{:S(2)}, u32[]{:S(2)}) collective-permute-start(bf16[196,2560]{1,0:T(8,128)(2,1)S(1)} %pad_maximum_fusion.refs_6_), channel_id=1, source_target_pairs={{0,6},{1,7},{2,0},{3,1},{4,2},{5,3},{6,4},{7,5},{8,14},{9,15},{10,... | collective-permute-start | bytes 3010568 | tf_op jit(solution)/shard_map/ppermute | solution.py:84
  38.1 77.2 %copy-start.6 = (bf16[196,2560]{1,0:T(8,128)(2,1)}, bf16[196,2560]{1,0:T(8,128)(2,1)S(1)}, u32[]{:S(2)}) copy-start(bf16[196,2560]{1,0:T(8,128)(2,1)S(1)} %slice.29.refs_0_) | copy-start | bytes 3010564
  38.1 25.5 %collective-permute-start = (bf16[196,2560]{1,0:T(8,128)(2,1)S(1)}, bf16[196,2560]{1,0:T(8,128)(2,1)S(1)}, u32[]{:S(2)}, u32[]{:S(2)}) collective-permute-start(bf16[196,2560]{1,0:T(8,128)(2,1)S(1)} %slice.29.refs_0_), channel_id=1, source_target_pairs={{0,2},{1,3},{2,4},{3,5},{4,6},{5,7},{6,0},{7,1},{8,10},{9,11},{10,... | collective-permute-start | bytes 3010568 | tf_op jit(solution)/shard_map/ppermute | solution.py:84
  60.1 55.2 %copy-start.8 = (bf16[196,2560]{1,0:T(8,128)(2,1)}, bf16[196,2560]{1,0:T(8,128)(2,1)S(1)}, u32[]{:S(2)}) copy-start(bf16[196,2560]{1,0:T(8,128)(2,1)S(1)} %collective-permute-done.1.refs_10_) | copy-start | bytes 3010564
  63.6 51.7 %copy-start.9 = (bf16[196,2560]{1,0:T(8,128)(2,1)}, bf16[196,2560]{1,0:T(8,128)(2,1)S(1)}, u32[]{:S(2)}) copy-start(bf16[196,2560]{1,0:T(8,128)(2,1)S(1)} %collective-permute-done.refs_2_) | copy-start | bytes 3010564
  63.6 24.5 %collective-permute-start.2 = (bf16[196,2560]{1,0:T(8,128)(2,1)S(1)}, bf16[196,2560]{1,0:T(8,128)(2,1)S(1)}, u32[]{:S(2)}, u32[]{:S(2)}) collective-permute-start(bf16[196,2560]{1,0:T(8,128)(2,1)S(1)} %pad_maximum_fusion.refs_6_), channel_id=1, source_target_pairs={{0,2},{1,3},{2,4},{3,5},{4,6},{5,7},{6,0},{7,1},{8,10},{9,11},{10,... | collective-permute-start | bytes 3010568 | tf_op jit(solution)/shard_map/ppermute | solution.py:84
  63.6 24.5 %collective-permute-start.3 = (bf16[196,2560]{1,0:T(8,128)(2,1)S(1)}, bf16[196,2560]{1,0:T(8,128)(2,1)S(1)}, u32[]{:S(2)}, u32[]{:S(2)}) collective-permute-start(bf16[196,2560]{1,0:T(8,128)(2,1)S(1)} %slice.29.refs_0_), channel_id=1, source_target_pairs={{0,6},{1,7},{2,0},{3,1},{4,2},{5,3},{6,4},{7,5},{8,14},{9,15},{10,... | collective-permute-start | bytes 3010568 | tf_op jit(solution)/shard_map/ppermute | solution.py:84
  66.9 24.7 %collective-permute-start.12 = (bf16[196,2560]{1,0:T(8,128)(2,1)S(1)}, bf16[196,2560]{1,0:T(8,128)(2,1)S(1)}, u32[]{:S(2)}, u32[]{:S(2)}) collective-permute-start(bf16[196,2560]{1,0:T(8,128)(2,1)S(1)} %slice.29.refs_0_), channel_id=1, source_target_pairs={{0,1},{1,0},{2,3},{3,2},{4,5},{5,4},{6,7},{7,6},{8,9},{9,8},{10,11... | collective-permute-start | bytes 3010568 | tf_op jit(solution)/shard_map/ppermute | solution.py:88
  66.9 24.7 %collective-permute-start.15 = (bf16[196,2560]{1,0:T(8,128)(2,1)S(1)}, bf16[196,2560]{1,0:T(8,128)(2,1)S(1)}, u32[]{:S(2)}, u32[]{:S(2)}) collective-permute-start(bf16[196,2560]{1,0:T(8,128)(2,1)S(1)} %pad_maximum_fusion.refs_6_), channel_id=1, source_target_pairs={{0,1},{1,0},{2,3},{3,2},{4,5},{5,4},{6,7},{7,6},{8,9},{9,8},{10,11... | collective-permute-start | bytes 3010568 | tf_op jit(solution)/shard_map/ppermute | solution.py:88
  88.2 3.9 %collective-permute-start.13 = (bf16[196,2560]{1,0:T(8,128)(2,1)S(1)}, bf16[196,2560]{1,0:T(8,128)(2,1)S(1)}, u32[]{:S(2)}, u32[]{:S(2)}) collective-permute-start(bf16[196,2560]{1,0:T(8,128)(2,1)S(1)} %collective-permute-done.refs_2_), channel_id=1, source_target_pairs={{0,1},{1,0},{2,3},{3,2},{4,5},{5,4},{6,7},{7,6},{8,9},{9,8},{10,11... | collective-permute-start | bytes 3010568 | tf_op jit(solution)/shard_map/ppermute | solution.py:88
  88.3 26.3 %collective-permute-start.4 = (bf16[196,2560]{1,0:T(8,128)(2,1)S(1)}, bf16[196,2560]{1,0:T(8,128)(2,1)S(1)}, u32[]{:S(2)}, u32[]{:S(2)}) collective-permute-start(bf16[196,2560]{1,0:T(8,128)(2,1)S(1)} %collective-permute-done.refs_2_), channel_id=1, source_target_pairs={{0,2},{1,3},{2,4},{3,5},{4,6},{5,7},{6,0},{7,1},{8,10},{9,11},{10,... | collective-permute-start | bytes 3010568 | tf_op jit(solution)/shard_map/ppermute | solution.py:84
  88.3 26.2 %collective-permute-start.6 = (bf16[196,2560]{1,0:T(8,128)(2,1)S(1)}, bf16[196,2560]{1,0:T(8,128)(2,1)S(1)}, u32[]{:S(2)}, u32[]{:S(2)}) collective-permute-start(bf16[196,2560]{1,0:T(8,128)(2,1)S(1)} %collective-permute-done.1.refs_10_), channel_id=1, source_target_pairs={{0,6},{1,7},{2,0},{3,1},{4,2},{5,3},{6,4},{7,5},{8,14},{9,15},{10,... | collective-permute-start | bytes 3010568 | tf_op jit(solution)/shard_map/ppermute | solution.py:84
  91.6 23.7 %collective-permute-start.17 = (bf16[196,2560]{1,0:T(8,128)(2,1)S(1)}, bf16[196,2560]{1,0:T(8,128)(2,1)S(1)}, u32[]{:S(2)}, u32[]{:S(2)}) collective-permute-start(bf16[196,2560]{1,0:T(8,128)(2,1)S(1)} %collective-permute-done.1.refs_10_), channel_id=1, source_target_pairs={{0,1},{1,0},{2,3},{3,2},{4,5},{5,4},{6,7},{7,6},{8,9},{9,8},{10,11... | collective-permute-start | bytes 3010568 | tf_op jit(solution)/shard_map/ppermute | solution.py:88
  91.6 23.7 %collective-permute-start.14 = (bf16[196,2560]{1,0:T(8,128)(2,1)S(1)}, bf16[196,2560]{1,0:T(8,128)(2,1)S(1)}, u32[]{:S(2)}, u32[]{:S(2)}) collective-permute-start(bf16[196,2560]{1,0:T(8,128)(2,1)S(1)} %collective-permute-done.3.refs_4_), channel_id=1, source_target_pairs={{0,1},{1,0},{2,3},{3,2},{4,5},{5,4},{6,7},{7,6},{8,9},{9,8},{10,11... | collective-permute-start | bytes 3010568 | tf_op jit(solution)/shard_map/ppermute | solution.py:88
  92.1 25.2 %collective-permute-start.16 = (bf16[196,2560]{1,0:T(8,128)(2,1)S(1)}, bf16[196,2560]{1,0:T(8,128)(2,1)}, u32[]{:S(2)}, u32[]{:S(2)}) collective-permute-start(bf16[196,2560]{1,0:T(8,128)(2,1)S(1)} %collective-permute-done.2.refs_8_), channel_id=1, source_target_pairs={{0,1},{1,0},{2,3},{3,2},{4,5},{5,4},{6,7},{7,6},{8,9},{9,8},{10,11... | collective-permute-start | bytes 3010568 | tf_op jit(solution)/shard_map/ppermute | solution.py:88
  114.5 26.0 %collective-permute-start.5 = (bf16[196,2560]{1,0:T(8,128)(2,1)S(1)}, bf16[196,2560]{1,0:T(8,128)(2,1)}, u32[]{:S(2)}, u32[]{:S(2)}) collective-permute-start(bf16[196,2560]{1,0:T(8,128)(2,1)S(1)} %collective-permute-done.4.refs_0_), channel_id=1, source_target_pairs={{0,1},{1,0},{2,3},{3,2},{4,5},{5,4},{6,7},{7,6},{8,9},{9,8},{10,11... | collective-permute-start | bytes 3010568 | tf_op jit(solution)/shard_map/ppermute | solution.py:88
  114.5 26.0 %collective-permute-start.7 = (bf16[196,2560]{1,0:T(8,128)(2,1)S(1)}, bf16[196,2560]{1,0:T(8,128)(2,1)}, u32[]{:S(2)}, u32[]{:S(2)}) collective-permute-start(bf16[196,2560]{1,0:T(8,128)(2,1)S(1)} %collective-permute-done.6.refs_2_), channel_id=1, source_target_pairs={{0,1},{1,0},{2,3},{3,2},{4,5},{5,4},{6,7},{7,6},{8,9},{9,8},{10,11... | collective-permute-start | bytes 3010568 | tf_op jit(solution)/shard_map/ppermute | solution.py:88
  (13 other events, 187.4 us)
Sparse Core Ops, SparseCore 0:
  34.3 60.3 all-gather.1

commit v3 on v2

v3 whole, which is shorter than its diff:
```python
import functools

import jax
import jax.numpy as jnp
from jax import lax
from jax.experimental import pallas as pl
from jax.experimental.pallas import tpu as pltpu
from jax.sharding import PartitionSpec as P

POS = 49
CHIPS = 4
CORES = 2
TOP = 13.0
F32, BF16, I32 = jnp.float32, jnp.bfloat16, jnp.int32


def accumulate(n, chunk, staged, block, *refs):
    lows, highs = refs[:n], refs[n : 2 * n]
    basis, *before, out, flip, total = refs[2 * n : len(refs) - (6 if staged else 0)]
    total = out if staged else total
    rows, half = lows[0].shape
    kin, cols = basis.shape
    rest = kin - half
    gout = half - rest
    parts = 4
    if staged:
        low, high, held, low_sems, high_sems, basis_sems = refs[-6:]
        lefts = [pltpu.make_async_copy(lows[k], low.at[k % 2], low_sems.at[k % 2]) for k in range(n)]
        rights = [pltpu.make_async_copy(highs[k], high.at[k % 2], high_sems.at[k % 2]) for k in range(n)]
        edges = [half * i // parts for i in range(parts)] + [half + rest * i // parts for i in range(parts + 1)]
        spans = [pl.ds(a, b - a) for a, b in zip(edges, edges[1:])]
        pieces = [pltpu.make_async_copy(basis.at[s], held.at[s], basis_sems.at[i]) for i, s in enumerate(spans)]
        lefts[0].start()
        for piece in pieces[:parts]:
            piece.start()
        rights[0].start()
        for piece in pieces[parts:]:
            piece.start()
        lows, highs, basis = [low.at[k % 2] for k in range(n)], [high.at[k % 2] for k in range(n)], held
    image = lax.broadcasted_iota(I32, (rows, gout), 0) // POS
    for k in range(n):
        if staged:
            lefts[k].wait()
            if k + 1 < n:
                lefts[k + 1].start()
        if staged and k == 0:
            proj = jnp.zeros((rows, cols), F32)
            for i in range(2 * parts):
                if i == parts:
                    rights[0].wait()
                    rights[1].start()
                pieces[i].wait()
                a, b = edges[i], edges[i + 1]
                left = lows[0][:, a:b] if i < parts else highs[0][:, a - half : b - half]
                proj += jnp.dot(left, basis[a:b], preferred_element_type=F32)
        else:
            proj = jnp.dot(lows[k][...], basis[:half], preferred_element_type=F32)
            if staged:
                rights[k].wait()
                if k + 1 < n:
                    rights[k + 1].start()
            proj += jnp.dot(highs[k][:, :rest], basis[half:], preferred_element_type=F32)
        flip[k % 2] = proj.astype(BF16).T
        grads = highs[k][:, rest:]
        apart = [jnp.where(image == m, grads, jnp.zeros_like(grads)) for m in range(rows // POS)]
        source = total if k else before[0] if before else None
        for s in range(0, cols, chunk):
            left = flip[k % 2, s : s + chunk]
            squares = jnp.zeros((chunk, gout), F32) if source is None else source[s : s + chunk]
            for one in apart:
                coef = jnp.dot(left, one, preferred_element_type=F32)
                squares += coef * coef
            total[s : s + chunk] = squares
    if not staged:
        peak = jnp.max(jnp.max(total[...], axis=0, keepdims=True), axis=1, keepdims=True)
        level = jnp.floor(jnp.log(jnp.maximum(peak, 1e-30)) * 1.4426950408889634)
        row = lax.rem(lax.broadcasted_iota(I32, (cols, gout), 0), jnp.int32(block[1]))
        out[...] = jnp.where(row == block[0], level, total[...] * jnp.exp2(TOP - level))


def added(lows, highs, basis, *before, staged=False, block=()):
    n = len(lows)
    rows, half = lows[0].shape
    kin, cols = basis.shape
    gout = 2 * half - kin
    inside = pl.BlockSpec(memory_space=pltpu.VMEM)
    source = pl.BlockSpec(memory_space=pltpu.HBM) if staged else inside
    room = [
        pltpu.VMEM((2, rows, half), BF16),
        pltpu.VMEM((2, rows, half), BF16),
        pltpu.VMEM((kin, cols), BF16),
        pltpu.SemaphoreType.DMA((2,)),
        pltpu.SemaphoreType.DMA((2,)),
        pltpu.SemaphoreType.DMA((8,)),
    ]
    return pl.pallas_call(
        functools.partial(accumulate, n, cols // 2, staged, block),
        out_shape=jax.ShapeDtypeStruct((cols, gout), F32),
        in_specs=[source] * (2 * n + 1) + [inside] * len(before),
        out_specs=inside,
        scratch_shapes=[pltpu.VMEM((2, cols, rows), BF16), pltpu.VMEM((8, 128) if staged else (cols, gout), F32)]
        + (room if staged else []),
        compiler_params=pltpu.CompilerParams(vmem_limit_bytes=(60 if staged else 28) << 20),
        cost_estimate=pl.CostEstimate(
            flops=2 * n * rows * kin * cols, bytes_accessed=4 * n * rows * half + 2 * kin * cols, transcendentals=0
        ),
    )(*lows, *highs, basis, *before)


def place(blk, ring, me, counts, slots, kept, given, held, sem):
    depth, cap = held.shape
    owners = CHIPS * CORES
    stripe, per = blk * owners, ring // owners
    img, own = me[0], me[1]
    z, c = own // CORES, own % CORES
    copy = pltpu.make_async_copy(slots.at[pl.ds(pl.multiple_of(img * depth, 16), depth)], held, sem)
    copy.start()
    start = jnp.int32(0)
    for o in range(owners):
        start += jnp.where(o < own, counts[o], 0)
    slot = lax.broadcasted_iota(I32, (1, cap), 1)
    spot = lax.rem(start + slot, jnp.int32(ring))
    goal = lax.div(lax.rem(spot, jnp.int32(stripe)), jnp.int32(blk))
    hop = ((goal // CORES - z + CHIPS) & (CHIPS - 1)) + CHIPS * ((goal & 1) ^ c)
    row = hop * per + lax.div(spot, jnp.int32(stripe)) * blk + lax.rem(spot, jnp.int32(blk))
    row = jnp.where(slot < counts[own], row, -1)
    copy.wait()
    for r in range(0, ring, per):
        here = lax.broadcasted_iota(I32, (per, cap), 0) + r == row
        out = kept if r < ring // CORES else given
        out[r % (ring // CORES) // per] = lax.dot_general(
            here.astype(F32).astype(BF16), held[...], (((1,), (1,)), ((), ())), preferred_element_type=F32
        ).astype(BF16)


def placed(basis_slots, col_counts, img, own, groups, blk, ring):
    kin, cap = basis_slots.shape
    depth = kin // groups
    scalars = pl.BlockSpec(memory_space=pltpu.SMEM)
    return pl.pallas_call(
        functools.partial(place, blk, ring),
        out_shape=[jax.ShapeDtypeStruct((CHIPS, ring // CHIPS // CORES, depth), BF16)] * CORES,
        in_specs=[scalars, scalars, pl.BlockSpec(memory_space=pltpu.HBM)],
        out_specs=[pl.BlockSpec(memory_space=pltpu.VMEM)] * CORES,
        scratch_shapes=[pltpu.VMEM((depth, cap), BF16), pltpu.SemaphoreType.DMA],
        compiler_params=pltpu.CompilerParams(vmem_limit_bytes=55 << 20),
        cost_estimate=pl.CostEstimate(flops=2 * ring * cap * depth, bytes_accessed=4 * depth * cap, transcendentals=0),
    )(jnp.stack([img, own]).astype(I32), col_counts, basis_slots)


def up(a, step):
    pairs = [(z * CORES + c, (z + step) % CHIPS * CORES + c) for z in range(CHIPS) for c in range(CORES)]
    return lax.ppermute(a, "own", pairs)


def swap(a):
    return lax.ppermute(a, "own", [(o, o ^ 1) for o in range(CHIPS * CORES)])


def balanced_basis(basis_slots, col_counts, img, own, groups, blk, wide):
    owners = CHIPS * CORES
    kin, cap = basis_slots.shape
    stripe = blk * owners
    ring = -(-cap // stripe) * stripe
    per = ring // owners
    depth = kin // groups
    starts = jnp.cumsum(col_counts) - col_counts
    z, c = own // CORES, own % CORES
    kept, given = placed(basis_slots, col_counts, img, own, groups, blk, ring)
    both = jnp.stack([kept, swap(given)], axis=1)
    incoming = jnp.stack([both[0], up(both[1], 1), up(both[2], 2), up(both[3], -1)])
    source = ((z - jnp.arange(CHIPS, dtype=I32)) % CHIPS * CORES)[:, None] + (jnp.arange(CORES, dtype=I32) ^ c)[None, :]
    source = source.reshape(owners)
    begin, count = starts[source], col_counts[source]
    spot = jnp.arange(per, dtype=I32)
    at = spot // blk * stripe + own * blk + spot % blk
    offset = (at[None, :] - begin[:, None]) % ring
    column = begin[:, None] + offset
    target = jnp.where(offset < count[:, None], column // stripe * wide + column % blk, -1)
    keep = target.reshape(ring)[:, None] == jnp.arange(groups * wide, dtype=I32)[None, :]
    mine = lax.dot_general(
        incoming.reshape(ring, depth), keep.astype(BF16), (((0,), (0,)), ((), ())), preferred_element_type=F32
    )
    return lax.all_gather(mine.astype(BF16), "img", axis=0, tiled=True)


def gathered(low, high):
    low_down, high_up = up(low, 1), up(high, -1)
    low, high, low_down, high_up = lax.optimization_barrier((low, high, low_down, high_up))
    high_down, low_up = up(high, 1), up(low, -1)
    low_down, high_up, high_down, low_up = lax.optimization_barrier((low_down, high_up, high_down, low_up))
    low_far, high_far = up(low_down, 1), up(high_up, -1)
    return [low, low_down, low_up, low_far], [high, high_down, high_up, high_far]


def shared(arrays):
    return [b for a in arrays for b in (a, swap(a))]


def shards(patches, grads, basis_g, basis_slots, col_counts):
    groups = lax.axis_size("img")
    owners = CHIPS * CORES
    img, own = lax.axis_index("img"), lax.axis_index("own")
    rows, kin = patches.shape
    gout = basis_g.shape[1]
    blk = kin // (groups * owners)
    proj = jnp.dot(grads, basis_g, preferred_element_type=F32).astype(BF16)
    half = (kin + gout) // 2
    low, high = patches[:, :half], jnp.concatenate([patches[:, half:], proj], axis=1)
    lows, highs = gathered(low, high)
    wide = -(-(blk + 1) // 8) * 8
    basis = balanced_basis(basis_slots, col_counts, img, own, groups, blk, wide)
    total = added(shared(lows[:-1]), shared(highs[:-1]), basis, staged=True)
    low, high, total = lax.optimization_barrier((lows[-1], highs[-1], total))
    total = added(shared([low]), shared([high]), basis, total, block=(blk, wide))
    parts = lax.all_to_all(total.astype(jnp.float16).reshape(groups, wide, gout), "img", 0, 0, tiled=True)
    level = parts[:, blk : blk + 1, :1].astype(F32) - TOP
    return jnp.sum(parts[:, :blk].astype(F32) * jnp.exp2(level), axis=0) / F32(owners * rows // POS * groups)


def solution(mesh):
    in_specs = (P(("img", "own"), None), P(("img", "own"), None), P(), P(None, "own"), P())
    out_specs = P(("img", "own"), None)
    return jax.shard_map(shards, mesh=mesh, in_specs=in_specs, out_specs=out_specs, check_vma=False)
```

time: 188 us -> 160 us (0.85)
  waiting for transfers between devices: 78.1 us -> 62.7 us
  blocking collectives: 27.3 us -> 20.1 us
  Pallas kernels: 35 us -> 31.3 us
  matrix products: 4.26 us -> 1.9 us
    ppermute x9, waiting for transfers between devices: 78.1 us -> 55.8 us  [up(): return lax.ppermute(a, 'own', pairs)]
    all_to_all x1, blocking collectives: 27.3 us -> 20.1 us  [shards(): lax.all_to_all(total.astype(jnp.float16).reshape(groups, wide, gout), 'im...]
    ppermute x9, waiting for transfers between devices: 0.02 us -> 6.89 us  [swap(): return lax.ppermute(a, 'own', [(o, o ^ 1) for o in range(CHIPS * CORES)])]
    unnamed x34 -> x31, local copies, waits for them, and re-layouts: 1.96 us -> 6.1 us
    pallas_call x2 -> x3, Pallas kernels: 35 us -> 31.3 us  [the longest x2 26.4 us: added(): pl.pallas_call(functools.partial(accumulate, n, cols // 2, staged, block)...]
    dot_general x1 -> x0, matrix products: 2.32 us -> none  [balanced_basis(): lax.dot_general(send.astype(BF16), piece, (((1,), (1,)), ((), ())), prefe...]
    dynamic_slice x2 -> x0, local copies, waits for them, and re-layouts: 1.88 us -> none  [the longest x1 1.3 us: balanced_basis(): col_counts[own]]
  transfers between devices with their start and end apart: 19 -> 19, of which waited for: 6 -> 9; matrix products, arithmetic and copies ran while one was open for 1% -> 2% of each run, Pallas kernels for 12% -> 13%
where the time goes in v3:
time: 160 us; the launch traced here: 159 us
  waiting for transfers between devices  62.7 us (39%)
  Pallas kernels  31.3 us (20%)
  blocking collectives  20.1 us (13%)
  starting transfers between devices  17.4 us (11%)
  between operations  13.7 us (9%)
  local copies, waits for them, and re-layouts  8.77 us (5%)
  other arithmetic  3.47 us (2%)
  matrix products  1.9 us (1%)
    ppermute x9, waiting for transfers between devices, up(): return lax.ppermute(a, 'own', pairs)  55.8 us
    pallas_call x2, Pallas kernels, added(): pl.pallas_call(functools.partial(accumulate, n, cols // 2, staged, block)...  26.4 us
    all_to_all x1, blocking collectives, shards(): lax.all_to_all(total.astype(jnp.float16).reshape(groups, wide, gout), 'im...  20.1 us
    ppermute x9, starting transfers between devices, up(): return lax.ppermute(a, 'own', pairs)  15.1 us
    ppermute x9, waiting for transfers between devices, swap(): return lax.ppermute(a, 'own', [(o, o ^ 1) for o in range(CHIPS * CORES)])  6.89 us
    unnamed x31, local copies, waits for them, and re-layouts  6.1 us
    pallas_call x1, Pallas kernels, placed(): pl.pallas_call(functools.partial(place, blk, ring), out_shape=[jax.ShapeD...  4.93 us
  transfers between devices with their start and end apart: 19, of which 9 were waited for; matrix products, arithmetic and copies ran while one was open for 2% of the time, Pallas kernels for 13%

profile of v3, /device:TPU:0, one launch (start us, length us, event | category | flops | bytes accessed | tf_op | source)
XLA Modules:
  0.0 159.4 jit_solution(14000547404875887776)
XLA Ops:
  7.2 4.9 %shard_map.55 = (bf16[4,144,288]{2,1,0:T(8,128)(2,1)}, bf16[4,144,288]{2,1,0:T(8,128)(2,1)}) custom-call(s32[2]{0:T(128)} %pad_add_fusion.me, s32[8]{0:T(128)} %counts.1, bf16[4608,1152]{1,0:T(8,128)(2,1)} %slots.1), custom_call_target="tpu_custom_call" | custom-call | flops 764411904 | bytes 1327104 | tf_op jit(solution)/shard_map/pallas_call | solution.py:140
  14.4 1.2 fusion.6
  15.6 2.1 %collective-permute-start.13 = (bf16[2,144,288]{2,1,0:T(8,128)(2,1)S(1)}, bf16[2,144,288]{2,1,0:T(8,128)(2,1)S(1)}, u32[]{:S(2)}, u32[]{:S(2)}) collective-permute-start(bf16[2,144,288]{2,1,0:T(8,128)(2,1)S(1)} %get-tuple-element.32), channel_id=1, source_target_pairs={{0,2},{1,3},{2,4},{3,5},{4,6},{5,7},{6,0},{7,1},{8,10},{9,11},{10,... | collective-permute-start | bytes 497672 | tf_op jit(solution)/shard_map/ppermute | solution.py:153
  17.7 3.6 %collective-permute-start.14 = (bf16[2,144,288]{2,1,0:T(8,128)(2,1)S(1)}, bf16[2,144,288]{2,1,0:T(8,128)(2,1)S(1)}, u32[]{:S(2)}, u32[]{:S(2)}) collective-permute-start(bf16[2,144,288]{2,1,0:T(8,128)(2,1)S(1)} %get-tuple-element.34), channel_id=1, source_target_pairs={{0,4},{1,5},{2,6},{3,7},{4,0},{5,1},{6,2},{7,3},{8,12},{9,13},{10,... | collective-permute-start | bytes 497672 | tf_op jit(solution)/shard_map/ppermute | solution.py:153
  21.3 1.0 collective-permute-start.15
  22.3 3.5 %collective-permute-done.13 = bf16[2,144,288]{2,1,0:T(8,128)(2,1)S(1)} collective-permute-done((bf16[2,144,288]{2,1,0:T(8,128)(2,1)S(1)}, bf16[2,144,288]{2,1,0:T(8,128)(2,1)S(1)}, u32[]{:S(2)}, u32[]{:S(2)}) %collective-permute-start.13) | collective-permute-done | bytes 165920 | tf_op jit(solution)/shard_map/ppermute | solution.py:153
  25.9 5.9 %collective-permute-done.14 = bf16[2,144,288]{2,1,0:T(8,128)(2,1)S(1)} collective-permute-done((bf16[2,144,288]{2,1,0:T(8,128)(2,1)S(1)}, bf16[2,144,288]{2,1,0:T(8,128)(2,1)S(1)}, u32[]{:S(2)}, u32[]{:S(2)}) %collective-permute-start.14) | collective-permute-done | bytes 165920 | tf_op jit(solution)/shard_map/ppermute | solution.py:153
  32.0 1.6 %fusion.2 = bf16[288,640]{1,0:T(8,128)(2,1)} fusion(bf16[1152,288]{1,0:T(8,128)(2,1)S(1)} %bitcast.33, s32[1152]{0:T(1024)S(1)} %fusion.12), kind=kOutput, calls=%fused_computation.6 | convolution fusion | flops 425594880 | bytes 1036800 | tf_op jit(solution)/shard_map/dot_general | solution.py:181
  34.9 2.3 %collective-permute-start.1 = (bf16[196,2560]{1,0:T(8,128)(2,1)S(1)}, bf16[196,2560]{1,0:T(8,128)(2,1)}, u32[]{:S(2)}, u32[]{:S(2)}) collective-permute-start(bf16[196,2560]{1,0:T(8,128)(2,1)S(1)} %pad_maximum_fusion.refs_6_), channel_id=1, source_target_pairs={{0,6},{1,7},{2,0},{3,1},{4,2},{5,3},{6,4},{7,5},{8,14},{9,15},{10,... | collective-permute-start | bytes 3010568 | tf_op jit(solution)/shard_map/ppermute | solution.py:153
  37.3 22.0 %collective-permute-done.1.refs_10_ = bf16[196,2560]{1,0:T(8,128)(2,1)} collective-permute-done((bf16[196,2560]{1,0:T(8,128)(2,1)S(1)}, bf16[196,2560]{1,0:T(8,128)(2,1)}, u32[]{:S(2)}, u32[]{:S(2)}) %collective-permute-start.1) | collective-permute-done | bytes 1003552 | tf_op jit(solution)/shard_map/ppermute | solution.py:153
  59.3 3.6 %collective-permute-done.refs_2_ = bf16[196,2560]{1,0:T(8,128)(2,1)} collective-permute-done((bf16[196,2560]{1,0:T(8,128)(2,1)S(1)}, bf16[196,2560]{1,0:T(8,128)(2,1)}, u32[]{:S(2)}, u32[]{:S(2)}) %collective-permute-start) | collective-permute-done | bytes 1003552 | tf_op jit(solution)/shard_map/ppermute | solution.py:153
  62.9 3.2 %collective-permute-start.3 = (bf16[196,2560]{1,0:T(8,128)(2,1)S(1)}, bf16[196,2560]{1,0:T(8,128)(2,1)S(1)}, u32[]{:S(2)}, u32[]{:S(2)}) collective-permute-start(bf16[196,2560]{1,0:T(8,128)(2,1)S(1)} %slice.24.refs_0_), channel_id=1, source_target_pairs={{0,6},{1,7},{2,0},{3,1},{4,2},{5,3},{6,4},{7,5},{8,14},{9,15},{10,... | collective-permute-start | bytes 3010568 | tf_op jit(solution)/shard_map/ppermute | solution.py:153
  66.6 20.8 %collective-permute-done.2.refs_8_ = bf16[196,2560]{1,0:T(8,128)(2,1)S(1)} collective-permute-done((bf16[196,2560]{1,0:T(8,128)(2,1)S(1)}, bf16[196,2560]{1,0:T(8,128)(2,1)S(1)}, u32[]{:S(2)}, u32[]{:S(2)}) %collective-permute-start.2) | collective-permute-done | bytes 1003552 | tf_op jit(solution)/shard_map/ppermute | solution.py:153
  88.5 1.8 %collective-permute-done.11.refs_11_ = bf16[196,2560]{1,0:T(8,128)(2,1)S(1)} collective-permute-done((bf16[196,2560]{1,0:T(8,128)(2,1)}, bf16[196,2560]{1,0:T(8,128)(2,1)S(1)}, u32[]{:S(2)}, u32[]{:S(2)}) %collective-permute-start.11) | collective-permute-done | bytes 1003552 | tf_op jit(solution)/shard_map/ppermute | solution.py:157
  90.3 2.9 %collective-permute-start.5 = (bf16[196,2560]{1,0:T(8,128)(2,1)}, bf16[196,2560]{1,0:T(8,128)(2,1)S(1)}, u32[]{:S(2)}, u32[]{:S(2)}) collective-permute-start(bf16[196,2560]{1,0:T(8,128)(2,1)} %collective-permute-done.1.refs_10_), channel_id=1, source_target_pairs={{0,6},{1,7},{2,0},{3,1},{4,2},{5,3},{6,4},{7,5},{8,14},{9,15},{10,... | collective-permute-start | bytes 3010568 | tf_op jit(solution)/shard_map/ppermute | solution.py:153
  93.2 1.5 collective-permute-done.7.refs_3_
  95.7 1.0 copy-done.14
  96.7 21.5 %shard_map.56.refs_5_ = f32[640,512]{1,0:T(8,128)} custom-call(bf16[196,2560]{1,0:T(8,128)(2,1)} %copy-done.6, bf16[196,2560]{1,0:T(8,128)(2,1)} %copy-done.10, bf16[196,2560]{1,0:T(8,128)(2,1)} %collective-permute-done.refs_2_, bf16[196,2560]{1,0:T(8,128)(2,1)} %copy-done.13, bf16[196,2560]{1,0:T(8,128)(2,1)} %copy-done.9, ...), custom_call_target="tpu_custom_call" | custom-call | flops 6936330240 | bytes 17940480 | tf_op jit(solution)/shard_map/pallas_call | solution.py:96
  118.8 2.1 %collective-permute-done.16.refs_1_ = bf16[196,2560]{1,0:T(8,128)(2,1)S(1)} collective-permute-done((bf16[196,2560]{1,0:T(8,128)(2,1)S(1)}, bf16[196,2560]{1,0:T(8,128)(2,1)S(1)}, u32[]{:S(2)}, u32[]{:S(2)}) %collective-permute-start.16) | collective-permute-done | bytes 1003552 | tf_op jit(solution)/shard_map/ppermute | solution.py:157
  120.9 1.5 collective-permute-done.17.refs_3_
  122.4 2.7 %copy-done.1 = bf16[4608,640]{1,0:T(8,128)(2,1)S(1)} copy-done((bf16[4608,640]{1,0:T(8,128)(2,1)S(1)}, bf16[4608,640]{1,0:T(8,128)(2,1)}, u32[]{:S(2)}) %copy-start.1) | copy-done | bytes 5898264
  125.1 1.3 copy-done.2
  126.4 4.9 %shard_map.57 = f32[640,512]{1,0:T(8,128)S(1)} custom-call(bf16[196,2560]{1,0:T(8,128)(2,1)S(1)} %collective-permute-done.4.refs_0_, bf16[196,2560]{1,0:T(8,128)(2,1)S(1)} %collective-permute-done.16.refs_1_, bf16[196,2560]{1,0:T(8,128)(2,1)S(1)} %collective-permute-done.5.refs_2_, bf16[196,2560]{1,0:T(8,128)(2,1)S(1)} %collective-permute-done.17.refs_3_, ...), custom_call_target="tpu_custom_call" | custom-call | flops 2312110080 | bytes 9912320 | tf_op jit(solution)/shard_map/pallas_call | solution.py:96
  131.4 20.1 %all_to_all.5 = f16[16,40,512]{2,1,0:T(8,128)(2,1)S(1)} all-to-all(f16[16,40,512]{2,1,0:T(8,128)(2,1)S(1)} %bitcast.32), channel_id=1, replica_groups=mesh['img'=16,'own'=8] {'img'}, dimensions={0} | all-to-all | bytes 1310720 | tf_op jit(solution)/shard_map/all_to_all | solution.py:216
  (82 shorter events, 8.7 us)
Async XLA Ops:
  6.5 27.2 %copy-start = (bf16[512,512]{1,0:T(8,128)(2,1)S(1)}, bf16[512,512]{1,0:T(8,128)(2,1)}, u32[]{:S(2)}) copy-start(bf16[512,512]{1,0:T(8,128)(2,1)} %param.7) | copy-start | bytes 1572868
  6.5 90.2 %all-gather.2.cloned.1.call-start = ((), (), s32[]{:S(2)}) async-start(), calls=%async_computation.1 | async-start | bytes 6266880 | tf_op jit(solution)/shard_map/all_gather | solution.py:184
  12.1 2.3 %collective-permute-start.12 = (bf16[4,144,288]{2,1,0:T(8,128)(2,1)}, bf16[4,144,288]{2,1,0:T(8,128)(2,1)S(1)}, u32[]{:S(2)}, u32[]{:S(2)}) collective-permute-start(bf16[4,144,288]{2,1,0:T(8,128)(2,1)} %get-tuple-element.27), channel_id=1, source_target_pairs={{0,1},{1,0},{2,3},{3,2},{4,5},{5,4},{6,7},{7,6},{8,9},{9,8},{10,11... | collective-permute-start | bytes 995336 | tf_op jit(solution)/shard_map/ppermute | solution.py:157
  15.6 10.2 %collective-permute-start.13 = (bf16[2,144,288]{2,1,0:T(8,128)(2,1)S(1)}, bf16[2,144,288]{2,1,0:T(8,128)(2,1)S(1)}, u32[]{:S(2)}, u32[]{:S(2)}) collective-permute-start(bf16[2,144,288]{2,1,0:T(8,128)(2,1)S(1)} %get-tuple-element.32), channel_id=1, source_target_pairs={{0,2},{1,3},{2,4},{3,5},{4,6},{5,7},{6,0},{7,1},{8,10},{9,11},{10,... | collective-permute-start | bytes 497672 | tf_op jit(solution)/shard_map/ppermute | solution.py:153
  17.7 14.1 %collective-permute-start.14 = (bf16[2,144,288]{2,1,0:T(8,128)(2,1)S(1)}, bf16[2,144,288]{2,1,0:T(8,128)(2,1)S(1)}, u32[]{:S(2)}, u32[]{:S(2)}) collective-permute-start(bf16[2,144,288]{2,1,0:T(8,128)(2,1)S(1)} %get-tuple-element.34), channel_id=1, source_target_pairs={{0,4},{1,5},{2,6},{3,7},{4,0},{5,1},{6,2},{7,3},{8,12},{9,13},{10,... | collective-permute-start | bytes 497672 | tf_op jit(solution)/shard_map/ppermute | solution.py:153
  21.3 10.5 %collective-permute-start.15 = (bf16[2,144,288]{2,1,0:T(8,128)(2,1)S(1)}, bf16[2,144,288]{2,1,0:T(8,128)(2,1)S(1)}, u32[]{:S(2)}, u32[]{:S(2)}) collective-permute-start(bf16[2,144,288]{2,1,0:T(8,128)(2,1)S(1)} %get-tuple-element.33), channel_id=1, source_target_pairs={{0,6},{1,7},{2,0},{3,1},{4,2},{5,3},{6,4},{7,5},{8,14},{9,15},{10,... | collective-permute-start | bytes 497672 | tf_op jit(solution)/shard_map/ppermute | solution.py:153
  34.9 53.7 %copy-start.5 = (bf16[196,2560]{1,0:T(8,128)(2,1)}, bf16[196,2560]{1,0:T(8,128)(2,1)S(1)}, u32[]{:S(2)}) copy-start(bf16[196,2560]{1,0:T(8,128)(2,1)S(1)} %pad_maximum_fusion.refs_6_) | copy-start | bytes 3010564
  34.9 24.4 %collective-permute-start.1 = (bf16[196,2560]{1,0:T(8,128)(2,1)S(1)}, bf16[196,2560]{1,0:T(8,128)(2,1)}, u32[]{:S(2)}, u32[]{:S(2)}) collective-permute-start(bf16[196,2560]{1,0:T(8,128)(2,1)S(1)} %pad_maximum_fusion.refs_6_), channel_id=1, source_target_pairs={{0,6},{1,7},{2,0},{3,1},{4,2},{5,3},{6,4},{7,5},{8,14},{9,15},{10,... | collective-permute-start | bytes 3010568 | tf_op jit(solution)/shard_map/ppermute | solution.py:153
  37.2 53.1 %copy-start.6 = (bf16[196,2560]{1,0:T(8,128)(2,1)}, bf16[196,2560]{1,0:T(8,128)(2,1)S(1)}, u32[]{:S(2)}) copy-start(bf16[196,2560]{1,0:T(8,128)(2,1)S(1)} %slice.24.refs_0_) | copy-start | bytes 3010564
  37.2 25.6 %collective-permute-start = (bf16[196,2560]{1,0:T(8,128)(2,1)S(1)}, bf16[196,2560]{1,0:T(8,128)(2,1)}, u32[]{:S(2)}, u32[]{:S(2)}) collective-permute-start(bf16[196,2560]{1,0:T(8,128)(2,1)S(1)} %slice.24.refs_0_), channel_id=1, source_target_pairs={{0,2},{1,3},{2,4},{3,5},{4,6},{5,7},{6,0},{7,1},{8,10},{9,11},{10,... | collective-permute-start | bytes 3010568 | tf_op jit(solution)/shard_map/ppermute | solution.py:153
  62.9 24.6 %collective-permute-start.2 = (bf16[196,2560]{1,0:T(8,128)(2,1)S(1)}, bf16[196,2560]{1,0:T(8,128)(2,1)S(1)}, u32[]{:S(2)}, u32[]{:S(2)}) collective-permute-start(bf16[196,2560]{1,0:T(8,128)(2,1)S(1)} %pad_maximum_fusion.refs_6_), channel_id=1, source_target_pairs={{0,2},{1,3},{2,4},{3,5},{4,6},{5,7},{6,0},{7,1},{8,10},{9,11},{10,... | collective-permute-start | bytes 3010568 | tf_op jit(solution)/shard_map/ppermute | solution.py:153
  62.9 24.6 %collective-permute-start.3 = (bf16[196,2560]{1,0:T(8,128)(2,1)S(1)}, bf16[196,2560]{1,0:T(8,128)(2,1)S(1)}, u32[]{:S(2)}, u32[]{:S(2)}) collective-permute-start(bf16[196,2560]{1,0:T(8,128)(2,1)S(1)} %slice.24.refs_0_), channel_id=1, source_target_pairs={{0,6},{1,7},{2,0},{3,1},{4,2},{5,3},{6,4},{7,5},{8,14},{9,15},{10,... | collective-permute-start | bytes 3010568 | tf_op jit(solution)/shard_map/ppermute | solution.py:153
  66.1 22.0 %collective-permute-start.6 = (bf16[196,2560]{1,0:T(8,128)(2,1)S(1)}, bf16[196,2560]{1,0:T(8,128)(2,1)S(1)}, u32[]{:S(2)}, u32[]{:S(2)}) collective-permute-start(bf16[196,2560]{1,0:T(8,128)(2,1)S(1)} %slice.24.refs_0_), channel_id=1, source_target_pairs={{0,1},{1,0},{2,3},{3,2},{4,5},{5,4},{6,7},{7,6},{8,9},{9,8},{10,11... | collective-permute-start | bytes 3010568 | tf_op jit(solution)/shard_map/ppermute | solution.py:157
  66.1 22.4 %collective-permute-start.9 = (bf16[196,2560]{1,0:T(8,128)(2,1)S(1)}, bf16[196,2560]{1,0:T(8,128)(2,1)S(1)}, u32[]{:S(2)}, u32[]{:S(2)}) collective-permute-start(bf16[196,2560]{1,0:T(8,128)(2,1)S(1)} %pad_maximum_fusion.refs_6_), channel_id=1, source_target_pairs={{0,1},{1,0},{2,3},{3,2},{4,5},{5,4},{6,7},{7,6},{8,9},{9,8},{10,11... | collective-permute-start | bytes 3010568 | tf_op jit(solution)/shard_map/ppermute | solution.py:157
  87.4 7.3 %copy-start.9 = (bf16[196,2560]{1,0:T(8,128)(2,1)}, bf16[196,2560]{1,0:T(8,128)(2,1)S(1)}, u32[]{:S(2)}) copy-start(bf16[196,2560]{1,0:T(8,128)(2,1)S(1)} %collective-permute-done.3.refs_4_) | copy-start | bytes 3010564
  87.4 2.9 %collective-permute-start.11 = (bf16[196,2560]{1,0:T(8,128)(2,1)}, bf16[196,2560]{1,0:T(8,128)(2,1)S(1)}, u32[]{:S(2)}, u32[]{:S(2)}) collective-permute-start(bf16[196,2560]{1,0:T(8,128)(2,1)} %collective-permute-done.1.refs_10_), channel_id=1, source_target_pairs={{0,1},{1,0},{2,3},{3,2},{4,5},{5,4},{6,7},{7,6},{8,9},{9,8},{10,11... | collective-permute-start | bytes 3010568 | tf_op jit(solution)/shard_map/ppermute | solution.py:157
  87.5 7.2 %collective-permute-start.7 = (bf16[196,2560]{1,0:T(8,128)(2,1)}, bf16[196,2560]{1,0:T(8,128)(2,1)S(1)}, u32[]{:S(2)}, u32[]{:S(2)}) collective-permute-start(bf16[196,2560]{1,0:T(8,128)(2,1)} %collective-permute-done.refs_2_), channel_id=1, source_target_pairs={{0,1},{1,0},{2,3},{3,2},{4,5},{5,4},{6,7},{7,6},{8,9},{9,8},{10,11... | collective-permute-start | bytes 3010568 | tf_op jit(solution)/shard_map/ppermute | solution.py:157
  88.0 6.7 %collective-permute-start.10 = (bf16[196,2560]{1,0:T(8,128)(2,1)S(1)}, bf16[196,2560]{1,0:T(8,128)(2,1)S(1)}, u32[]{:S(2)}, u32[]{:S(2)}) collective-permute-start(bf16[196,2560]{1,0:T(8,128)(2,1)S(1)} %collective-permute-done.2.refs_8_), channel_id=1, source_target_pairs={{0,1},{1,0},{2,3},{3,2},{4,5},{5,4},{6,7},{7,6},{8,9},{9,8},{10,11... | collective-permute-start | bytes 3010568 | tf_op jit(solution)/shard_map/ppermute | solution.py:157
  88.1 6.6 %copy-start.10 = (bf16[196,2560]{1,0:T(8,128)(2,1)}, bf16[196,2560]{1,0:T(8,128)(2,1)S(1)}, u32[]{:S(2)}) copy-start(bf16[196,2560]{1,0:T(8,128)(2,1)S(1)} %collective-permute-done.6.refs_1_) | copy-start | bytes 3010564
  88.1 8.6 %collective-permute-start.8 = (bf16[196,2560]{1,0:T(8,128)(2,1)S(1)}, bf16[196,2560]{1,0:T(8,128)(2,1)}, u32[]{:S(2)}, u32[]{:S(2)}) collective-permute-start(bf16[196,2560]{1,0:T(8,128)(2,1)S(1)} %collective-permute-done.3.refs_4_), channel_id=1, source_target_pairs={{0,1},{1,0},{2,3},{3,2},{4,5},{5,4},{6,7},{7,6},{8,9},{9,8},{10,11... | collective-permute-start | bytes 3010568 | tf_op jit(solution)/shard_map/ppermute | solution.py:157
  88.5 29.7 %collective-permute-start.4 = (bf16[196,2560]{1,0:T(8,128)(2,1)}, bf16[196,2560]{1,0:T(8,128)(2,1)S(1)}, u32[]{:S(2)}, u32[]{:S(2)}) collective-permute-start(bf16[196,2560]{1,0:T(8,128)(2,1)} %collective-permute-done.refs_2_), channel_id=1, source_target_pairs={{0,2},{1,3},{2,4},{3,5},{4,6},{5,7},{6,0},{7,1},{8,10},{9,11},{10,... | collective-permute-start | bytes 3010568 | tf_op jit(solution)/shard_map/ppermute | solution.py:153
  90.3 27.9 %collective-permute-start.5 = (bf16[196,2560]{1,0:T(8,128)(2,1)}, bf16[196,2560]{1,0:T(8,128)(2,1)S(1)}, u32[]{:S(2)}, u32[]{:S(2)}) collective-permute-start(bf16[196,2560]{1,0:T(8,128)(2,1)} %collective-permute-done.1.refs_10_), channel_id=1, source_target_pairs={{0,6},{1,7},{2,0},{3,1},{4,2},{5,3},{6,4},{7,5},{8,14},{9,15},{10,... | collective-permute-start | bytes 3010568 | tf_op jit(solution)/shard_map/ppermute | solution.py:153
  118.2 2.7 %collective-permute-start.16 = (bf16[196,2560]{1,0:T(8,128)(2,1)S(1)}, bf16[196,2560]{1,0:T(8,128)(2,1)S(1)}, u32[]{:S(2)}, u32[]{:S(2)}) collective-permute-start(bf16[196,2560]{1,0:T(8,128)(2,1)S(1)} %collective-permute-done.4.refs_0_), channel_id=1, source_target_pairs={{0,1},{1,0},{2,3},{3,2},{4,5},{5,4},{6,7},{7,6},{8,9},{9,8},{10,11... | collective-permute-start | bytes 3010568 | tf_op jit(solution)/shard_map/ppermute | solution.py:157
  118.5 4.0 %collective-permute-start.17 = (bf16[196,2560]{1,0:T(8,128)(2,1)S(1)}, bf16[196,2560]{1,0:T(8,128)(2,1)S(1)}, u32[]{:S(2)}, u32[]{:S(2)}) collective-permute-start(bf16[196,2560]{1,0:T(8,128)(2,1)S(1)} %collective-permute-done.5.refs_2_), channel_id=1, source_target_pairs={{0,1},{1,0},{2,3},{3,2},{4,5},{5,4},{6,7},{7,6},{8,9},{9,8},{10,11... | collective-permute-start | bytes 3010568 | tf_op jit(solution)/shard_map/ppermute | solution.py:157
  (11 other events, 34.0 us)
Sparse Core Ops, SparseCore 0:
  33.8 59.9 all-gather.1

commit v4 on v3

--- a/solution.py
+++ b/solution.py
@@ -11,32 +11,38 @@
 CHIPS = 4
 CORES = 2
 TOP = 13.0
+LIMITS = {"near": 54, "far": 28, "last": 28}
 F32, BF16, I32 = jnp.float32, jnp.bfloat16, jnp.int32
 
 
-def accumulate(n, chunk, staged, block, *refs):
+def accumulate(n, chunk, mode, block, *refs):
     lows, highs = refs[:n], refs[n : 2 * n]
-    basis, *before, out, flip, total = refs[2 * n : len(refs) - (6 if staged else 0)]
-    total = out if staged else total
+    staged = mode == "near"
+    before = []
+    if staged:
+        basis, total, flip, held, basis_sems, low, high, low_sems, high_sems = refs[2 * n :]
+    elif mode == "far":
+        basis, total, flip = refs[2 * n :]
+    else:
+        basis, *before, out, flip, total = refs[2 * n :]
     rows, half = lows[0].shape
     kin, cols = basis.shape
     rest = kin - half
     gout = half - rest
-    parts = 4
+    parts = 2
     if staged:
-        low, high, held, low_sems, high_sems, basis_sems = refs[-6:]
         lefts = [pltpu.make_async_copy(lows[k], low.at[k % 2], low_sems.at[k % 2]) for k in range(n)]
         rights = [pltpu.make_async_copy(highs[k], high.at[k % 2], high_sems.at[k % 2]) for k in range(n)]
+        lows, highs = [low.at[k % 2] for k in range(n)], [high.at[k % 2] for k in range(n)]
+        lefts[0].start()
         edges = [half * i // parts for i in range(parts)] + [half + rest * i // parts for i in range(parts + 1)]
         spans = [pl.ds(a, b - a) for a, b in zip(edges, edges[1:])]
         pieces = [pltpu.make_async_copy(basis.at[s], held.at[s], basis_sems.at[i]) for i, s in enumerate(spans)]
-        lefts[0].start()
-        for piece in pieces[:parts]:
+        for i, piece in enumerate(pieces):
+            if i == parts:
+                rights[0].start()
             piece.start()
-        rights[0].start()
-        for piece in pieces[parts:]:
-            piece.start()
-        lows, highs, basis = [low.at[k % 2] for k in range(n)], [high.at[k % 2] for k in range(n)], held
+        basis = held
     image = lax.broadcasted_iota(I32, (rows, gout), 0) // POS
     for k in range(n):
         if staged:
@@ -63,51 +69,50 @@
         flip[k % 2] = proj.astype(BF16).T
         grads = highs[k][:, rest:]
         apart = [jnp.where(image == m, grads, jnp.zeros_like(grads)) for m in range(rows // POS)]
-        source = total if k else before[0] if before else None
+        sources = [total] if k else before
         for s in range(0, cols, chunk):
             left = flip[k % 2, s : s + chunk]
-            squares = jnp.zeros((chunk, gout), F32) if source is None else source[s : s + chunk]
+            squares = jnp.zeros((chunk, gout), F32)
+            for source in sources:
+                squares += source[s : s + chunk]
             for one in apart:
                 coef = jnp.dot(left, one, preferred_element_type=F32)
                 squares += coef * coef
             total[s : s + chunk] = squares
-    if not staged:
+    if block:
         peak = jnp.max(jnp.max(total[...], axis=0, keepdims=True), axis=1, keepdims=True)
         level = jnp.floor(jnp.log(jnp.maximum(peak, 1e-30)) * 1.4426950408889634)
         row = lax.rem(lax.broadcasted_iota(I32, (cols, gout), 0), jnp.int32(block[1]))
         out[...] = jnp.where(row == block[0], level, total[...] * jnp.exp2(TOP - level))
 
 
-def added(lows, highs, basis, *before, staged=False, block=()):
-    n = len(lows)
+def added(mode, pairs, basis, *before, block=()):
+    n = len(pairs)
+    lows, highs = zip(*pairs)
     rows, half = lows[0].shape
     kin, cols = basis.shape
     gout = 2 * half - kin
-    inside = pl.BlockSpec(memory_space=pltpu.VMEM)
-    source = pl.BlockSpec(memory_space=pltpu.HBM) if staged else inside
-    room = [
-        pltpu.VMEM((2, rows, half), BF16),
-        pltpu.VMEM((2, rows, half), BF16),
-        pltpu.VMEM((kin, cols), BF16),
-        pltpu.SemaphoreType.DMA((2,)),
-        pltpu.SemaphoreType.DMA((2,)),
-        pltpu.SemaphoreType.DMA((8,)),
-    ]
+    inside, outside = pl.BlockSpec(memory_space=pltpu.VMEM), pl.BlockSpec(memory_space=pltpu.HBM)
+    room = [pltpu.VMEM((2, cols, rows), BF16)]
+    if mode == "near":
+        pair, sems = pltpu.VMEM((2, rows, half), BF16), pltpu.SemaphoreType.DMA
+        room += [pltpu.VMEM((kin, cols), BF16), sems((4,)), pair, pair, sems((2,)), sems((2,))]
+    elif mode == "last":
+        room += [pltpu.VMEM((cols, gout), F32)]
     return pl.pallas_call(
-        functools.partial(accumulate, n, cols // 2, staged, block),
+        functools.partial(accumulate, n, cols // 2, mode, block),
         out_shape=jax.ShapeDtypeStruct((cols, gout), F32),
-        in_specs=[source] * (2 * n + 1) + [inside] * len(before),
+        in_specs=[outside if mode == "near" else inside] * (2 * n + 1) + [inside] * len(before),
         out_specs=inside,
-        scratch_shapes=[pltpu.VMEM((2, cols, rows), BF16), pltpu.VMEM((8, 128) if staged else (cols, gout), F32)]
-        + (room if staged else []),
-        compiler_params=pltpu.CompilerParams(vmem_limit_bytes=(60 if staged else 28) << 20),
+        scratch_shapes=room,
+        compiler_params=pltpu.CompilerParams(vmem_limit_bytes=LIMITS[mode] << 20),
         cost_estimate=pl.CostEstimate(
             flops=2 * n * rows * kin * cols, bytes_accessed=4 * n * rows * half + 2 * kin * cols, transcendentals=0
         ),
     )(*lows, *highs, basis, *before)
 
 
-def place(blk, ring, me, counts, slots, kept, given, held, sem):
+def place(blk, ring, me, counts, slots, kept, given, held, hot, sem):
     depth, cap = held.shape
     owners = CHIPS * CORES
     stripe, per = blk * owners, ring // owners
@@ -124,13 +129,14 @@
     hop = ((goal // CORES - z + CHIPS) & (CHIPS - 1)) + CHIPS * ((goal & 1) ^ c)
     row = hop * per + lax.div(spot, jnp.int32(stripe)) * blk + lax.rem(spot, jnp.int32(blk))
     row = jnp.where(slot < counts[own], row, -1)
-    copy.wait()
     for r in range(0, ring, per):
         here = lax.broadcasted_iota(I32, (per, cap), 0) + r == row
+        hot[r : r + per] = here.astype(F32).astype(BF16)
+    copy.wait()
+    laid = lax.dot_general(hot[...], held[...], (((1,), (1,)), ((), ())), preferred_element_type=F32).astype(BF16)
+    for r in range(0, ring, per):
         out = kept if r < ring // CORES else given
-        out[r % (ring // CORES) // per] = lax.dot_general(
-            here.astype(F32).astype(BF16), held[...], (((1,), (1,)), ((), ())), preferred_element_type=F32
-        ).astype(BF16)
+        out[r % (ring // CORES) // per] = laid[r : r + per]
 
 
 def placed(basis_slots, col_counts, img, own, groups, blk, ring):
@@ -142,7 +148,7 @@
         out_shape=[jax.ShapeDtypeStruct((CHIPS, ring // CHIPS // CORES, depth), BF16)] * CORES,
         in_specs=[scalars, scalars, pl.BlockSpec(memory_space=pltpu.HBM)],
         out_specs=[pl.BlockSpec(memory_space=pltpu.VMEM)] * CORES,
-        scratch_shapes=[pltpu.VMEM((depth, cap), BF16), pltpu.SemaphoreType.DMA],
+        scratch_shapes=[pltpu.VMEM((depth, cap), BF16), pltpu.VMEM((ring, cap), BF16), pltpu.SemaphoreType.DMA],
         compiler_params=pltpu.CompilerParams(vmem_limit_bytes=55 << 20),
         cost_estimate=pl.CostEstimate(flops=2 * ring * cap * depth, bytes_accessed=4 * depth * cap, transcendentals=0),
     )(jnp.stack([img, own]).astype(I32), col_counts, basis_slots)
@@ -186,15 +192,16 @@
 
 def gathered(low, high):
     low_down, high_up = up(low, 1), up(high, -1)
-    low, high, low_down, high_up = lax.optimization_barrier((low, high, low_down, high_up))
+    mine = (low, high, swap(low), swap(high))
+    low, high, low_down, high_up, mine = lax.optimization_barrier((low, high, low_down, high_up, mine))
     high_down, low_up = up(high, 1), up(low, -1)
-    low_down, high_up, high_down, low_up = lax.optimization_barrier((low_down, high_up, high_down, low_up))
-    low_far, high_far = up(low_down, 1), up(high_up, -1)
-    return [low, low_down, low_up, low_far], [high, high_down, high_up, high_far]
-
-
-def shared(arrays):
-    return [b for a in arrays for b in (a, swap(a))]
+    other_low, other_high = swap(low_down), swap(high_up)
+    low_down, high_up, high_down, low_up, other_low, other_high = lax.optimization_barrier(
+        (low_down, high_up, high_down, low_up, other_low, other_high)
+    )
+    far = (up(low_down, 1), up(high_up, -1))
+    pairs = [mine[:2], mine[2:], (low_down, high_down), (other_low, swap(high_down)), (low_up, high_up)]
+    return pairs + [(swap(low_up), other_high)], far
 
 
 def shards(patches, grads, basis_g, basis_slots, col_counts):
@@ -207,12 +214,14 @@
     proj = jnp.dot(grads, basis_g, preferred_element_type=F32).astype(BF16)
     half = (kin + gout) // 2
     low, high = patches[:, :half], jnp.concatenate([patches[:, half:], proj], axis=1)
-    lows, highs = gathered(low, high)
+    near, far = gathered(low, high)
     wide = -(-(blk + 1) // 8) * 8
     basis = balanced_basis(basis_slots, col_counts, img, own, groups, blk, wide)
-    total = added(shared(lows[:-1]), shared(highs[:-1]), basis, staged=True)
-    low, high, total = lax.optimization_barrier((lows[-1], highs[-1], total))
-    total = added(shared([low]), shared([high]), basis, total, block=(blk, wide))
+    sums = added("near", near, basis)
+    far, sums = lax.optimization_barrier((far, sums))
+    partner = swap(far[0]), swap(far[1])
+    more = added("far", [far], basis)
+    total = added("last", [partner], basis, more, sums, block=(blk, wide))
     parts = lax.all_to_all(total.astype(jnp.float16).reshape(groups, wide, gout), "img", 0, 0, tiled=True)
     level = parts[:, blk : blk + 1, :1].astype(F32) - TOP
     return jnp.sum(parts[:, :blk].astype(F32) * jnp.exp2(level), axis=0) / F32(owners * rows // POS * groups)

time: 160 us -> 151 us (0.944)
  local copies, waits for them, and re-layouts: 8.77 us -> 3.8 us
  waiting for transfers between devices: 62.7 us -> 60.3 us
    ppermute x9, waiting for transfers between devices: 6.89 us -> 1.77 us  [swap(): return lax.ppermute(a, 'own', [(o, o ^ 1) for o in range(CHIPS * CORES)])]
    unnamed x31, local copies, waits for them, and re-layouts: 6.1 us -> 1.13 us
    ppermute x9, waiting for transfers between devices: 55.8 us -> 58.5 us  [up(): return lax.ppermute(a, 'own', pairs)]
    pallas_call x2 -> x3, Pallas kernels: 26.4 us -> 25.7 us  [added(): pl.pallas_call(functools.partial(accumulate, n, cols // 2, mode, block),...]
  transfers between devices with their start and end apart: 19 -> 19, of which waited for: 9 -> 8; matrix products, arithmetic and copies ran while one was open for 2% -> 2% of each run, Pallas kernels for 13% -> 15%
where the time goes in v4:
time: 151 us
  waiting for transfers between devices  60.3 us (40%)
  Pallas kernels  30 us (20%)
  blocking collectives  20.1 us (13%)
  starting transfers between devices  17.7 us (12%)
  between operations  13.7 us (9%)
  local copies, waits for them, and re-layouts  3.8 us (3%)
  other arithmetic  3.47 us (2%)
  matrix products  1.9 us (1%)
    ppermute x9, waiting for transfers between devices, up(): return lax.ppermute(a, 'own', pairs)  58.5 us
    pallas_call x3, Pallas kernels, added(): pl.pallas_call(functools.partial(accumulate, n, cols // 2, mode, block),...  25.7 us
    all_to_all x1, blocking collectives, shards(): lax.all_to_all(total.astype(jnp.float16).reshape(groups, wide, gout), 'im...  20.1 us
    ppermute x9, starting transfers between devices, up(): return lax.ppermute(a, 'own', pairs)  15.5 us
    pallas_call x1, Pallas kernels, placed(): pl.pallas_call(functools.partial(place, blk, ring), out_shape=[jax.ShapeD...  4.39 us
  transfers between devices with their start and end apart: 19, of which 8 were waited for; matrix products, arithmetic and copies ran while one was open for 2% of the time, Pallas kernels for 15%

profile of v4, /device:TPU:0, one launch (start us, length us, event | category | flops | bytes accessed | tf_op | source)
XLA Modules:
  0.0 151.0 jit_solution(286852444872612115)
XLA Ops:
  6.5 0.7 pad_add_fusion.me
  7.2 4.4 %shard_map.55 = (bf16[4,144,288]{2,1,0:T(8,128)(2,1)}, bf16[4,144,288]{2,1,0:T(8,128)(2,1)}) custom-call(s32[2]{0:T(128)} %pad_add_fusion.me, s32[8]{0:T(128)} %counts.1, bf16[4608,1152]{1,0:T(8,128)(2,1)} %slots.1), custom_call_target="tpu_custom_call" | custom-call | flops 764411904 | bytes 1327104 | tf_op jit(solution)/shard_map/pallas_call | solution.py:146
  12.8 0.6 gather_fusion
  13.9 1.2 fusion.6
  15.1 2.1 %collective-permute-start.13 = (bf16[2,144,288]{2,1,0:T(8,128)(2,1)S(1)}, bf16[2,144,288]{2,1,0:T(8,128)(2,1)S(1)}, u32[]{:S(2)}, u32[]{:S(2)}) collective-permute-start(bf16[2,144,288]{2,1,0:T(8,128)(2,1)S(1)} %get-tuple-element.44), channel_id=1, source_target_pairs={{0,2},{1,3},{2,4},{3,5},{4,6},{5,7},{6,0},{7,1},{8,10},{9,11},{10,... | collective-permute-start | bytes 497672 | tf_op jit(solution)/shard_map/ppermute | solution.py:159
  17.2 3.6 %collective-permute-start.14 = (bf16[2,144,288]{2,1,0:T(8,128)(2,1)S(1)}, bf16[2,144,288]{2,1,0:T(8,128)(2,1)S(1)}, u32[]{:S(2)}, u32[]{:S(2)}) collective-permute-start(bf16[2,144,288]{2,1,0:T(8,128)(2,1)S(1)} %get-tuple-element.46), channel_id=1, source_target_pairs={{0,4},{1,5},{2,6},{3,7},{4,0},{5,1},{6,2},{7,3},{8,12},{9,13},{10,... | collective-permute-start | bytes 497672 | tf_op jit(solution)/shard_map/ppermute | solution.py:159
  20.7 1.0 collective-permute-start.15
  21.8 3.5 %collective-permute-done.13 = bf16[2,144,288]{2,1,0:T(8,128)(2,1)S(1)} collective-permute-done((bf16[2,144,288]{2,1,0:T(8,128)(2,1)S(1)}, bf16[2,144,288]{2,1,0:T(8,128)(2,1)S(1)}, u32[]{:S(2)}, u32[]{:S(2)}) %collective-permute-start.13) | collective-permute-done | bytes 165920 | tf_op jit(solution)/shard_map/ppermute | solution.py:159
  25.3 5.9 %collective-permute-done.14 = bf16[2,144,288]{2,1,0:T(8,128)(2,1)S(1)} collective-permute-done((bf16[2,144,288]{2,1,0:T(8,128)(2,1)S(1)}, bf16[2,144,288]{2,1,0:T(8,128)(2,1)S(1)}, u32[]{:S(2)}, u32[]{:S(2)}) %collective-permute-start.14) | collective-permute-done | bytes 165920 | tf_op jit(solution)/shard_map/ppermute | solution.py:159
  31.5 1.6 %fusion.2 = bf16[288,640]{1,0:T(8,128)(2,1)} fusion(bf16[1152,288]{1,0:T(8,128)(2,1)S(1)} %bitcast.33, s32[1152]{0:T(1024)S(1)} %fusion.12), kind=kOutput, calls=%fused_computation.6 | convolution fusion | flops 425594880 | bytes 1036800 | tf_op jit(solution)/shard_map/dot_general | solution.py:187
  33.4 0.8 slice-done
  34.3 2.3 %collective-permute-start.1 = (bf16[196,2560]{1,0:T(8,128)(2,1)S(1)}, bf16[196,2560]{1,0:T(8,128)(2,1)}, u32[]{:S(2)}, u32[]{:S(2)}) collective-permute-start(bf16[196,2560]{1,0:T(8,128)(2,1)S(1)} %pad_maximum_fusion.refs_6_), channel_id=1, source_target_pairs={{0,6},{1,7},{2,0},{3,1},{4,2},{5,3},{6,4},{7,5},{8,14},{9,15},{10,... | collective-permute-start | bytes 3010568 | tf_op jit(solution)/shard_map/ppermute | solution.py:159
  37.4 21.4 %collective-permute-done.1.refs_10_ = bf16[196,2560]{1,0:T(8,128)(2,1)} collective-permute-done((bf16[196,2560]{1,0:T(8,128)(2,1)S(1)}, bf16[196,2560]{1,0:T(8,128)(2,1)}, u32[]{:S(2)}, u32[]{:S(2)}) %collective-permute-start.1) | collective-permute-done | bytes 1003552 | tf_op jit(solution)/shard_map/ppermute | solution.py:159
  58.7 4.4 %collective-permute-done.refs_2_ = bf16[196,2560]{1,0:T(8,128)(2,1)} collective-permute-done((bf16[196,2560]{1,0:T(8,128)(2,1)S(1)}, bf16[196,2560]{1,0:T(8,128)(2,1)}, u32[]{:S(2)}, u32[]{:S(2)}) %collective-permute-start) | collective-permute-done | bytes 1003552 | tf_op jit(solution)/shard_map/ppermute | solution.py:159
  63.6 3.2 %collective-permute-start.5 = (bf16[196,2560]{1,0:T(8,128)(2,1)S(1)}, bf16[196,2560]{1,0:T(8,128)(2,1)S(1)}, u32[]{:S(2)}, u32[]{:S(2)}) collective-permute-start(bf16[196,2560]{1,0:T(8,128)(2,1)S(1)} %slice.24.refs_0_), channel_id=1, source_target_pairs={{0,6},{1,7},{2,0},{3,1},{4,2},{5,3},{6,4},{7,5},{8,14},{9,15},{10,... | collective-permute-start | bytes 3010568 | tf_op jit(solution)/shard_map/ppermute | solution.py:159
  67.4 22.0 %collective-permute-done.4.refs_8_ = bf16[196,2560]{1,0:T(8,128)(2,1)S(1)} collective-permute-done((bf16[196,2560]{1,0:T(8,128)(2,1)S(1)}, bf16[196,2560]{1,0:T(8,128)(2,1)S(1)}, u32[]{:S(2)}, u32[]{:S(2)}) %collective-permute-start.4) | collective-permute-done | bytes 1003552 | tf_op jit(solution)/shard_map/ppermute | solution.py:159
  90.1 3.2 %collective-permute-start.9 = (bf16[196,2560]{1,0:T(8,128)(2,1)}, bf16[196,2560]{1,0:T(8,128)(2,1)S(1)}, u32[]{:S(2)}, u32[]{:S(2)}) collective-permute-start(bf16[196,2560]{1,0:T(8,128)(2,1)} %collective-permute-done.1.refs_10_), channel_id=1, source_target_pairs={{0,6},{1,7},{2,0},{3,1},{4,2},{5,3},{6,4},{7,5},{8,14},{9,15},{10,... | collective-permute-start | bytes 3010568 | tf_op jit(solution)/shard_map/ppermute | solution.py:159
  93.4 1.0 copy-done.14
  94.3 20.5 %shard_map.56.refs_4_ = f32[640,512]{1,0:T(8,128)} custom-call(bf16[196,2560]{1,0:T(8,128)(2,1)} %copy-done.6, bf16[196,2560]{1,0:T(8,128)(2,1)} %copy-done.9, bf16[196,2560]{1,0:T(8,128)(2,1)} %collective-permute-done.refs_2_, bf16[196,2560]{1,0:T(8,128)(2,1)} %copy-done.10, bf16[196,2560]{1,0:T(8,128)(2,1)} %copy-done.13, bf16[196,2560]{1,0:T(8,128)(2,1)} %copy-done.14, ...), custom_call_target="tpu_custom_call" | custom-call | flops 6936330240 | bytes 17940480 | tf_op jit(solution)/shard_map/pallas_call | solution.py:102
  114.9 1.2 collective-permute-done.8.refs_0_
  116.6 2.4 %shard_map.57.refs_3_ = f32[640,512]{1,0:T(8,128)S(1)} custom-call(bf16[196,2560]{1,0:T(8,128)(2,1)S(1)} %collective-permute-done.8.refs_0_, bf16[196,2560]{1,0:T(8,128)(2,1)S(1)} %collective-permute-done.9.refs_1_, bf16[4608,640]{1,0:T(8,128)(2,1)S(1)} %copy-done.1), custom_call_target="tpu_custom_call" | custom-call | flops 1156055040 | bytes 7905280 | tf_op jit(solution)/shard_map/pallas_call | solution.py:102
  119.0 1.2 collective-permute-done.17.refs_1_
  120.2 2.8 %shard_map.58 = f32[640,512]{1,0:T(8,128)S(1)} custom-call(bf16[196,2560]{1,0:T(8,128)(2,1)S(1)} %collective-permute-done.16.refs_0_, bf16[196,2560]{1,0:T(8,128)(2,1)S(1)} %collective-permute-done.17.refs_1_, bf16[4608,640]{1,0:T(8,128)(2,1)S(1)} %copy-done.1, f32[640,512]{1,0:T(8,128)S(1)} %shard_map.57.refs_3_, f32[640,512]{1,0:T(8,128)S(1)} %copy-done.2), custom_call_target="tpu_custom_call" | custom-call | flops 1156055040 | bytes 7905280 | tf_op jit(solution)/shard_map/pallas_call | solution.py:102
  123.1 20.1 %all_to_all.5 = f16[16,40,512]{2,1,0:T(8,128)(2,1)S(1)} all-to-all(f16[16,40,512]{2,1,0:T(8,128)(2,1)S(1)} %bitcast.32), channel_id=1, replica_groups=mesh['img'=16,'own'=8] {'img'}, dimensions={0} | all-to-all | bytes 1310720 | tf_op jit(solution)/shard_map/all_to_all | solution.py:225
  (83 shorter events, 6.2 us)
Async XLA Ops:
  6.5 26.6 %copy-start = (bf16[512,512]{1,0:T(8,128)(2,1)S(1)}, bf16[512,512]{1,0:T(8,128)(2,1)}, u32[]{:S(2)}) copy-start(bf16[512,512]{1,0:T(8,128)(2,1)} %param.7) | copy-start | bytes 1572868
  6.5 87.8 %all-gather.2.cloned.1.call-start = ((), (), s32[]{:S(2)}) async-start(), calls=%async_computation.1 | async-start | bytes 6266880 | tf_op jit(solution)/shard_map/all_gather | solution.py:190
  11.6 2.3 %collective-permute-start.12 = (bf16[4,144,288]{2,1,0:T(8,128)(2,1)}, bf16[4,144,288]{2,1,0:T(8,128)(2,1)S(1)}, u32[]{:S(2)}, u32[]{:S(2)}) collective-permute-start(bf16[4,144,288]{2,1,0:T(8,128)(2,1)} %get-tuple-element.39), channel_id=1, source_target_pairs={{0,1},{1,0},{2,3},{3,2},{4,5},{5,4},{6,7},{7,6},{8,9},{9,8},{10,11... | collective-permute-start | bytes 995336 | tf_op jit(solution)/shard_map/ppermute | solution.py:163
  15.1 10.2 %collective-permute-start.13 = (bf16[2,144,288]{2,1,0:T(8,128)(2,1)S(1)}, bf16[2,144,288]{2,1,0:T(8,128)(2,1)S(1)}, u32[]{:S(2)}, u32[]{:S(2)}) collective-permute-start(bf16[2,144,288]{2,1,0:T(8,128)(2,1)S(1)} %get-tuple-element.44), channel_id=1, source_target_pairs={{0,2},{1,3},{2,4},{3,5},{4,6},{5,7},{6,0},{7,1},{8,10},{9,11},{10,... | collective-permute-start | bytes 497672 | tf_op jit(solution)/shard_map/ppermute | solution.py:159
  17.2 14.1 %collective-permute-start.14 = (bf16[2,144,288]{2,1,0:T(8,128)(2,1)S(1)}, bf16[2,144,288]{2,1,0:T(8,128)(2,1)S(1)}, u32[]{:S(2)}, u32[]{:S(2)}) collective-permute-start(bf16[2,144,288]{2,1,0:T(8,128)(2,1)S(1)} %get-tuple-element.46), channel_id=1, source_target_pairs={{0,4},{1,5},{2,6},{3,7},{4,0},{5,1},{6,2},{7,3},{8,12},{9,13},{10,... | collective-permute-start | bytes 497672 | tf_op jit(solution)/shard_map/ppermute | solution.py:159
  20.7 10.5 %collective-permute-start.15 = (bf16[2,144,288]{2,1,0:T(8,128)(2,1)S(1)}, bf16[2,144,288]{2,1,0:T(8,128)(2,1)S(1)}, u32[]{:S(2)}, u32[]{:S(2)}) collective-permute-start(bf16[2,144,288]{2,1,0:T(8,128)(2,1)S(1)} %get-tuple-element.45), channel_id=1, source_target_pairs={{0,6},{1,7},{2,0},{3,1},{4,2},{5,3},{6,4},{7,5},{8,14},{9,15},{10,... | collective-permute-start | bytes 497672 | tf_op jit(solution)/shard_map/ppermute | solution.py:159
  34.3 55.7 %copy-start.5 = (bf16[196,2560]{1,0:T(8,128)(2,1)}, bf16[196,2560]{1,0:T(8,128)(2,1)S(1)}, u32[]{:S(2)}) copy-start(bf16[196,2560]{1,0:T(8,128)(2,1)S(1)} %pad_maximum_fusion.refs_6_) | copy-start | bytes 3010564
  34.3 24.4 %collective-permute-start.1 = (bf16[196,2560]{1,0:T(8,128)(2,1)S(1)}, bf16[196,2560]{1,0:T(8,128)(2,1)}, u32[]{:S(2)}, u32[]{:S(2)}) collective-permute-start(bf16[196,2560]{1,0:T(8,128)(2,1)S(1)} %pad_maximum_fusion.refs_6_), channel_id=1, source_target_pairs={{0,6},{1,7},{2,0},{3,1},{4,2},{5,3},{6,4},{7,5},{8,14},{9,15},{10,... | collective-permute-start | bytes 3010568 | tf_op jit(solution)/shard_map/ppermute | solution.py:159
  36.6 22.1 %collective-permute-start.3 = (bf16[196,2560]{1,0:T(8,128)(2,1)S(1)}, bf16[196,2560]{1,0:T(8,128)(2,1)S(1)}, u32[]{:S(2)}, u32[]{:S(2)}) collective-permute-start(bf16[196,2560]{1,0:T(8,128)(2,1)S(1)} %pad_maximum_fusion.refs_6_), channel_id=1, source_target_pairs={{0,1},{1,0},{2,3},{3,2},{4,5},{5,4},{6,7},{7,6},{8,9},{9,8},{10,11... | collective-permute-start | bytes 3010568 | tf_op jit(solution)/shard_map/ppermute | solution.py:163
  36.7 53.4 %copy-start.6 = (bf16[196,2560]{1,0:T(8,128)(2,1)}, bf16[196,2560]{1,0:T(8,128)(2,1)S(1)}, u32[]{:S(2)}) copy-start(bf16[196,2560]{1,0:T(8,128)(2,1)S(1)} %slice.24.refs_0_) | copy-start | bytes 3010564
  36.7 26.4 %collective-permute-start = (bf16[196,2560]{1,0:T(8,128)(2,1)S(1)}, bf16[196,2560]{1,0:T(8,128)(2,1)}, u32[]{:S(2)}, u32[]{:S(2)}) collective-permute-start(bf16[196,2560]{1,0:T(8,128)(2,1)S(1)} %slice.24.refs_0_), channel_id=1, source_target_pairs={{0,2},{1,3},{2,4},{3,5},{4,6},{5,7},{6,0},{7,1},{8,10},{9,11},{10,... | collective-permute-start | bytes 3010568 | tf_op jit(solution)/shard_map/ppermute | solution.py:159
  36.8 26.3 %collective-permute-start.2 = (bf16[196,2560]{1,0:T(8,128)(2,1)S(1)}, bf16[196,2560]{1,0:T(8,128)(2,1)S(1)}, u32[]{:S(2)}, u32[]{:S(2)}) collective-permute-start(bf16[196,2560]{1,0:T(8,128)(2,1)S(1)} %slice.24.refs_0_), channel_id=1, source_target_pairs={{0,1},{1,0},{2,3},{3,2},{4,5},{5,4},{6,7},{7,6},{8,9},{9,8},{10,11... | collective-permute-start | bytes 3010568 | tf_op jit(solution)/shard_map/ppermute | solution.py:163
  58.7 34.6 %copy-start.8 = (bf16[196,2560]{1,0:T(8,128)(2,1)}, bf16[196,2560]{1,0:T(8,128)(2,1)S(1)}, u32[]{:S(2)}) copy-start(bf16[196,2560]{1,0:T(8,128)(2,1)S(1)} %collective-permute-done.3.refs_7_) | copy-start | bytes 3010564
  63.1 30.2 %copy-start.9 = (bf16[196,2560]{1,0:T(8,128)(2,1)}, bf16[196,2560]{1,0:T(8,128)(2,1)S(1)}, u32[]{:S(2)}) copy-start(bf16[196,2560]{1,0:T(8,128)(2,1)S(1)} %collective-permute-done.2.refs_1_) | copy-start | bytes 3010564
  63.1 3.8 %collective-permute-start.6 = (bf16[196,2560]{1,0:T(8,128)(2,1)}, bf16[196,2560]{1,0:T(8,128)(2,1)S(1)}, u32[]{:S(2)}, u32[]{:S(2)}) collective-permute-start(bf16[196,2560]{1,0:T(8,128)(2,1)} %collective-permute-done.refs_2_), channel_id=1, source_target_pairs={{0,1},{1,0},{2,3},{3,2},{4,5},{5,4},{6,7},{7,6},{8,9},{9,8},{10,11... | collective-permute-start | bytes 3010568 | tf_op jit(solution)/shard_map/ppermute | solution.py:163
  63.1 4.3 %collective-permute-start.7 = (bf16[196,2560]{1,0:T(8,128)(2,1)}, bf16[196,2560]{1,0:T(8,128)(2,1)S(1)}, u32[]{:S(2)}, u32[]{:S(2)}) collective-permute-start(bf16[196,2560]{1,0:T(8,128)(2,1)} %collective-permute-done.1.refs_10_), channel_id=1, source_target_pairs={{0,1},{1,0},{2,3},{3,2},{4,5},{5,4},{6,7},{7,6},{8,9},{9,8},{10,11... | collective-permute-start | bytes 3010568 | tf_op jit(solution)/shard_map/ppermute | solution.py:163
  63.6 25.8 %collective-permute-start.4 = (bf16[196,2560]{1,0:T(8,128)(2,1)S(1)}, bf16[196,2560]{1,0:T(8,128)(2,1)S(1)}, u32[]{:S(2)}, u32[]{:S(2)}) collective-permute-start(bf16[196,2560]{1,0:T(8,128)(2,1)S(1)} %pad_maximum_fusion.refs_6_), channel_id=1, source_target_pairs={{0,2},{1,3},{2,4},{3,5},{4,6},{5,7},{6,0},{7,1},{8,10},{9,11},{10,... | collective-permute-start | bytes 3010568 | tf_op jit(solution)/shard_map/ppermute | solution.py:159
  63.6 25.8 %collective-permute-start.5 = (bf16[196,2560]{1,0:T(8,128)(2,1)S(1)}, bf16[196,2560]{1,0:T(8,128)(2,1)S(1)}, u32[]{:S(2)}, u32[]{:S(2)}) collective-permute-start(bf16[196,2560]{1,0:T(8,128)(2,1)S(1)} %slice.24.refs_0_), channel_id=1, source_target_pairs={{0,6},{1,7},{2,0},{3,1},{4,2},{5,3},{6,4},{7,5},{8,14},{9,15},{10,... | collective-permute-start | bytes 3010568 | tf_op jit(solution)/shard_map/ppermute | solution.py:159
  89.5 3.8 %collective-permute-start.10 = (bf16[196,2560]{1,0:T(8,128)(2,1)S(1)}, bf16[196,2560]{1,0:T(8,128)(2,1)S(1)}, u32[]{:S(2)}, u32[]{:S(2)}) collective-permute-start(bf16[196,2560]{1,0:T(8,128)(2,1)S(1)} %collective-permute-done.5.refs_4_), channel_id=1, source_target_pairs={{0,1},{1,0},{2,3},{3,2},{4,5},{5,4},{6,7},{7,6},{8,9},{9,8},{10,11... | collective-permute-start | bytes 3010568 | tf_op jit(solution)/shard_map/ppermute | solution.py:163
  89.6 4.8 %collective-permute-start.11 = (bf16[196,2560]{1,0:T(8,128)(2,1)S(1)}, bf16[196,2560]{1,0:T(8,128)(2,1)}, u32[]{:S(2)}, u32[]{:S(2)}) collective-permute-start(bf16[196,2560]{1,0:T(8,128)(2,1)S(1)} %collective-permute-done.4.refs_8_), channel_id=1, source_target_pairs={{0,1},{1,0},{2,3},{3,2},{4,5},{5,4},{6,7},{7,6},{8,9},{9,8},{10,11... | collective-permute-start | bytes 3010568 | tf_op jit(solution)/shard_map/ppermute | solution.py:163
  90.1 26.1 %collective-permute-start.8 = (bf16[196,2560]{1,0:T(8,128)(2,1)}, bf16[196,2560]{1,0:T(8,128)(2,1)S(1)}, u32[]{:S(2)}, u32[]{:S(2)}) collective-permute-start(bf16[196,2560]{1,0:T(8,128)(2,1)} %collective-permute-done.refs_2_), channel_id=1, source_target_pairs={{0,2},{1,3},{2,4},{3,5},{4,6},{5,7},{6,0},{7,1},{8,10},{9,11},{10,... | collective-permute-start | bytes 3010568 | tf_op jit(solution)/shard_map/ppermute | solution.py:159
  90.1 26.0 %collective-permute-start.9 = (bf16[196,2560]{1,0:T(8,128)(2,1)}, bf16[196,2560]{1,0:T(8,128)(2,1)S(1)}, u32[]{:S(2)}, u32[]{:S(2)}) collective-permute-start(bf16[196,2560]{1,0:T(8,128)(2,1)} %collective-permute-done.1.refs_10_), channel_id=1, source_target_pairs={{0,6},{1,7},{2,0},{3,1},{4,2},{5,3},{6,4},{7,5},{8,14},{9,15},{10,... | collective-permute-start | bytes 3010568 | tf_op jit(solution)/shard_map/ppermute | solution.py:159
  116.1 2.9 %collective-permute-start.16 = (bf16[196,2560]{1,0:T(8,128)(2,1)S(1)}, bf16[196,2560]{1,0:T(8,128)(2,1)S(1)}, u32[]{:S(2)}, u32[]{:S(2)}) collective-permute-start(bf16[196,2560]{1,0:T(8,128)(2,1)S(1)} %collective-permute-done.8.refs_0_), channel_id=1, source_target_pairs={{0,1},{1,0},{2,3},{3,2},{4,5},{5,4},{6,7},{7,6},{8,9},{9,8},{10,11... | collective-permute-start | bytes 3010568 | tf_op jit(solution)/shard_map/ppermute | solution.py:163
  116.1 4.1 %collective-permute-start.17 = (bf16[196,2560]{1,0:T(8,128)(2,1)S(1)}, bf16[196,2560]{1,0:T(8,128)(2,1)S(1)}, u32[]{:S(2)}, u32[]{:S(2)}) collective-permute-start(bf16[196,2560]{1,0:T(8,128)(2,1)S(1)} %collective-permute-done.9.refs_1_), channel_id=1, source_target_pairs={{0,1},{1,0},{2,3},{3,2},{4,5},{5,4},{6,7},{7,6},{8,9},{9,8},{10,11... | collective-permute-start | bytes 3010568 | tf_op jit(solution)/shard_map/ppermute | solution.py:163
  (11 other events, 99.7 us)
Sparse Core Ops, SparseCore 0:
  33.3 59.9 all-gather.1

commit v5 on v4

--- a/solution.py
+++ b/solution.py
@@ -112,46 +112,44 @@
     )(*lows, *highs, basis, *before)
 
 
-def place(blk, ring, me, counts, slots, kept, given, held, hot, sem):
-    depth, cap = held.shape
+def place(blk, ring, me, counts, slots, *refs):
+    *hops, hot = refs
+    cap = slots.shape[1]
     owners = CHIPS * CORES
     stripe, per = blk * owners, ring // owners
-    img, own = me[0], me[1]
+    own = me[0]
     z, c = own // CORES, own % CORES
-    copy = pltpu.make_async_copy(slots.at[pl.ds(pl.multiple_of(img * depth, 16), depth)], held, sem)
-    copy.start()
     start = jnp.int32(0)
     for o in range(owners):
         start += jnp.where(o < own, counts[o], 0)
     slot = lax.broadcasted_iota(I32, (1, cap), 1)
     spot = lax.rem(start + slot, jnp.int32(ring))
     goal = lax.div(lax.rem(spot, jnp.int32(stripe)), jnp.int32(blk))
-    hop = ((goal // CORES - z + CHIPS) & (CHIPS - 1)) + CHIPS * ((goal & 1) ^ c)
+    hop = ((goal // CORES - z + CHIPS) & (CHIPS - 1)) * CORES + ((goal & 1) ^ c)
     row = hop * per + lax.div(spot, jnp.int32(stripe)) * blk + lax.rem(spot, jnp.int32(blk))
     row = jnp.where(slot < counts[own], row, -1)
     for r in range(0, ring, per):
         here = lax.broadcasted_iota(I32, (per, cap), 0) + r == row
         hot[r : r + per] = here.astype(F32).astype(BF16)
-    copy.wait()
-    laid = lax.dot_general(hot[...], held[...], (((1,), (1,)), ((), ())), preferred_element_type=F32).astype(BF16)
+    laid = lax.dot_general(hot[...], slots[...], (((1,), (1,)), ((), ())), preferred_element_type=F32).astype(BF16)
     for r in range(0, ring, per):
-        out = kept if r < ring // CORES else given
-        out[r % (ring // CORES) // per] = laid[r : r + per]
+        hops[r // per // CORES][r // per % CORES] = laid[r : r + per]
 
 
 def placed(basis_slots, col_counts, img, own, groups, blk, ring):
     kin, cap = basis_slots.shape
     depth = kin // groups
-    scalars = pl.BlockSpec(memory_space=pltpu.SMEM)
+    piece = lax.dynamic_slice(basis_slots, (img * depth, jnp.int32(0)), (depth, cap))
+    scalars, inside = pl.BlockSpec(memory_space=pltpu.SMEM), pl.BlockSpec(memory_space=pltpu.VMEM)
     return pl.pallas_call(
         functools.partial(place, blk, ring),
-        out_shape=[jax.ShapeDtypeStruct((CHIPS, ring // CHIPS // CORES, depth), BF16)] * CORES,
-        in_specs=[scalars, scalars, pl.BlockSpec(memory_space=pltpu.HBM)],
-        out_specs=[pl.BlockSpec(memory_space=pltpu.VMEM)] * CORES,
-        scratch_shapes=[pltpu.VMEM((depth, cap), BF16), pltpu.VMEM((ring, cap), BF16), pltpu.SemaphoreType.DMA],
-        compiler_params=pltpu.CompilerParams(vmem_limit_bytes=55 << 20),
+        out_shape=[jax.ShapeDtypeStruct((CORES, ring // CHIPS // CORES, depth), BF16)] * CHIPS,
+        in_specs=[scalars, scalars, inside],
+        out_specs=[inside] * CHIPS,
+        scratch_shapes=[pltpu.VMEM((ring, cap), BF16)],
+        compiler_params=pltpu.CompilerParams(vmem_limit_bytes=28 << 20),
         cost_estimate=pl.CostEstimate(flops=2 * ring * cap * depth, bytes_accessed=4 * depth * cap, transcendentals=0),
-    )(jnp.stack([img, own]).astype(I32), col_counts, basis_slots)
+    )(own.astype(I32).reshape(1), col_counts, piece)
 
 
 def up(a, step):
@@ -163,7 +161,7 @@
     return lax.ppermute(a, "own", [(o, o ^ 1) for o in range(CHIPS * CORES)])
 
 
-def balanced_basis(basis_slots, col_counts, img, own, groups, blk, wide):
+def balanced_basis(basis_slots, col_counts, img, own, groups, blk, wide, first):
     owners = CHIPS * CORES
     kin, cap = basis_slots.shape
     stripe = blk * owners
@@ -172,11 +170,13 @@
     depth = kin // groups
     starts = jnp.cumsum(col_counts) - col_counts
     z, c = own // CORES, own % CORES
-    kept, given = placed(basis_slots, col_counts, img, own, groups, blk, ring)
-    both = jnp.stack([kept, swap(given)], axis=1)
-    incoming = jnp.stack([both[0], up(both[1], 1), up(both[2], 2), up(both[3], -1)])
-    source = ((z - jnp.arange(CHIPS, dtype=I32)) % CHIPS * CORES)[:, None] + (jnp.arange(CORES, dtype=I32) ^ c)[None, :]
-    source = source.reshape(owners)
+    hops = placed(basis_slots, col_counts, img, own, groups, blk, ring)
+    hops = [hops[0], up(hops[1], 1), up(hops[2], 2), up(hops[3], -1)]
+    hops, first = lax.optimization_barrier((hops, first))
+    given = swap(jnp.stack([hop[1] for hop in hops]))
+    incoming = jnp.concatenate([jnp.stack([hop[0] for hop in hops]), given])
+    source = (z - jnp.arange(CHIPS, dtype=I32)) % CHIPS * CORES
+    source = jnp.concatenate([source + c, source + (c ^ 1)])
     begin, count = starts[source], col_counts[source]
     spot = jnp.arange(per, dtype=I32)
     at = spot // blk * stripe + own * blk + spot % blk
@@ -187,7 +187,7 @@
     mine = lax.dot_general(
         incoming.reshape(ring, depth), keep.astype(BF16), (((0,), (0,)), ((), ())), preferred_element_type=F32
     )
-    return lax.all_gather(mine.astype(BF16), "img", axis=0, tiled=True)
+    return lax.all_gather(mine.astype(BF16), "img", axis=0, tiled=True), first
 
 
 def gathered(low, high):
@@ -214,9 +214,9 @@
     proj = jnp.dot(grads, basis_g, preferred_element_type=F32).astype(BF16)
     half = (kin + gout) // 2
     low, high = patches[:, :half], jnp.concatenate([patches[:, half:], proj], axis=1)
+    wide = -(-(blk + 1) // 8) * 8
+    basis, (low, high) = balanced_basis(basis_slots, col_counts, img, own, groups, blk, wide, (low, high))
     near, far = gathered(low, high)
-    wide = -(-(blk + 1) // 8) * 8
-    basis = balanced_basis(basis_slots, col_counts, img, own, groups, blk, wide)
     sums = added("near", near, basis)
     far, sums = lax.optimization_barrier((far, sums))
     partner = swap(far[0]), swap(far[1])

time: 151 us -> 149 us (0.987)
  local copies, waits for them, and re-layouts: 3.8 us -> 9.64 us
  waiting for transfers between devices: 60.3 us -> 55.4 us
  matrix products: 1.9 us -> 4.02 us
  Pallas kernels: 30 us -> 27.9 us
  other arithmetic: 3.47 us -> 1.5 us
    ppermute x9, waiting for transfers between devices: 58.5 us -> 49.8 us  [up(): return lax.ppermute(a, 'own', pairs)]
    all_gather x1, waiting for transfers between devices: 0.01 us -> 2.69 us  [balanced_basis(): return (lax.all_gather(mine.astype(BF16), 'img', axis=0, tiled=True), first)]
    pallas_call x1, Pallas kernels: 4.39 us -> 2.28 us  [placed(): pl.pallas_call(functools.partial(place, blk, ring), out_shape=[jax.ShapeD...]
    slice x0 -> x4, local copies, waits for them, and re-layouts: none -> 2.02 us  [balanced_basis(): given = swap(jnp.stack([hop[1] for hop in hops]))]
    unnamed x31 -> x33, local copies, waits for them, and re-layouts: 1.13 us -> 2.77 us
  transfers between devices with their start and end apart: 19 -> 19, of which waited for: 8 -> 6; matrix products, arithmetic and copies ran while one was open for 2% -> 3% of each run, Pallas kernels for 15% -> 15%
where the time goes in v5:
time: 149 us
  waiting for transfers between devices  55.4 us (37%)
  Pallas kernels  27.9 us (19%)
  blocking collectives  18.6 us (12%)
  starting transfers between devices  18.4 us (12%)
  between operations  13.7 us (9%)
  local copies, waits for them, and re-layouts  9.64 us (6%)
  matrix products  4.02 us (3%)
  other arithmetic  1.5 us (1%)
    ppermute x9, waiting for transfers between devices, up(): return lax.ppermute(a, 'own', pairs)  49.8 us
    pallas_call x3, Pallas kernels, added(): pl.pallas_call(functools.partial(accumulate, n, cols // 2, mode, block),...  25.7 us
    all_to_all x1, blocking collectives, shards(): lax.all_to_all(total.astype(jnp.float16).reshape(groups, wide, gout), 'im...  18.6 us
    ppermute x9, starting transfers between devices, up(): return lax.ppermute(a, 'own', pairs)  16.5 us
  transfers between devices with their start and end apart: 19, of which 6 were waited for; matrix products, arithmetic and copies ran while one was open for 3% of the time, Pallas kernels for 15%

profile of v5, /device:TPU:0, one launch (start us, length us, event | category | flops | bytes accessed | tf_op | source)
XLA Modules:
  0.0 149.1 jit_solution(16088463133761879410)
XLA Ops:
  6.5 1.2 constant_dynamic-slice_fusion.slots
  8.4 2.3 %shard_map.55 = (bf16[2,144,288]{2,1,0:T(8,128)(2,1)S(1)}, bf16[2,144,288]{2,1,0:T(8,128)(2,1)S(1)}, bf16[2,144,288]{2,1,0:T(8,128)(2,1)S(1)}, bf16[2,144,288]{2,1,0:T(8,128)(2,1)S(1)}) custom-call(s32[1]{0:T(128)} %bitcast.me, s32[8]{0:T(128)S(1)} %copy-done.1, bf16[288,1152]{1,0:T(8,128)(2,1)S(1)} %constant_dynamic-slice_fusion.slots), custom_call_target="tpu_custom_call" | custom-call | flops 764411904 | bytes 1327104 | tf_op jit(solution)/shard_map/pallas_call | solution.py:144
  10.7 2.1 %collective-permute-start = (bf16[2,144,288]{2,1,0:T(8,128)(2,1)S(1)}, bf16[2,144,288]{2,1,0:T(8,128)(2,1)}, u32[]{:S(2)}, u32[]{:S(2)}) collective-permute-start(bf16[2,144,288]{2,1,0:T(8,128)(2,1)S(1)} %get-tuple-element.33), channel_id=1, source_target_pairs={{0,2},{1,3},{2,4},{3,5},{4,6},{5,7},{6,0},{7,1},{8,10},{9,11},{10,... | collective-permute-start | bytes 497672 | tf_op jit(solution)/shard_map/ppermute | solution.py:157
  12.8 3.6 %collective-permute-start.1 = (bf16[2,144,288]{2,1,0:T(8,128)(2,1)S(1)}, bf16[2,144,288]{2,1,0:T(8,128)(2,1)}, u32[]{:S(2)}, u32[]{:S(2)}) collective-permute-start(bf16[2,144,288]{2,1,0:T(8,128)(2,1)S(1)} %get-tuple-element.34), channel_id=1, source_target_pairs={{0,4},{1,5},{2,6},{3,7},{4,0},{5,1},{6,2},{7,3},{8,12},{9,13},{10,... | collective-permute-start | bytes 497672 | tf_op jit(solution)/shard_map/ppermute | solution.py:157
  16.4 1.0 collective-permute-start.2
  17.4 1.1 slice.36.refs_0_
  19.4 1.2 convolution_convert_fusion
  21.7 4.6 %collective-permute-done.1 = bf16[2,144,288]{2,1,0:T(8,128)(2,1)} collective-permute-done((bf16[2,144,288]{2,1,0:T(8,128)(2,1)S(1)}, bf16[2,144,288]{2,1,0:T(8,128)(2,1)}, u32[]{:S(2)}, u32[]{:S(2)}) %collective-permute-start.1) | collective-permute-done | bytes 165920 | tf_op jit(solution)/shard_map/ppermute | solution.py:157
  28.4 1.0 copy-done.8
  29.8 1.6 %collective-permute-done.15 = bf16[4,144,288]{2,1,0:T(8,128)(2,1)S(1)} collective-permute-done((bf16[4,144,288]{2,1,0:T(8,128)(2,1)S(1)}, bf16[4,144,288]{2,1,0:T(8,128)(2,1)S(1)}, u32[]{:S(2)}, u32[]{:S(2)}) %collective-permute-start.15) | collective-permute-done | bytes 331808 | tf_op jit(solution)/shard_map/ppermute | solution.py:161
  32.2 2.8 %fusion.2 = bf16[288,640]{1,0:T(8,128)(2,1)} fusion(bf16[1152,288]{1,0:T(8,128)(2,1)} %bitcast.19, s32[1152]{0:T(1024)S(1)} %fusion.5), kind=kOutput, calls=%fused_computation.6 | convolution fusion | flops 425594880 | bytes 1036800 | tf_op jit(solution)/shard_map/dot_general | solution.py:187
  35.1 1.2 collective-permute-start.3
  36.3 2.1 %collective-permute-start.4 = (bf16[196,2560]{1,0:T(8,128)(2,1)S(1)}, bf16[196,2560]{1,0:T(8,128)(2,1)}, u32[]{:S(2)}, u32[]{:S(2)}) collective-permute-start(bf16[196,2560]{1,0:T(8,128)(2,1)S(1)} %pad_maximum_fusion.refs_6_), channel_id=1, source_target_pairs={{0,6},{1,7},{2,0},{3,1},{4,2},{5,3},{6,4},{7,5},{8,14},{9,15},{10,... | collective-permute-start | bytes 3010568 | tf_op jit(solution)/shard_map/ppermute | solution.py:157
  38.9 22.2 %collective-permute-done.3.refs_2_ = bf16[196,2560]{1,0:T(8,128)(2,1)} collective-permute-done((bf16[196,2560]{1,0:T(8,128)(2,1)S(1)}, bf16[196,2560]{1,0:T(8,128)(2,1)}, u32[]{:S(2)}, u32[]{:S(2)}) %collective-permute-start.3) | collective-permute-done | bytes 1003552 | tf_op jit(solution)/shard_map/ppermute | solution.py:157
  61.9 2.7 %collective-permute-start.8 = (bf16[196,2560]{1,0:T(8,128)(2,1)S(1)}, bf16[196,2560]{1,0:T(8,128)(2,1)S(1)}, u32[]{:S(2)}, u32[]{:S(2)}) collective-permute-start(bf16[196,2560]{1,0:T(8,128)(2,1)S(1)} %copy-done.6), channel_id=1, source_target_pairs={{0,6},{1,7},{2,0},{3,1},{4,2},{5,3},{6,4},{7,5},{8,14},{9,15},{10,... | collective-permute-start | bytes 3010568 | tf_op jit(solution)/shard_map/ppermute | solution.py:157
  64.6 22.9 %collective-permute-done.7.refs_8_ = bf16[196,2560]{1,0:T(8,128)(2,1)S(1)} collective-permute-done((bf16[196,2560]{1,0:T(8,128)(2,1)S(1)}, bf16[196,2560]{1,0:T(8,128)(2,1)S(1)}, u32[]{:S(2)}, u32[]{:S(2)}) %collective-permute-start.7) | collective-permute-done | bytes 1003552 | tf_op jit(solution)/shard_map/ppermute | solution.py:157
  88.1 1.1 collective-permute-start.11
  89.2 2.1 %collective-permute-start.12 = (bf16[196,2560]{1,0:T(8,128)(2,1)}, bf16[196,2560]{1,0:T(8,128)(2,1)S(1)}, u32[]{:S(2)}, u32[]{:S(2)}) collective-permute-start(bf16[196,2560]{1,0:T(8,128)(2,1)} %collective-permute-done.4.refs_10_), channel_id=1, source_target_pairs={{0,6},{1,7},{2,0},{3,1},{4,2},{5,3},{6,4},{7,5},{8,14},{9,15},{10,... | collective-permute-start | bytes 3010568 | tf_op jit(solution)/shard_map/ppermute | solution.py:157
  92.4 2.7 %all-gather.2.cloned.1.call-done.refs_12_.refs_2_ = bf16[4608,640]{1,0:T(8,128)(2,1)} async-done(((bf16[288,640]{1,0:T(8,128)(2,1)}), bf16[4608,640]{1,0:T(8,128)(2,1)}) %all-gather.2.cloned.1.call-update) | async-done | bytes 5898256 | tf_op jit(solution)/shard_map/all_gather | solution.py:190
  95.1 20.5 %shard_map.56.refs_4_ = f32[640,512]{1,0:T(8,128)} custom-call(bf16[196,2560]{1,0:T(8,128)(2,1)} %slice.36.refs_0_, bf16[196,2560]{1,0:T(8,128)(2,1)} %copy-done.9, bf16[196,2560]{1,0:T(8,128)(2,1)} %collective-permute-done.3.refs_2_, bf16[196,2560]{1,0:T(8,128)(2,1)} %copy-done.14, bf16[196,2560]{1,0:T(8,128)(2,1)} %copy-done.13, ...), custom_call_target="tpu_custom_call" | custom-call | flops 6936330240 | bytes 17940480 | tf_op jit(solution)/shard_map/pallas_call | solution.py:102
  116.2 2.4 %shard_map.57.refs_3_ = f32[640,512]{1,0:T(8,128)S(1)} custom-call(bf16[196,2560]{1,0:T(8,128)(2,1)S(1)} %collective-permute-done.11.refs_0_, bf16[196,2560]{1,0:T(8,128)(2,1)S(1)} %collective-permute-done.12.refs_1_, bf16[4608,640]{1,0:T(8,128)(2,1)S(1)} %copy-done.3), custom_call_target="tpu_custom_call" | custom-call | flops 1156055040 | bytes 7905280 | tf_op jit(solution)/shard_map/pallas_call | solution.py:102
  118.6 1.2 collective-permute-done.17.refs_1_
  119.8 2.8 %shard_map.58 = f32[640,512]{1,0:T(8,128)S(1)} custom-call(bf16[196,2560]{1,0:T(8,128)(2,1)S(1)} %collective-permute-done.16.refs_0_, bf16[196,2560]{1,0:T(8,128)(2,1)S(1)} %collective-permute-done.17.refs_1_, bf16[4608,640]{1,0:T(8,128)(2,1)S(1)} %copy-done.3, f32[640,512]{1,0:T(8,128)S(1)} %shard_map.57.refs_3_, f32[640,512]{1,0:T(8,128)S(1)} %copy-done.4), custom_call_target="tpu_custom_call" | custom-call | flops 1156055040 | bytes 7905280 | tf_op jit(solution)/shard_map/pallas_call | solution.py:102
  122.7 18.6 %all_to_all.5 = f16[16,40,512]{2,1,0:T(8,128)(2,1)S(1)} all-to-all(f16[16,40,512]{2,1,0:T(8,128)(2,1)S(1)} %bitcast.18), channel_id=1, replica_groups=mesh['img'=16,'own'=8] {'img'}, dimensions={0} | all-to-all | bytes 1310720 | tf_op jit(solution)/shard_map/all_to_all | solution.py:225
  (86 shorter events, 10.4 us)
Async XLA Ops:
  6.5 88.5 %all-gather.2.cloned.1.call-start = ((), (), s32[]{:S(2)}) async-start(), calls=%async_computation.1 | async-start | bytes 6266880 | tf_op jit(solution)/shard_map/all_gather | solution.py:190
  10.7 11.0 %collective-permute-start = (bf16[2,144,288]{2,1,0:T(8,128)(2,1)S(1)}, bf16[2,144,288]{2,1,0:T(8,128)(2,1)}, u32[]{:S(2)}, u32[]{:S(2)}) collective-permute-start(bf16[2,144,288]{2,1,0:T(8,128)(2,1)S(1)} %get-tuple-element.33), channel_id=1, source_target_pairs={{0,2},{1,3},{2,4},{3,5},{4,6},{5,7},{6,0},{7,1},{8,10},{9,11},{10,... | collective-permute-start | bytes 497672 | tf_op jit(solution)/shard_map/ppermute | solution.py:157
  12.8 13.6 %collective-permute-start.1 = (bf16[2,144,288]{2,1,0:T(8,128)(2,1)S(1)}, bf16[2,144,288]{2,1,0:T(8,128)(2,1)}, u32[]{:S(2)}, u32[]{:S(2)}) collective-permute-start(bf16[2,144,288]{2,1,0:T(8,128)(2,1)S(1)} %get-tuple-element.34), channel_id=1, source_target_pairs={{0,4},{1,5},{2,6},{3,7},{4,0},{5,1},{6,2},{7,3},{8,12},{9,13},{10,... | collective-permute-start | bytes 497672 | tf_op jit(solution)/shard_map/ppermute | solution.py:157
  16.4 10.0 %collective-permute-start.2 = (bf16[2,144,288]{2,1,0:T(8,128)(2,1)S(1)}, bf16[2,144,288]{2,1,0:T(8,128)(2,1)S(1)}, u32[]{:S(2)}, u32[]{:S(2)}) collective-permute-start(bf16[2,144,288]{2,1,0:T(8,128)(2,1)S(1)} %get-tuple-element.35), channel_id=1, source_target_pairs={{0,6},{1,7},{2,0},{3,1},{4,2},{5,3},{6,4},{7,5},{8,14},{9,15},{10,... | collective-permute-start | bytes 497672 | tf_op jit(solution)/shard_map/ppermute | solution.py:157
  20.7 40.5 %copy-start.7 = (bf16[196,2560]{1,0:T(8,128)(2,1)}, bf16[196,2560]{1,0:T(8,128)(2,1)S(1)}, u32[]{:S(2)}) copy-start(bf16[196,2560]{1,0:T(8,128)(2,1)S(1)} %pad_maximum_fusion.refs_6_) | copy-start | bytes 3010564
  29.5 1.9 %collective-permute-start.15 = (bf16[4,144,288]{2,1,0:T(8,128)(2,1)S(1)}, bf16[4,144,288]{2,1,0:T(8,128)(2,1)S(1)}, u32[]{:S(2)}, u32[]{:S(2)}) collective-permute-start(bf16[4,144,288]{2,1,0:T(8,128)(2,1)S(1)} %pad_maximum_fusion.1), channel_id=1, source_target_pairs={{0,1},{1,0},{2,3},{3,2},{4,5},{5,4},{6,7},{7,6},{8,9},{9,8},{10,11... | collective-permute-start | bytes 995336 | tf_op jit(solution)/shard_map/ppermute | solution.py:161
  35.1 26.1 %collective-permute-start.3 = (bf16[196,2560]{1,0:T(8,128)(2,1)S(1)}, bf16[196,2560]{1,0:T(8,128)(2,1)}, u32[]{:S(2)}, u32[]{:S(2)}) collective-permute-start(bf16[196,2560]{1,0:T(8,128)(2,1)S(1)} %copy-done.6), channel_id=1, source_target_pairs={{0,2},{1,3},{2,4},{3,5},{4,6},{5,7},{6,0},{7,1},{8,10},{9,11},{10,... | collective-permute-start | bytes 3010568 | tf_op jit(solution)/shard_map/ppermute | solution.py:157
  36.3 24.9 %collective-permute-start.4 = (bf16[196,2560]{1,0:T(8,128)(2,1)S(1)}, bf16[196,2560]{1,0:T(8,128)(2,1)}, u32[]{:S(2)}, u32[]{:S(2)}) collective-permute-start(bf16[196,2560]{1,0:T(8,128)(2,1)S(1)} %pad_maximum_fusion.refs_6_), channel_id=1, source_target_pairs={{0,6},{1,7},{2,0},{3,1},{4,2},{5,3},{6,4},{7,5},{8,14},{9,15},{10,... | collective-permute-start | bytes 3010568 | tf_op jit(solution)/shard_map/ppermute | solution.py:157
  38.4 22.8 %collective-permute-start.5 = (bf16[196,2560]{1,0:T(8,128)(2,1)S(1)}, bf16[196,2560]{1,0:T(8,128)(2,1)S(1)}, u32[]{:S(2)}, u32[]{:S(2)}) collective-permute-start(bf16[196,2560]{1,0:T(8,128)(2,1)S(1)} %copy-done.6), channel_id=1, source_target_pairs={{0,1},{1,0},{2,3},{3,2},{4,5},{5,4},{6,7},{7,6},{8,9},{9,8},{10,11... | collective-permute-start | bytes 3010568 | tf_op jit(solution)/shard_map/ppermute | solution.py:161
  38.4 22.8 %collective-permute-start.6 = (bf16[196,2560]{1,0:T(8,128)(2,1)S(1)}, bf16[196,2560]{1,0:T(8,128)(2,1)S(1)}, u32[]{:S(2)}, u32[]{:S(2)}) collective-permute-start(bf16[196,2560]{1,0:T(8,128)(2,1)S(1)} %pad_maximum_fusion.refs_6_), channel_id=1, source_target_pairs={{0,1},{1,0},{2,3},{3,2},{4,5},{5,4},{6,7},{7,6},{8,9},{9,8},{10,11... | collective-permute-start | bytes 3010568 | tf_op jit(solution)/shard_map/ppermute | solution.py:161
  61.1 27.0 %copy-start.9 = (bf16[196,2560]{1,0:T(8,128)(2,1)}, bf16[196,2560]{1,0:T(8,128)(2,1)S(1)}, u32[]{:S(2)}) copy-start(bf16[196,2560]{1,0:T(8,128)(2,1)S(1)} %collective-permute-done.5.refs_1_) | copy-start | bytes 3010564
  61.1 28.1 %copy-start.10 = (bf16[196,2560]{1,0:T(8,128)(2,1)}, bf16[196,2560]{1,0:T(8,128)(2,1)S(1)}, u32[]{:S(2)}) copy-start(bf16[196,2560]{1,0:T(8,128)(2,1)S(1)} %collective-permute-done.6.refs_7_) | copy-start | bytes 3010564
  61.2 3.4 %collective-permute-start.10 = (bf16[196,2560]{1,0:T(8,128)(2,1)}, bf16[196,2560]{1,0:T(8,128)(2,1)S(1)}, u32[]{:S(2)}, u32[]{:S(2)}) collective-permute-start(bf16[196,2560]{1,0:T(8,128)(2,1)} %collective-permute-done.4.refs_10_), channel_id=1, source_target_pairs={{0,1},{1,0},{2,3},{3,2},{4,5},{5,4},{6,7},{7,6},{8,9},{9,8},{10,11... | collective-permute-start | bytes 3010568 | tf_op jit(solution)/shard_map/ppermute | solution.py:161
  61.3 26.3 %collective-permute-start.7 = (bf16[196,2560]{1,0:T(8,128)(2,1)S(1)}, bf16[196,2560]{1,0:T(8,128)(2,1)S(1)}, u32[]{:S(2)}, u32[]{:S(2)}) collective-permute-start(bf16[196,2560]{1,0:T(8,128)(2,1)S(1)} %pad_maximum_fusion.refs_6_), channel_id=1, source_target_pairs={{0,2},{1,3},{2,4},{3,5},{4,6},{5,7},{6,0},{7,1},{8,10},{9,11},{10,... | collective-permute-start | bytes 3010568 | tf_op jit(solution)/shard_map/ppermute | solution.py:157
  61.9 25.6 %collective-permute-start.8 = (bf16[196,2560]{1,0:T(8,128)(2,1)S(1)}, bf16[196,2560]{1,0:T(8,128)(2,1)S(1)}, u32[]{:S(2)}, u32[]{:S(2)}) collective-permute-start(bf16[196,2560]{1,0:T(8,128)(2,1)S(1)} %copy-done.6), channel_id=1, source_target_pairs={{0,6},{1,7},{2,0},{3,1},{4,2},{5,3},{6,4},{7,5},{8,14},{9,15},{10,... | collective-permute-start | bytes 3010568 | tf_op jit(solution)/shard_map/ppermute | solution.py:157
  64.6 23.0 %collective-permute-start.9 = (bf16[196,2560]{1,0:T(8,128)(2,1)}, bf16[196,2560]{1,0:T(8,128)(2,1)S(1)}, u32[]{:S(2)}, u32[]{:S(2)}) collective-permute-start(bf16[196,2560]{1,0:T(8,128)(2,1)} %collective-permute-done.3.refs_2_), channel_id=1, source_target_pairs={{0,1},{1,0},{2,3},{3,2},{4,5},{5,4},{6,7},{7,6},{8,9},{9,8},{10,11... | collective-permute-start | bytes 3010568 | tf_op jit(solution)/shard_map/ppermute | solution.py:161
  64.6 26.8 %copy-start.11 = (bf16[196,2560]{1,0:T(8,128)(2,1)}, bf16[196,2560]{1,0:T(8,128)(2,1)S(1)}, u32[]{:S(2)}) copy-start(bf16[196,2560]{1,0:T(8,128)(2,1)S(1)} %collective-permute-done.10.refs_11_) | copy-start | bytes 3010564
  87.5 3.8 %collective-permute-start.13 = (bf16[196,2560]{1,0:T(8,128)(2,1)S(1)}, bf16[196,2560]{1,0:T(8,128)(2,1)S(1)}, u32[]{:S(2)}, u32[]{:S(2)}) collective-permute-start(bf16[196,2560]{1,0:T(8,128)(2,1)S(1)} %collective-permute-done.8.refs_4_), channel_id=1, source_target_pairs={{0,1},{1,0},{2,3},{3,2},{4,5},{5,4},{6,7},{7,6},{8,9},{9,8},{10,11... | collective-permute-start | bytes 3010568 | tf_op jit(solution)/shard_map/ppermute | solution.py:161
  87.6 4.7 %collective-permute-start.14 = (bf16[196,2560]{1,0:T(8,128)(2,1)S(1)}, bf16[196,2560]{1,0:T(8,128)(2,1)}, u32[]{:S(2)}, u32[]{:S(2)}) collective-permute-start(bf16[196,2560]{1,0:T(8,128)(2,1)S(1)} %collective-permute-done.7.refs_8_), channel_id=1, source_target_pairs={{0,1},{1,0},{2,3},{3,2},{4,5},{5,4},{6,7},{7,6},{8,9},{9,8},{10,11... | collective-permute-start | bytes 3010568 | tf_op jit(solution)/shard_map/ppermute | solution.py:161
  88.1 27.5 %collective-permute-start.11 = (bf16[196,2560]{1,0:T(8,128)(2,1)}, bf16[196,2560]{1,0:T(8,128)(2,1)S(1)}, u32[]{:S(2)}, u32[]{:S(2)}) collective-permute-start(bf16[196,2560]{1,0:T(8,128)(2,1)} %collective-permute-done.3.refs_2_), channel_id=1, source_target_pairs={{0,2},{1,3},{2,4},{3,5},{4,6},{5,7},{6,0},{7,1},{8,10},{9,11},{10,... | collective-permute-start | bytes 3010568 | tf_op jit(solution)/shard_map/ppermute | solution.py:157
  89.2 26.4 %collective-permute-start.12 = (bf16[196,2560]{1,0:T(8,128)(2,1)}, bf16[196,2560]{1,0:T(8,128)(2,1)S(1)}, u32[]{:S(2)}, u32[]{:S(2)}) collective-permute-start(bf16[196,2560]{1,0:T(8,128)(2,1)} %collective-permute-done.4.refs_10_), channel_id=1, source_target_pairs={{0,6},{1,7},{2,0},{3,1},{4,2},{5,3},{6,4},{7,5},{8,14},{9,15},{10,... | collective-permute-start | bytes 3010568 | tf_op jit(solution)/shard_map/ppermute | solution.py:157
  95.1 21.2 %copy-start.3 = (bf16[4608,640]{1,0:T(8,128)(2,1)S(1)}, bf16[4608,640]{1,0:T(8,128)(2,1)}, u32[]{:S(2)}) copy-start(bf16[4608,640]{1,0:T(8,128)(2,1)} %all-gather.2.cloned.1.call-done.refs_12_.refs_2_) | copy-start | bytes 17694724
  115.6 3.0 %collective-permute-start.16 = (bf16[196,2560]{1,0:T(8,128)(2,1)S(1)}, bf16[196,2560]{1,0:T(8,128)(2,1)S(1)}, u32[]{:S(2)}, u32[]{:S(2)}) collective-permute-start(bf16[196,2560]{1,0:T(8,128)(2,1)S(1)} %collective-permute-done.11.refs_0_), channel_id=1, source_target_pairs={{0,1},{1,0},{2,3},{3,2},{4,5},{5,4},{6,7},{7,6},{8,9},{9,8},{10,11... | collective-permute-start | bytes 3010568 | tf_op jit(solution)/shard_map/ppermute | solution.py:161
  115.7 4.1 %collective-permute-start.17 = (bf16[196,2560]{1,0:T(8,128)(2,1)S(1)}, bf16[196,2560]{1,0:T(8,128)(2,1)S(1)}, u32[]{:S(2)}, u32[]{:S(2)}) collective-permute-start(bf16[196,2560]{1,0:T(8,128)(2,1)S(1)} %collective-permute-done.12.refs_1_), channel_id=1, source_target_pairs={{0,1},{1,0},{2,3},{3,2},{4,5},{5,4},{6,7},{7,6},{8,9},{9,8},{10,11... | collective-permute-start | bytes 3010568 | tf_op jit(solution)/shard_map/ppermute | solution.py:161
  (12 other events, 54.0 us)
Sparse Core Ops, SparseCore 0:
  35.2 59.8 all-gather.1

commit v6 on v5

--- a/solution.py
+++ b/solution.py
@@ -152,6 +152,47 @@
     )(own.astype(I32).reshape(1), col_counts, piece)
 
 
+def collect(blk, ring, wide, me, counts, *refs):
+    kept, given, out = refs[:CHIPS], refs[CHIPS : 2 * CHIPS], refs[-1]
+    owners = CHIPS * CORES
+    stripe, per = blk * owners, ring // owners
+    own = me[0]
+    z, c = own // CORES, own % CORES
+    spot = lax.broadcasted_iota(I32, (per, 1), 0)
+    at = lax.div(spot, jnp.int32(blk)) * stripe + own * blk + lax.rem(spot, jnp.int32(blk))
+    column = lax.broadcasted_iota(I32, (per, out.shape[1]), 1)
+    total = jnp.zeros(out.shape, F32)
+    for hop in range(CHIPS):
+        for other in range(CORES):
+            source = ((z - hop + CHIPS) & (CHIPS - 1)) * CORES + (c ^ other)
+            begin = jnp.int32(0)
+            for o in range(owners):
+                begin += jnp.where(o < source, counts[o], 0)
+            offset = lax.rem(at - begin + owners * ring, jnp.int32(ring))
+            index = begin + offset
+            target = lax.div(index, jnp.int32(stripe)) * wide + lax.rem(index, jnp.int32(blk))
+            target = jnp.where(offset < counts[source], target, -1)
+            keep = (column == target).astype(F32).astype(BF16)
+            piece = given[hop][...] if other else kept[hop][0]
+            total += jnp.dot(piece.T, keep, preferred_element_type=F32)
+    out[...] = total.astype(BF16)
+
+
+def collected(hops, given, col_counts, own, groups, blk, ring, wide):
+    per, depth = given[0].shape
+    scalars, inside = pl.BlockSpec(memory_space=pltpu.SMEM), pl.BlockSpec(memory_space=pltpu.VMEM)
+    return pl.pallas_call(
+        functools.partial(collect, blk, ring, wide),
+        out_shape=jax.ShapeDtypeStruct((depth, groups * wide), BF16),
+        in_specs=[scalars, scalars] + [inside] * (2 * CHIPS),
+        out_specs=inside,
+        compiler_params=pltpu.CompilerParams(vmem_limit_bytes=28 << 20),
+        cost_estimate=pl.CostEstimate(
+            flops=2 * ring * depth * groups * wide, bytes_accessed=4 * depth * groups * wide, transcendentals=0
+        ),
+    )(own.astype(I32).reshape(1), col_counts, *hops, *given)
+
+
 def up(a, step):
     pairs = [(z * CORES + c, (z + step) % CHIPS * CORES + c) for z in range(CHIPS) for c in range(CORES)]
     return lax.ppermute(a, "own", pairs)
@@ -166,28 +207,12 @@
     kin, cap = basis_slots.shape
     stripe = blk * owners
     ring = -(-cap // stripe) * stripe
-    per = ring // owners
-    depth = kin // groups
-    starts = jnp.cumsum(col_counts) - col_counts
-    z, c = own // CORES, own % CORES
     hops = placed(basis_slots, col_counts, img, own, groups, blk, ring)
     hops = [hops[0], up(hops[1], 1), up(hops[2], 2), up(hops[3], -1)]
-    hops, first = lax.optimization_barrier((hops, first))
-    given = swap(jnp.stack([hop[1] for hop in hops]))
-    incoming = jnp.concatenate([jnp.stack([hop[0] for hop in hops]), given])
-    source = (z - jnp.arange(CHIPS, dtype=I32)) % CHIPS * CORES
-    source = jnp.concatenate([source + c, source + (c ^ 1)])
-    begin, count = starts[source], col_counts[source]
-    spot = jnp.arange(per, dtype=I32)
-    at = spot // blk * stripe + own * blk + spot % blk
-    offset = (at[None, :] - begin[:, None]) % ring
-    column = begin[:, None] + offset
-    target = jnp.where(offset < count[:, None], column // stripe * wide + column % blk, -1)
-    keep = target.reshape(ring)[:, None] == jnp.arange(groups * wide, dtype=I32)[None, :]
-    mine = lax.dot_general(
-        incoming.reshape(ring, depth), keep.astype(BF16), (((0,), (0,)), ((), ())), preferred_element_type=F32
-    )
-    return lax.all_gather(mine.astype(BF16), "img", axis=0, tiled=True), first
+    given = [swap(hop[1]) for hop in hops]
+    hops, given, first = lax.optimization_barrier((hops, given, first))
+    mine = collected(hops, given, col_counts, own, groups, blk, ring, wide)
+    return lax.all_gather(mine, "img", axis=0, tiled=True), first
 
 
 def gathered(low, high):

time: 149 us -> 144 us (0.966)
  local copies, waits for them, and re-layouts: 9.64 us -> 3.11 us
  matrix products: 4.02 us -> 0.26 us
  Pallas kernels: 27.9 us -> 30.5 us
  waiting for transfers between devices: 55.4 us -> 57.8 us
    dot_general x1 -> x0, matrix products: 2.83 us -> none  [balanced_basis(): lax.dot_general(incoming.reshape(ring, depth), keep.astype(BF16), (((0,),...]
    ppermute x9, waiting for transfers between devices: 49.8 us -> 52.4 us  [up(): return lax.ppermute(a, 'own', pairs)]
    pallas_call x0 -> x1, Pallas kernels: none -> 2.6 us  [collected(): pl.pallas_call(functools.partial(collect, blk, ring, wide), out_shape=jax...]
    slice x4 -> x0, local copies, waits for them, and re-layouts: 2.02 us -> none  [balanced_basis(): given = swap(jnp.stack([hop[1] for hop in hops]))]
  transfers between devices with their start and end apart: 19 -> 22, of which waited for: 6 -> 8; matrix products, arithmetic and copies ran while one was open for 3% -> 0% of each run, Pallas kernels for 15% -> 16%
where the time goes in v6:
time: 144 us
  waiting for transfers between devices  57.8 us (40%)
  Pallas kernels  30.5 us (21%)
  starting transfers between devices  19.4 us (13%)
  blocking collectives  18.3 us (13%)
  between operations  13.7 us (10%)
  local copies, waits for them, and re-layouts  3.11 us (2%)
    ppermute x9, waiting for transfers between devices, up(): return lax.ppermute(a, 'own', pairs)  52.4 us
    pallas_call x3, Pallas kernels, added(): pl.pallas_call(functools.partial(accumulate, n, cols // 2, mode, block),...  25.7 us
    all_to_all x1, blocking collectives, shards(): lax.all_to_all(total.astype(jnp.float16).reshape(groups, wide, gout), 'im...  18.3 us
    ppermute x9, starting transfers between devices, up(): return lax.ppermute(a, 'own', pairs)  16.4 us
    all_gather x1, waiting for transfers between devices, balanced_basis(): return (lax.all_gather(mine, 'img', axis=0, tiled=True), first)  3.37 us
    ppermute x12, starting transfers between devices, swap(): return lax.ppermute(a, 'own', [(o, o ^ 1) for o in range(CHIPS * CORES)])  2.93 us
  transfers between devices with their start and end apart: 22, of which 8 were waited for; matrix products, arithmetic and copies ran while one was open for 0% of the time, Pallas kernels for 16%

profile of v6, /device:TPU:0, one launch (start us, length us, event | category | flops | bytes accessed | tf_op | source)
XLA Modules:
  0.0 144.2 jit_solution(7553006407616169160)
XLA Ops:
  6.5 1.2 constant_dynamic-slice_fusion.slots
  7.8 0.6 copy-done.3
  8.4 2.3 %shard_map.55 = (bf16[2,144,288]{2,1,0:T(8,128)(2,1)S(1)}, bf16[2,144,288]{2,1,0:T(8,128)(2,1)S(1)}, bf16[2,144,288]{2,1,0:T(8,128)(2,1)S(1)}, bf16[2,144,288]{2,1,0:T(8,128)(2,1)S(1)}) custom-call(s32[1]{0:T(128)} %bitcast.me, s32[8]{0:T(128)S(1)} %copy-done.3, bf16[288,1152]{1,0:T(8,128)(2,1)S(1)} %constant_dynamic-slice_fusion.slots), custom_call_target="tpu_custom_call" | custom-call | flops 764411904 | bytes 1327104 | tf_op jit(solution)/shard_map/pallas_call | solution.py:144
  10.7 2.1 %collective-permute-start = (bf16[2,144,288]{2,1,0:T(8,128)(2,1)S(1)}, bf16[2,144,288]{2,1,0:T(8,128)(2,1)S(1)}, u32[]{:S(2)}, u32[]{:S(2)}) collective-permute-start(bf16[2,144,288]{2,1,0:T(8,128)(2,1)S(1)} %get-tuple-element.37), channel_id=1, source_target_pairs={{0,2},{1,3},{2,4},{3,5},{4,6},{5,7},{6,0},{7,1},{8,10},{9,11},{10,... | collective-permute-start | bytes 497672 | tf_op jit(solution)/shard_map/ppermute | solution.py:198
  12.8 3.6 %collective-permute-start.1 = (bf16[2,144,288]{2,1,0:T(8,128)(2,1)S(1)}, bf16[2,144,288]{2,1,0:T(8,128)(2,1)S(1)}, u32[]{:S(2)}, u32[]{:S(2)}) collective-permute-start(bf16[2,144,288]{2,1,0:T(8,128)(2,1)S(1)} %get-tuple-element.38), channel_id=1, source_target_pairs={{0,4},{1,5},{2,6},{3,7},{4,0},{5,1},{6,2},{7,3},{8,12},{9,13},{10,... | collective-permute-start | bytes 497672 | tf_op jit(solution)/shard_map/ppermute | solution.py:198
  16.4 1.0 collective-permute-start.2
  17.8 2.5 %collective-permute-done.refs_1_ = bf16[2,144,288]{2,1,0:T(8,128)(2,1)S(1)} collective-permute-done((bf16[2,144,288]{2,1,0:T(8,128)(2,1)S(1)}, bf16[2,144,288]{2,1,0:T(8,128)(2,1)S(1)}, u32[]{:S(2)}, u32[]{:S(2)}) %collective-permute-start) | collective-permute-done | bytes 165920 | tf_op jit(solution)/shard_map/ppermute | solution.py:198
  20.4 5.8 %collective-permute-done.1.refs_2_ = bf16[2,144,288]{2,1,0:T(8,128)(2,1)S(1)} collective-permute-done((bf16[2,144,288]{2,1,0:T(8,128)(2,1)S(1)}, bf16[2,144,288]{2,1,0:T(8,128)(2,1)S(1)}, u32[]{:S(2)}, u32[]{:S(2)}) %collective-permute-start.1) | collective-permute-done | bytes 165920 | tf_op jit(solution)/shard_map/ppermute | solution.py:198
  27.9 2.6 %shard_map.56 = bf16[288,640]{1,0:T(8,128)(2,1)} custom-call(s32[1]{0:T(128)} %bitcast.me, s32[8]{0:T(128)S(1)} %copy-done.3, bf16[2,144,288]{2,1,0:T(8,128)(2,1)S(1)} %get-tuple-element.56.refs_0_, bf16[2,144,288]{2,1,0:T(8,128)(2,1)S(1)} %collective-permute-done.refs_1_, bf16[2,144,288]{2,1,0:T(8,128)(2,1)S(1)} %collective-permute-done.1.refs_2_, ...), custom_call_target="tpu_custom_call" | custom-call | flops 424673280 | bytes 737280 | tf_op jit(solution)/shard_map/pallas_call | solution.py:184
  31.0 0.8 collective-permute-start.7
  31.8 2.4 %collective-permute-start.8 = (bf16[196,2560]{1,0:T(8,128)(2,1)S(1)}, bf16[196,2560]{1,0:T(8,128)(2,1)}, u32[]{:S(2)}, u32[]{:S(2)}) collective-permute-start(bf16[196,2560]{1,0:T(8,128)(2,1)S(1)} %pad_maximum_fusion.refs_6_), channel_id=1, source_target_pairs={{0,6},{1,7},{2,0},{3,1},{4,2},{5,3},{6,4},{7,5},{8,14},{9,15},{10,... | collective-permute-start | bytes 3010568 | tf_op jit(solution)/shard_map/ppermute | solution.py:198
  34.2 22.8 %collective-permute-done.7.refs_2_ = bf16[196,2560]{1,0:T(8,128)(2,1)} collective-permute-done((bf16[196,2560]{1,0:T(8,128)(2,1)S(1)}, bf16[196,2560]{1,0:T(8,128)(2,1)}, u32[]{:S(2)}, u32[]{:S(2)}) %collective-permute-start.7) | collective-permute-done | bytes 1003552 | tf_op jit(solution)/shard_map/ppermute | solution.py:198
  57.5 2.8 %collective-permute-start.12 = (bf16[196,2560]{1,0:T(8,128)(2,1)S(1)}, bf16[196,2560]{1,0:T(8,128)(2,1)S(1)}, u32[]{:S(2)}, u32[]{:S(2)}) collective-permute-start(bf16[196,2560]{1,0:T(8,128)(2,1)S(1)} %slice.28.refs_0_), channel_id=1, source_target_pairs={{0,6},{1,7},{2,0},{3,1},{4,2},{5,3},{6,4},{7,5},{8,14},{9,15},{10,... | collective-permute-start | bytes 3010568 | tf_op jit(solution)/shard_map/ppermute | solution.py:198
  60.8 21.3 %collective-permute-done.11.refs_8_ = bf16[196,2560]{1,0:T(8,128)(2,1)S(1)} collective-permute-done((bf16[196,2560]{1,0:T(8,128)(2,1)S(1)}, bf16[196,2560]{1,0:T(8,128)(2,1)S(1)}, u32[]{:S(2)}, u32[]{:S(2)}) %collective-permute-start.11) | collective-permute-done | bytes 1003552 | tf_op jit(solution)/shard_map/ppermute | solution.py:198
  82.8 0.8 collective-permute-start.15
  83.6 2.4 %collective-permute-start.16 = (bf16[196,2560]{1,0:T(8,128)(2,1)}, bf16[196,2560]{1,0:T(8,128)(2,1)S(1)}, u32[]{:S(2)}, u32[]{:S(2)}) collective-permute-start(bf16[196,2560]{1,0:T(8,128)(2,1)} %collective-permute-done.8.refs_10_), channel_id=1, source_target_pairs={{0,6},{1,7},{2,0},{3,1},{4,2},{5,3},{6,4},{7,5},{8,14},{9,15},{10,... | collective-permute-start | bytes 3010568 | tf_op jit(solution)/shard_map/ppermute | solution.py:198
  86.1 1.0 copy-done.14
  87.0 3.4 %all-gather.2.cloned.1.call-done.refs_12_.refs_2_ = bf16[4608,640]{1,0:T(8,128)(2,1)} async-done(((bf16[288,640]{1,0:T(8,128)(2,1)}), bf16[4608,640]{1,0:T(8,128)(2,1)}) %all-gather.2.cloned.1.call-update) | async-done | bytes 5898256 | tf_op jit(solution)/shard_map/all_gather | solution.py:215
  90.4 20.5 %shard_map.57.refs_4_ = f32[640,512]{1,0:T(8,128)} custom-call(bf16[196,2560]{1,0:T(8,128)(2,1)} %copy-done.6, bf16[196,2560]{1,0:T(8,128)(2,1)} %copy-done.9, bf16[196,2560]{1,0:T(8,128)(2,1)} %collective-permute-done.7.refs_2_, bf16[196,2560]{1,0:T(8,128)(2,1)} %copy-done.12, bf16[196,2560]{1,0:T(8,128)(2,1)} %copy-done.11, bf16[196,2560]{1,0:T(8,128)(2,1)} %copy-done.14, ...), custom_call_target="tpu_custom_call" | custom-call | flops 6936330240 | bytes 17940480 | tf_op jit(solution)/shard_map/pallas_call | solution.py:102
  111.5 2.4 %shard_map.58.refs_3_ = f32[640,512]{1,0:T(8,128)S(1)} custom-call(bf16[196,2560]{1,0:T(8,128)(2,1)S(1)} %collective-permute-done.15.refs_0_, bf16[196,2560]{1,0:T(8,128)(2,1)S(1)} %collective-permute-done.16.refs_1_, bf16[4608,640]{1,0:T(8,128)(2,1)S(1)} %copy-done.1), custom_call_target="tpu_custom_call" | custom-call | flops 1156055040 | bytes 7905280 | tf_op jit(solution)/shard_map/pallas_call | solution.py:102
  113.9 1.2 collective-permute-done.20.refs_1_
  115.1 2.8 %shard_map.59 = f32[640,512]{1,0:T(8,128)S(1)} custom-call(bf16[196,2560]{1,0:T(8,128)(2,1)S(1)} %collective-permute-done.19.refs_0_, bf16[196,2560]{1,0:T(8,128)(2,1)S(1)} %collective-permute-done.20.refs_1_, bf16[4608,640]{1,0:T(8,128)(2,1)S(1)} %copy-done.1, f32[640,512]{1,0:T(8,128)S(1)} %shard_map.58.refs_3_, f32[640,512]{1,0:T(8,128)S(1)} %copy-done.2), custom_call_target="tpu_custom_call" | custom-call | flops 1156055040 | bytes 7905280 | tf_op jit(solution)/shard_map/pallas_call | solution.py:102
  118.1 18.3 %all_to_all.5 = f16[16,40,512]{2,1,0:T(8,128)(2,1)S(1)} all-to-all(f16[16,40,512]{2,1,0:T(8,128)(2,1)S(1)} %bitcast.14), channel_id=1, replica_groups=mesh['img'=16,'own'=8] {'img'}, dimensions={0} | all-to-all | bytes 1310720 | tf_op jit(solution)/shard_map/all_to_all | solution.py:250
  136.7 0.6 broadcast_multiply_fusion
  (73 shorter events, 5.2 us)
Async XLA Ops:
  6.5 83.9 %all-gather.2.cloned.1.call-start = ((), (), s32[]{:S(2)}) async-start(), calls=%async_computation.1 | async-start | bytes 6266880 | tf_op jit(solution)/shard_map/all_gather | solution.py:215
  10.7 9.6 %collective-permute-start = (bf16[2,144,288]{2,1,0:T(8,128)(2,1)S(1)}, bf16[2,144,288]{2,1,0:T(8,128)(2,1)S(1)}, u32[]{:S(2)}, u32[]{:S(2)}) collective-permute-start(bf16[2,144,288]{2,1,0:T(8,128)(2,1)S(1)} %get-tuple-element.37), channel_id=1, source_target_pairs={{0,2},{1,3},{2,4},{3,5},{4,6},{5,7},{6,0},{7,1},{8,10},{9,11},{10,... | collective-permute-start | bytes 497672 | tf_op jit(solution)/shard_map/ppermute | solution.py:198
  12.8 13.5 %collective-permute-start.1 = (bf16[2,144,288]{2,1,0:T(8,128)(2,1)S(1)}, bf16[2,144,288]{2,1,0:T(8,128)(2,1)S(1)}, u32[]{:S(2)}, u32[]{:S(2)}) collective-permute-start(bf16[2,144,288]{2,1,0:T(8,128)(2,1)S(1)} %get-tuple-element.38), channel_id=1, source_target_pairs={{0,4},{1,5},{2,6},{3,7},{4,0},{5,1},{6,2},{7,3},{8,12},{9,13},{10,... | collective-permute-start | bytes 497672 | tf_op jit(solution)/shard_map/ppermute | solution.py:198
  16.4 10.0 %collective-permute-start.2 = (bf16[2,144,288]{2,1,0:T(8,128)(2,1)S(1)}, bf16[2,144,288]{2,1,0:T(8,128)(2,1)S(1)}, u32[]{:S(2)}, u32[]{:S(2)}) collective-permute-start(bf16[2,144,288]{2,1,0:T(8,128)(2,1)S(1)} %get-tuple-element.39), channel_id=1, source_target_pairs={{0,6},{1,7},{2,0},{3,1},{4,2},{5,3},{6,4},{7,5},{8,14},{9,15},{10,... | collective-permute-start | bytes 497672 | tf_op jit(solution)/shard_map/ppermute | solution.py:198
  17.4 9.8 %collective-permute-start.3 = (bf16[144,288]{1,0:T(8,128)(2,1)S(1)}, bf16[144,288]{1,0:T(8,128)(2,1)S(1)}, u32[]{:S(2)}, u32[]{:S(2)}) collective-permute-start(bf16[144,288]{1,0:T(8,128)(2,1)S(1)} %slice_bitcast_fusion.3), channel_id=1, source_target_pairs={{0,1},{1,0},{2,3},{3,2},{4,5},{5,4},{6,7},{7,6},{8,9},{9,8},{10,11... | collective-permute-start | bytes 248840 | tf_op jit(solution)/shard_map/ppermute | solution.py:202
  20.3 6.8 %collective-permute-start.4 = (bf16[144,288]{1,0:T(8,128)(2,1)S(1)}, bf16[144,288]{1,0:T(8,128)(2,1)S(1)}, u32[]{:S(2)}, u32[]{:S(2)}) collective-permute-start(bf16[144,288]{1,0:T(8,128)(2,1)S(1)} %slice_bitcast_fusion.2), channel_id=1, source_target_pairs={{0,1},{1,0},{2,3},{3,2},{4,5},{5,4},{6,7},{7,6},{8,9},{9,8},{10,11... | collective-permute-start | bytes 248840 | tf_op jit(solution)/shard_map/ppermute | solution.py:202
  26.3 1.4 collective-permute-start.5
  26.4 1.5 %collective-permute-start.6 = (bf16[144,288]{1,0:T(8,128)(2,1)S(1)}, bf16[144,288]{1,0:T(8,128)(2,1)S(1)}, u32[]{:S(2)}, u32[]{:S(2)}) collective-permute-start(bf16[144,288]{1,0:T(8,128)(2,1)S(1)} %slice_bitcast_fusion), channel_id=1, source_target_pairs={{0,1},{1,0},{2,3},{3,2},{4,5},{5,4},{6,7},{7,6},{8,9},{9,8},{10,11... | collective-permute-start | bytes 248840 | tf_op jit(solution)/shard_map/ppermute | solution.py:202
  27.1 55.6 %copy-start.6 = (bf16[196,2560]{1,0:T(8,128)(2,1)}, bf16[196,2560]{1,0:T(8,128)(2,1)S(1)}, u32[]{:S(2)}) copy-start(bf16[196,2560]{1,0:T(8,128)(2,1)S(1)} %slice.28.refs_0_) | copy-start | bytes 3010564
  30.5 3.7 %collective-permute-start.10 = (bf16[196,2560]{1,0:T(8,128)(2,1)S(1)}, bf16[196,2560]{1,0:T(8,128)(2,1)S(1)}, u32[]{:S(2)}, u32[]{:S(2)}) collective-permute-start(bf16[196,2560]{1,0:T(8,128)(2,1)S(1)} %pad_maximum_fusion.refs_6_), channel_id=1, source_target_pairs={{0,1},{1,0},{2,3},{3,2},{4,5},{5,4},{6,7},{7,6},{8,9},{9,8},{10,11... | collective-permute-start | bytes 3010568 | tf_op jit(solution)/shard_map/ppermute | solution.py:202
  31.0 26.0 %collective-permute-start.7 = (bf16[196,2560]{1,0:T(8,128)(2,1)S(1)}, bf16[196,2560]{1,0:T(8,128)(2,1)}, u32[]{:S(2)}, u32[]{:S(2)}) collective-permute-start(bf16[196,2560]{1,0:T(8,128)(2,1)S(1)} %slice.28.refs_0_), channel_id=1, source_target_pairs={{0,2},{1,3},{2,4},{3,5},{4,6},{5,7},{6,0},{7,1},{8,10},{9,11},{10,... | collective-permute-start | bytes 3010568 | tf_op jit(solution)/shard_map/ppermute | solution.py:198
  31.8 25.2 %collective-permute-start.8 = (bf16[196,2560]{1,0:T(8,128)(2,1)S(1)}, bf16[196,2560]{1,0:T(8,128)(2,1)}, u32[]{:S(2)}, u32[]{:S(2)}) collective-permute-start(bf16[196,2560]{1,0:T(8,128)(2,1)S(1)} %pad_maximum_fusion.refs_6_), channel_id=1, source_target_pairs={{0,6},{1,7},{2,0},{3,1},{4,2},{5,3},{6,4},{7,5},{8,14},{9,15},{10,... | collective-permute-start | bytes 3010568 | tf_op jit(solution)/shard_map/ppermute | solution.py:198
  34.2 22.8 %collective-permute-start.9 = (bf16[196,2560]{1,0:T(8,128)(2,1)S(1)}, bf16[196,2560]{1,0:T(8,128)(2,1)S(1)}, u32[]{:S(2)}, u32[]{:S(2)}) collective-permute-start(bf16[196,2560]{1,0:T(8,128)(2,1)S(1)} %slice.28.refs_0_), channel_id=1, source_target_pairs={{0,1},{1,0},{2,3},{3,2},{4,5},{5,4},{6,7},{7,6},{8,9},{9,8},{10,11... | collective-permute-start | bytes 3010568 | tf_op jit(solution)/shard_map/ppermute | solution.py:202
  34.2 49.4 %copy-start.8 = (bf16[196,2560]{1,0:T(8,128)(2,1)}, bf16[196,2560]{1,0:T(8,128)(2,1)S(1)}, u32[]{:S(2)}) copy-start(bf16[196,2560]{1,0:T(8,128)(2,1)S(1)} %collective-permute-done.10.refs_7_) | copy-start | bytes 3010564
  57.0 25.1 %collective-permute-start.11 = (bf16[196,2560]{1,0:T(8,128)(2,1)S(1)}, bf16[196,2560]{1,0:T(8,128)(2,1)S(1)}, u32[]{:S(2)}, u32[]{:S(2)}) collective-permute-start(bf16[196,2560]{1,0:T(8,128)(2,1)S(1)} %pad_maximum_fusion.refs_6_), channel_id=1, source_target_pairs={{0,2},{1,3},{2,4},{3,5},{4,6},{5,7},{6,0},{7,1},{8,10},{9,11},{10,... | collective-permute-start | bytes 3010568 | tf_op jit(solution)/shard_map/ppermute | solution.py:198
  57.5 24.6 %collective-permute-start.12 = (bf16[196,2560]{1,0:T(8,128)(2,1)S(1)}, bf16[196,2560]{1,0:T(8,128)(2,1)S(1)}, u32[]{:S(2)}, u32[]{:S(2)}) collective-permute-start(bf16[196,2560]{1,0:T(8,128)(2,1)S(1)} %slice.28.refs_0_), channel_id=1, source_target_pairs={{0,6},{1,7},{2,0},{3,1},{4,2},{5,3},{6,4},{7,5},{8,14},{9,15},{10,... | collective-permute-start | bytes 3010568 | tf_op jit(solution)/shard_map/ppermute | solution.py:198
  60.3 21.8 %collective-permute-start.13 = (bf16[196,2560]{1,0:T(8,128)(2,1)}, bf16[196,2560]{1,0:T(8,128)(2,1)S(1)}, u32[]{:S(2)}, u32[]{:S(2)}) collective-permute-start(bf16[196,2560]{1,0:T(8,128)(2,1)} %collective-permute-done.7.refs_2_), channel_id=1, source_target_pairs={{0,1},{1,0},{2,3},{3,2},{4,5},{5,4},{6,7},{7,6},{8,9},{9,8},{10,11... | collective-permute-start | bytes 3010568 | tf_op jit(solution)/shard_map/ppermute | solution.py:202
  60.3 21.9 %collective-permute-start.14 = (bf16[196,2560]{1,0:T(8,128)(2,1)}, bf16[196,2560]{1,0:T(8,128)(2,1)S(1)}, u32[]{:S(2)}, u32[]{:S(2)}) collective-permute-start(bf16[196,2560]{1,0:T(8,128)(2,1)} %collective-permute-done.8.refs_10_), channel_id=1, source_target_pairs={{0,1},{1,0},{2,3},{3,2},{4,5},{5,4},{6,7},{7,6},{8,9},{9,8},{10,11... | collective-permute-start | bytes 3010568 | tf_op jit(solution)/shard_map/ppermute | solution.py:202
  82.2 3.8 %collective-permute-start.17 = (bf16[196,2560]{1,0:T(8,128)(2,1)S(1)}, bf16[196,2560]{1,0:T(8,128)(2,1)S(1)}, u32[]{:S(2)}, u32[]{:S(2)}) collective-permute-start(bf16[196,2560]{1,0:T(8,128)(2,1)S(1)} %collective-permute-done.12.refs_4_), channel_id=1, source_target_pairs={{0,1},{1,0},{2,3},{3,2},{4,5},{5,4},{6,7},{7,6},{8,9},{9,8},{10,11... | collective-permute-start | bytes 3010568 | tf_op jit(solution)/shard_map/ppermute | solution.py:202
  82.3 4.8 %collective-permute-start.18 = (bf16[196,2560]{1,0:T(8,128)(2,1)S(1)}, bf16[196,2560]{1,0:T(8,128)(2,1)}, u32[]{:S(2)}, u32[]{:S(2)}) collective-permute-start(bf16[196,2560]{1,0:T(8,128)(2,1)S(1)} %collective-permute-done.11.refs_8_), channel_id=1, source_target_pairs={{0,1},{1,0},{2,3},{3,2},{4,5},{5,4},{6,7},{7,6},{8,9},{9,8},{10,11... | collective-permute-start | bytes 3010568 | tf_op jit(solution)/shard_map/ppermute | solution.py:202
  82.8 28.2 %collective-permute-start.15 = (bf16[196,2560]{1,0:T(8,128)(2,1)}, bf16[196,2560]{1,0:T(8,128)(2,1)S(1)}, u32[]{:S(2)}, u32[]{:S(2)}) collective-permute-start(bf16[196,2560]{1,0:T(8,128)(2,1)} %collective-permute-done.7.refs_2_), channel_id=1, source_target_pairs={{0,2},{1,3},{2,4},{3,5},{4,6},{5,7},{6,0},{7,1},{8,10},{9,11},{10,... | collective-permute-start | bytes 3010568 | tf_op jit(solution)/shard_map/ppermute | solution.py:198
  83.6 27.4 %collective-permute-start.16 = (bf16[196,2560]{1,0:T(8,128)(2,1)}, bf16[196,2560]{1,0:T(8,128)(2,1)S(1)}, u32[]{:S(2)}, u32[]{:S(2)}) collective-permute-start(bf16[196,2560]{1,0:T(8,128)(2,1)} %collective-permute-done.8.refs_10_), channel_id=1, source_target_pairs={{0,6},{1,7},{2,0},{3,1},{4,2},{5,3},{6,4},{7,5},{8,14},{9,15},{10,... | collective-permute-start | bytes 3010568 | tf_op jit(solution)/shard_map/ppermute | solution.py:198
  111.0 3.0 %collective-permute-start.19 = (bf16[196,2560]{1,0:T(8,128)(2,1)S(1)}, bf16[196,2560]{1,0:T(8,128)(2,1)S(1)}, u32[]{:S(2)}, u32[]{:S(2)}) collective-permute-start(bf16[196,2560]{1,0:T(8,128)(2,1)S(1)} %collective-permute-done.15.refs_0_), channel_id=1, source_target_pairs={{0,1},{1,0},{2,3},{3,2},{4,5},{5,4},{6,7},{7,6},{8,9},{9,8},{10,11... | collective-permute-start | bytes 3010568 | tf_op jit(solution)/shard_map/ppermute | solution.py:202
  111.0 4.1 %collective-permute-start.20 = (bf16[196,2560]{1,0:T(8,128)(2,1)S(1)}, bf16[196,2560]{1,0:T(8,128)(2,1)S(1)}, u32[]{:S(2)}, u32[]{:S(2)}) collective-permute-start(bf16[196,2560]{1,0:T(8,128)(2,1)S(1)} %collective-permute-done.16.refs_1_), channel_id=1, source_target_pairs={{0,1},{1,0},{2,3},{3,2},{4,5},{5,4},{6,7},{7,6},{8,9},{9,8},{10,11... | collective-permute-start | bytes 3010568 | tf_op jit(solution)/shard_map/ppermute | solution.py:202
  (14 other events, 147.3 us)
Sparse Core Ops, SparseCore 0:
  30.6 59.7 all-gather.1

commit v7 on v6

--- a/solution.py
+++ b/solution.py
@@ -20,7 +20,7 @@
     staged = mode == "near"
     before = []
     if staged:
-        basis, total, flip, held, basis_sems, low, high, low_sems, high_sems = refs[2 * n :]
+        basis, total, flip, low, high, low_sems, high_sems = refs[2 * n :]
     elif mode == "far":
         basis, total, flip = refs[2 * n :]
     else:
@@ -29,43 +29,24 @@
     kin, cols = basis.shape
     rest = kin - half
     gout = half - rest
-    parts = 2
     if staged:
         lefts = [pltpu.make_async_copy(lows[k], low.at[k % 2], low_sems.at[k % 2]) for k in range(n)]
         rights = [pltpu.make_async_copy(highs[k], high.at[k % 2], high_sems.at[k % 2]) for k in range(n)]
         lows, highs = [low.at[k % 2] for k in range(n)], [high.at[k % 2] for k in range(n)]
         lefts[0].start()
-        edges = [half * i // parts for i in range(parts)] + [half + rest * i // parts for i in range(parts + 1)]
-        spans = [pl.ds(a, b - a) for a, b in zip(edges, edges[1:])]
-        pieces = [pltpu.make_async_copy(basis.at[s], held.at[s], basis_sems.at[i]) for i, s in enumerate(spans)]
-        for i, piece in enumerate(pieces):
-            if i == parts:
-                rights[0].start()
-            piece.start()
-        basis = held
+        rights[0].start()
     image = lax.broadcasted_iota(I32, (rows, gout), 0) // POS
     for k in range(n):
         if staged:
             lefts[k].wait()
             if k + 1 < n:
                 lefts[k + 1].start()
-        if staged and k == 0:
-            proj = jnp.zeros((rows, cols), F32)
-            for i in range(2 * parts):
-                if i == parts:
-                    rights[0].wait()
-                    rights[1].start()
-                pieces[i].wait()
-                a, b = edges[i], edges[i + 1]
-                left = lows[0][:, a:b] if i < parts else highs[0][:, a - half : b - half]
-                proj += jnp.dot(left, basis[a:b], preferred_element_type=F32)
-        else:
-            proj = jnp.dot(lows[k][...], basis[:half], preferred_element_type=F32)
-            if staged:
-                rights[k].wait()
-                if k + 1 < n:
-                    rights[k + 1].start()
-            proj += jnp.dot(highs[k][:, :rest], basis[half:], preferred_element_type=F32)
+        proj = jnp.dot(lows[k][...], basis[:half], preferred_element_type=F32)
+        if staged:
+            rights[k].wait()
+            if k + 1 < n:
+                rights[k + 1].start()
+        proj += jnp.dot(highs[k][:, :rest], basis[half:], preferred_element_type=F32)
         flip[k % 2] = proj.astype(BF16).T
         grads = highs[k][:, rest:]
         apart = [jnp.where(image == m, grads, jnp.zeros_like(grads)) for m in range(rows // POS)]
@@ -96,13 +77,13 @@
     room = [pltpu.VMEM((2, cols, rows), BF16)]
     if mode == "near":
         pair, sems = pltpu.VMEM((2, rows, half), BF16), pltpu.SemaphoreType.DMA
-        room += [pltpu.VMEM((kin, cols), BF16), sems((4,)), pair, pair, sems((2,)), sems((2,))]
+        room += [pair, pair, sems((2,)), sems((2,))]
     elif mode == "last":
         room += [pltpu.VMEM((cols, gout), F32)]
     return pl.pallas_call(
         functools.partial(accumulate, n, cols // 2, mode, block),
         out_shape=jax.ShapeDtypeStruct((cols, gout), F32),
-        in_specs=[outside if mode == "near" else inside] * (2 * n + 1) + [inside] * len(before),
+        in_specs=[outside if mode == "near" else inside] * (2 * n) + [inside] * (1 + len(before)),
         out_specs=inside,
         scratch_shapes=room,
         compiler_params=pltpu.CompilerParams(vmem_limit_bytes=LIMITS[mode] << 20),

time: 144 us -> 146 us (1.014)
  transfers between devices with their start and end apart: 22 -> 22, of which waited for: 8 -> 8; matrix products, arithmetic and copies ran while one was open for 0% -> 0% of each run, Pallas kernels for 16% -> 17%
where the time goes in v7:
time: 146 us; the launch traced here: 145 us
  waiting for transfers between devices  57.8 us (40%)
  Pallas kernels  31.8 us (22%)
  starting transfers between devices  19.4 us (13%)
  blocking collectives  18.3 us (13%)
  between operations  13.7 us (9%)
  local copies, waits for them, and re-layouts  3.11 us (2%)
    ppermute x9, waiting for transfers between devices, up(): return lax.ppermute(a, 'own', pairs)  52.4 us
    pallas_call x3, Pallas kernels, added(): pl.pallas_call(functools.partial(accumulate, n, cols // 2, mode, block),...  26.9 us
    all_to_all x1, blocking collectives, shards(): lax.all_to_all(total.astype(jnp.float16).reshape(groups, wide, gout), 'im...  18.3 us
    ppermute x9, starting transfers between devices, up(): return lax.ppermute(a, 'own', pairs)  16.4 us
    all_gather x1, waiting for transfers between devices, balanced_basis(): return (lax.all_gather(mine, 'img', axis=0, tiled=True), first)  3.37 us
    ppermute x12, starting transfers between devices, swap(): return lax.ppermute(a, 'own', [(o, o ^ 1) for o in range(CHIPS * CORES)])  2.93 us
  transfers between devices with their start and end apart: 22, of which 8 were waited for; matrix products, arithmetic and copies ran while one was open for 0% of the time, Pallas kernels for 17%

profile of v7, /device:TPU:0, one launch (start us, length us, event | category | flops | bytes accessed | tf_op | source)
XLA Modules:
  0.0 145.4 jit_solution(16765644857789573499)
XLA Ops:
  6.5 1.2 constant_dynamic-slice_fusion.slots
  7.8 0.6 copy-done.3
  8.4 2.3 %shard_map.55 = (bf16[2,144,288]{2,1,0:T(8,128)(2,1)S(1)}, bf16[2,144,288]{2,1,0:T(8,128)(2,1)S(1)}, bf16[2,144,288]{2,1,0:T(8,128)(2,1)S(1)}, bf16[2,144,288]{2,1,0:T(8,128)(2,1)S(1)}) custom-call(s32[1]{0:T(128)} %bitcast.me, s32[8]{0:T(128)S(1)} %copy-done.3, bf16[288,1152]{1,0:T(8,128)(2,1)S(1)} %constant_dynamic-slice_fusion.slots), custom_call_target="tpu_custom_call" | custom-call | flops 764411904 | bytes 1327104 | tf_op jit(solution)/shard_map/pallas_call | solution.py:125
  10.7 2.1 %collective-permute-start = (bf16[2,144,288]{2,1,0:T(8,128)(2,1)S(1)}, bf16[2,144,288]{2,1,0:T(8,128)(2,1)S(1)}, u32[]{:S(2)}, u32[]{:S(2)}) collective-permute-start(bf16[2,144,288]{2,1,0:T(8,128)(2,1)S(1)} %get-tuple-element.37), channel_id=1, source_target_pairs={{0,2},{1,3},{2,4},{3,5},{4,6},{5,7},{6,0},{7,1},{8,10},{9,11},{10,... | collective-permute-start | bytes 497672 | tf_op jit(solution)/shard_map/ppermute | solution.py:179
  12.8 3.6 %collective-permute-start.1 = (bf16[2,144,288]{2,1,0:T(8,128)(2,1)S(1)}, bf16[2,144,288]{2,1,0:T(8,128)(2,1)S(1)}, u32[]{:S(2)}, u32[]{:S(2)}) collective-permute-start(bf16[2,144,288]{2,1,0:T(8,128)(2,1)S(1)} %get-tuple-element.38), channel_id=1, source_target_pairs={{0,4},{1,5},{2,6},{3,7},{4,0},{5,1},{6,2},{7,3},{8,12},{9,13},{10,... | collective-permute-start | bytes 497672 | tf_op jit(solution)/shard_map/ppermute | solution.py:179
  16.4 1.0 collective-permute-start.2
  17.8 2.5 %collective-permute-done.refs_1_ = bf16[2,144,288]{2,1,0:T(8,128)(2,1)S(1)} collective-permute-done((bf16[2,144,288]{2,1,0:T(8,128)(2,1)S(1)}, bf16[2,144,288]{2,1,0:T(8,128)(2,1)S(1)}, u32[]{:S(2)}, u32[]{:S(2)}) %collective-permute-start) | collective-permute-done | bytes 165920 | tf_op jit(solution)/shard_map/ppermute | solution.py:179
  20.4 5.8 %collective-permute-done.1.refs_2_ = bf16[2,144,288]{2,1,0:T(8,128)(2,1)S(1)} collective-permute-done((bf16[2,144,288]{2,1,0:T(8,128)(2,1)S(1)}, bf16[2,144,288]{2,1,0:T(8,128)(2,1)S(1)}, u32[]{:S(2)}, u32[]{:S(2)}) %collective-permute-start.1) | collective-permute-done | bytes 165920 | tf_op jit(solution)/shard_map/ppermute | solution.py:179
  27.9 2.6 %shard_map.56 = bf16[288,640]{1,0:T(8,128)(2,1)} custom-call(s32[1]{0:T(128)} %bitcast.me, s32[8]{0:T(128)S(1)} %copy-done.3, bf16[2,144,288]{2,1,0:T(8,128)(2,1)S(1)} %get-tuple-element.56.refs_0_, bf16[2,144,288]{2,1,0:T(8,128)(2,1)S(1)} %collective-permute-done.refs_1_, bf16[2,144,288]{2,1,0:T(8,128)(2,1)S(1)} %collective-permute-done.1.refs_2_, ...), custom_call_target="tpu_custom_call" | custom-call | flops 424673280 | bytes 737280 | tf_op jit(solution)/shard_map/pallas_call | solution.py:165
  31.0 0.8 collective-permute-start.7
  31.8 2.4 %collective-permute-start.8 = (bf16[196,2560]{1,0:T(8,128)(2,1)S(1)}, bf16[196,2560]{1,0:T(8,128)(2,1)}, u32[]{:S(2)}, u32[]{:S(2)}) collective-permute-start(bf16[196,2560]{1,0:T(8,128)(2,1)S(1)} %pad_maximum_fusion.refs_6_), channel_id=1, source_target_pairs={{0,6},{1,7},{2,0},{3,1},{4,2},{5,3},{6,4},{7,5},{8,14},{9,15},{10,... | collective-permute-start | bytes 3010568 | tf_op jit(solution)/shard_map/ppermute | solution.py:179
  34.2 22.8 %collective-permute-done.7.refs_2_ = bf16[196,2560]{1,0:T(8,128)(2,1)} collective-permute-done((bf16[196,2560]{1,0:T(8,128)(2,1)S(1)}, bf16[196,2560]{1,0:T(8,128)(2,1)}, u32[]{:S(2)}, u32[]{:S(2)}) %collective-permute-start.7) | collective-permute-done | bytes 1003552 | tf_op jit(solution)/shard_map/ppermute | solution.py:179
  57.5 2.8 %collective-permute-start.12 = (bf16[196,2560]{1,0:T(8,128)(2,1)S(1)}, bf16[196,2560]{1,0:T(8,128)(2,1)S(1)}, u32[]{:S(2)}, u32[]{:S(2)}) collective-permute-start(bf16[196,2560]{1,0:T(8,128)(2,1)S(1)} %slice.28.refs_0_), channel_id=1, source_target_pairs={{0,6},{1,7},{2,0},{3,1},{4,2},{5,3},{6,4},{7,5},{8,14},{9,15},{10,... | collective-permute-start | bytes 3010568 | tf_op jit(solution)/shard_map/ppermute | solution.py:179
  60.8 21.3 %collective-permute-done.11.refs_8_ = bf16[196,2560]{1,0:T(8,128)(2,1)S(1)} collective-permute-done((bf16[196,2560]{1,0:T(8,128)(2,1)S(1)}, bf16[196,2560]{1,0:T(8,128)(2,1)S(1)}, u32[]{:S(2)}, u32[]{:S(2)}) %collective-permute-start.11) | collective-permute-done | bytes 1003552 | tf_op jit(solution)/shard_map/ppermute | solution.py:179
  82.8 0.8 collective-permute-start.15
  83.6 2.4 %collective-permute-start.16 = (bf16[196,2560]{1,0:T(8,128)(2,1)}, bf16[196,2560]{1,0:T(8,128)(2,1)S(1)}, u32[]{:S(2)}, u32[]{:S(2)}) collective-permute-start(bf16[196,2560]{1,0:T(8,128)(2,1)} %collective-permute-done.8.refs_10_), channel_id=1, source_target_pairs={{0,6},{1,7},{2,0},{3,1},{4,2},{5,3},{6,4},{7,5},{8,14},{9,15},{10,... | collective-permute-start | bytes 3010568 | tf_op jit(solution)/shard_map/ppermute | solution.py:179
  86.1 1.0 copy-done.14
  87.0 3.4 %all-gather.2.cloned.1.call-done.refs_12_.refs_2_ = bf16[4608,640]{1,0:T(8,128)(2,1)} async-done(((bf16[288,640]{1,0:T(8,128)(2,1)}), bf16[4608,640]{1,0:T(8,128)(2,1)}) %all-gather.2.cloned.1.call-update) | async-done | bytes 5898256 | tf_op jit(solution)/shard_map/all_gather | solution.py:196
  90.4 21.8 %shard_map.57.refs_4_ = f32[640,512]{1,0:T(8,128)} custom-call(bf16[196,2560]{1,0:T(8,128)(2,1)} %copy-done.6, bf16[196,2560]{1,0:T(8,128)(2,1)} %copy-done.9, bf16[196,2560]{1,0:T(8,128)(2,1)} %collective-permute-done.7.refs_2_, bf16[196,2560]{1,0:T(8,128)(2,1)} %copy-done.12, bf16[196,2560]{1,0:T(8,128)(2,1)} %copy-done.11, bf16[196,2560]{1,0:T(8,128)(2,1)} %copy-done.14, ...), custom_call_target="tpu_custom_call" | custom-call | flops 6936330240 | bytes 17940480 | tf_op jit(solution)/shard_map/pallas_call | solution.py:83
  112.8 2.4 %shard_map.58.refs_3_ = f32[640,512]{1,0:T(8,128)S(1)} custom-call(bf16[196,2560]{1,0:T(8,128)(2,1)S(1)} %collective-permute-done.15.refs_0_, bf16[196,2560]{1,0:T(8,128)(2,1)S(1)} %collective-permute-done.16.refs_1_, bf16[4608,640]{1,0:T(8,128)(2,1)S(1)} %copy-done.1), custom_call_target="tpu_custom_call" | custom-call | flops 1156055040 | bytes 7905280 | tf_op jit(solution)/shard_map/pallas_call | solution.py:83
  115.2 1.2 collective-permute-done.20.refs_1_
  116.4 2.8 %shard_map.59 = f32[640,512]{1,0:T(8,128)S(1)} custom-call(bf16[196,2560]{1,0:T(8,128)(2,1)S(1)} %collective-permute-done.19.refs_0_, bf16[196,2560]{1,0:T(8,128)(2,1)S(1)} %collective-permute-done.20.refs_1_, bf16[4608,640]{1,0:T(8,128)(2,1)S(1)} %copy-done.1, f32[640,512]{1,0:T(8,128)S(1)} %shard_map.58.refs_3_, f32[640,512]{1,0:T(8,128)S(1)} %copy-done.2), custom_call_target="tpu_custom_call" | custom-call | flops 1156055040 | bytes 7905280 | tf_op jit(solution)/shard_map/pallas_call | solution.py:83
  119.3 18.3 %all_to_all.5 = f16[16,40,512]{2,1,0:T(8,128)(2,1)S(1)} all-to-all(f16[16,40,512]{2,1,0:T(8,128)(2,1)S(1)} %bitcast.14), channel_id=1, replica_groups=mesh['img'=16,'own'=8] {'img'}, dimensions={0} | all-to-all | bytes 1310720 | tf_op jit(solution)/shard_map/all_to_all | solution.py:231
  137.9 0.6 broadcast_multiply_fusion
  (73 shorter events, 5.2 us)
Async XLA Ops:
  6.5 83.9 %all-gather.2.cloned.1.call-start = ((), (), s32[]{:S(2)}) async-start(), calls=%async_computation.1 | async-start | bytes 6266880 | tf_op jit(solution)/shard_map/all_gather | solution.py:196
  10.7 9.6 %collective-permute-start = (bf16[2,144,288]{2,1,0:T(8,128)(2,1)S(1)}, bf16[2,144,288]{2,1,0:T(8,128)(2,1)S(1)}, u32[]{:S(2)}, u32[]{:S(2)}) collective-permute-start(bf16[2,144,288]{2,1,0:T(8,128)(2,1)S(1)} %get-tuple-element.37), channel_id=1, source_target_pairs={{0,2},{1,3},{2,4},{3,5},{4,6},{5,7},{6,0},{7,1},{8,10},{9,11},{10,... | collective-permute-start | bytes 497672 | tf_op jit(solution)/shard_map/ppermute | solution.py:179
  12.8 13.5 %collective-permute-start.1 = (bf16[2,144,288]{2,1,0:T(8,128)(2,1)S(1)}, bf16[2,144,288]{2,1,0:T(8,128)(2,1)S(1)}, u32[]{:S(2)}, u32[]{:S(2)}) collective-permute-start(bf16[2,144,288]{2,1,0:T(8,128)(2,1)S(1)} %get-tuple-element.38), channel_id=1, source_target_pairs={{0,4},{1,5},{2,6},{3,7},{4,0},{5,1},{6,2},{7,3},{8,12},{9,13},{10,... | collective-permute-start | bytes 497672 | tf_op jit(solution)/shard_map/ppermute | solution.py:179
  16.4 10.0 %collective-permute-start.2 = (bf16[2,144,288]{2,1,0:T(8,128)(2,1)S(1)}, bf16[2,144,288]{2,1,0:T(8,128)(2,1)S(1)}, u32[]{:S(2)}, u32[]{:S(2)}) collective-permute-start(bf16[2,144,288]{2,1,0:T(8,128)(2,1)S(1)} %get-tuple-element.39), channel_id=1, source_target_pairs={{0,6},{1,7},{2,0},{3,1},{4,2},{5,3},{6,4},{7,5},{8,14},{9,15},{10,... | collective-permute-start | bytes 497672 | tf_op jit(solution)/shard_map/ppermute | solution.py:179
  17.4 9.8 %collective-permute-start.3 = (bf16[144,288]{1,0:T(8,128)(2,1)S(1)}, bf16[144,288]{1,0:T(8,128)(2,1)S(1)}, u32[]{:S(2)}, u32[]{:S(2)}) collective-permute-start(bf16[144,288]{1,0:T(8,128)(2,1)S(1)} %slice_bitcast_fusion.3), channel_id=1, source_target_pairs={{0,1},{1,0},{2,3},{3,2},{4,5},{5,4},{6,7},{7,6},{8,9},{9,8},{10,11... | collective-permute-start | bytes 248840 | tf_op jit(solution)/shard_map/ppermute | solution.py:183
  20.3 6.8 %collective-permute-start.4 = (bf16[144,288]{1,0:T(8,128)(2,1)S(1)}, bf16[144,288]{1,0:T(8,128)(2,1)S(1)}, u32[]{:S(2)}, u32[]{:S(2)}) collective-permute-start(bf16[144,288]{1,0:T(8,128)(2,1)S(1)} %slice_bitcast_fusion.2), channel_id=1, source_target_pairs={{0,1},{1,0},{2,3},{3,2},{4,5},{5,4},{6,7},{7,6},{8,9},{9,8},{10,11... | collective-permute-start | bytes 248840 | tf_op jit(solution)/shard_map/ppermute | solution.py:183
  26.3 1.4 collective-permute-start.5
  26.4 1.5 %collective-permute-start.6 = (bf16[144,288]{1,0:T(8,128)(2,1)S(1)}, bf16[144,288]{1,0:T(8,128)(2,1)S(1)}, u32[]{:S(2)}, u32[]{:S(2)}) collective-permute-start(bf16[144,288]{1,0:T(8,128)(2,1)S(1)} %slice_bitcast_fusion), channel_id=1, source_target_pairs={{0,1},{1,0},{2,3},{3,2},{4,5},{5,4},{6,7},{7,6},{8,9},{9,8},{10,11... | collective-permute-start | bytes 248840 | tf_op jit(solution)/shard_map/ppermute | solution.py:183
  27.1 55.6 %copy-start.6 = (bf16[196,2560]{1,0:T(8,128)(2,1)}, bf16[196,2560]{1,0:T(8,128)(2,1)S(1)}, u32[]{:S(2)}) copy-start(bf16[196,2560]{1,0:T(8,128)(2,1)S(1)} %slice.28.refs_0_) | copy-start | bytes 3010564
  30.5 3.7 %collective-permute-start.10 = (bf16[196,2560]{1,0:T(8,128)(2,1)S(1)}, bf16[196,2560]{1,0:T(8,128)(2,1)S(1)}, u32[]{:S(2)}, u32[]{:S(2)}) collective-permute-start(bf16[196,2560]{1,0:T(8,128)(2,1)S(1)} %pad_maximum_fusion.refs_6_), channel_id=1, source_target_pairs={{0,1},{1,0},{2,3},{3,2},{4,5},{5,4},{6,7},{7,6},{8,9},{9,8},{10,11... | collective-permute-start | bytes 3010568 | tf_op jit(solution)/shard_map/ppermute | solution.py:183
  31.0 26.0 %collective-permute-start.7 = (bf16[196,2560]{1,0:T(8,128)(2,1)S(1)}, bf16[196,2560]{1,0:T(8,128)(2,1)}, u32[]{:S(2)}, u32[]{:S(2)}) collective-permute-start(bf16[196,2560]{1,0:T(8,128)(2,1)S(1)} %slice.28.refs_0_), channel_id=1, source_target_pairs={{0,2},{1,3},{2,4},{3,5},{4,6},{5,7},{6,0},{7,1},{8,10},{9,11},{10,... | collective-permute-start | bytes 3010568 | tf_op jit(solution)/shard_map/ppermute | solution.py:179
  31.8 25.2 %collective-permute-start.8 = (bf16[196,2560]{1,0:T(8,128)(2,1)S(1)}, bf16[196,2560]{1,0:T(8,128)(2,1)}, u32[]{:S(2)}, u32[]{:S(2)}) collective-permute-start(bf16[196,2560]{1,0:T(8,128)(2,1)S(1)} %pad_maximum_fusion.refs_6_), channel_id=1, source_target_pairs={{0,6},{1,7},{2,0},{3,1},{4,2},{5,3},{6,4},{7,5},{8,14},{9,15},{10,... | collective-permute-start | bytes 3010568 | tf_op jit(solution)/shard_map/ppermute | solution.py:179
  34.2 22.8 %collective-permute-start.9 = (bf16[196,2560]{1,0:T(8,128)(2,1)S(1)}, bf16[196,2560]{1,0:T(8,128)(2,1)S(1)}, u32[]{:S(2)}, u32[]{:S(2)}) collective-permute-start(bf16[196,2560]{1,0:T(8,128)(2,1)S(1)} %slice.28.refs_0_), channel_id=1, source_target_pairs={{0,1},{1,0},{2,3},{3,2},{4,5},{5,4},{6,7},{7,6},{8,9},{9,8},{10,11... | collective-permute-start | bytes 3010568 | tf_op jit(solution)/shard_map/ppermute | solution.py:183
  34.2 49.4 %copy-start.8 = (bf16[196,2560]{1,0:T(8,128)(2,1)}, bf16[196,2560]{1,0:T(8,128)(2,1)S(1)}, u32[]{:S(2)}) copy-start(bf16[196,2560]{1,0:T(8,128)(2,1)S(1)} %collective-permute-done.10.refs_7_) | copy-start | bytes 3010564
  57.0 25.1 %collective-permute-start.11 = (bf16[196,2560]{1,0:T(8,128)(2,1)S(1)}, bf16[196,2560]{1,0:T(8,128)(2,1)S(1)}, u32[]{:S(2)}, u32[]{:S(2)}) collective-permute-start(bf16[196,2560]{1,0:T(8,128)(2,1)S(1)} %pad_maximum_fusion.refs_6_), channel_id=1, source_target_pairs={{0,2},{1,3},{2,4},{3,5},{4,6},{5,7},{6,0},{7,1},{8,10},{9,11},{10,... | collective-permute-start | bytes 3010568 | tf_op jit(solution)/shard_map/ppermute | solution.py:179
  57.5 24.6 %collective-permute-start.12 = (bf16[196,2560]{1,0:T(8,128)(2,1)S(1)}, bf16[196,2560]{1,0:T(8,128)(2,1)S(1)}, u32[]{:S(2)}, u32[]{:S(2)}) collective-permute-start(bf16[196,2560]{1,0:T(8,128)(2,1)S(1)} %slice.28.refs_0_), channel_id=1, source_target_pairs={{0,6},{1,7},{2,0},{3,1},{4,2},{5,3},{6,4},{7,5},{8,14},{9,15},{10,... | collective-permute-start | bytes 3010568 | tf_op jit(solution)/shard_map/ppermute | solution.py:179
  60.3 21.8 %collective-permute-start.13 = (bf16[196,2560]{1,0:T(8,128)(2,1)}, bf16[196,2560]{1,0:T(8,128)(2,1)S(1)}, u32[]{:S(2)}, u32[]{:S(2)}) collective-permute-start(bf16[196,2560]{1,0:T(8,128)(2,1)} %collective-permute-done.7.refs_2_), channel_id=1, source_target_pairs={{0,1},{1,0},{2,3},{3,2},{4,5},{5,4},{6,7},{7,6},{8,9},{9,8},{10,11... | collective-permute-start | bytes 3010568 | tf_op jit(solution)/shard_map/ppermute | solution.py:183
  60.3 21.9 %collective-permute-start.14 = (bf16[196,2560]{1,0:T(8,128)(2,1)}, bf16[196,2560]{1,0:T(8,128)(2,1)S(1)}, u32[]{:S(2)}, u32[]{:S(2)}) collective-permute-start(bf16[196,2560]{1,0:T(8,128)(2,1)} %collective-permute-done.8.refs_10_), channel_id=1, source_target_pairs={{0,1},{1,0},{2,3},{3,2},{4,5},{5,4},{6,7},{7,6},{8,9},{9,8},{10,11... | collective-permute-start | bytes 3010568 | tf_op jit(solution)/shard_map/ppermute | solution.py:183
  82.2 3.8 %collective-permute-start.17 = (bf16[196,2560]{1,0:T(8,128)(2,1)S(1)}, bf16[196,2560]{1,0:T(8,128)(2,1)S(1)}, u32[]{:S(2)}, u32[]{:S(2)}) collective-permute-start(bf16[196,2560]{1,0:T(8,128)(2,1)S(1)} %collective-permute-done.12.refs_4_), channel_id=1, source_target_pairs={{0,1},{1,0},{2,3},{3,2},{4,5},{5,4},{6,7},{7,6},{8,9},{9,8},{10,11... | collective-permute-start | bytes 3010568 | tf_op jit(solution)/shard_map/ppermute | solution.py:183
  82.3 4.8 %collective-permute-start.18 = (bf16[196,2560]{1,0:T(8,128)(2,1)S(1)}, bf16[196,2560]{1,0:T(8,128)(2,1)}, u32[]{:S(2)}, u32[]{:S(2)}) collective-permute-start(bf16[196,2560]{1,0:T(8,128)(2,1)S(1)} %collective-permute-done.11.refs_8_), channel_id=1, source_target_pairs={{0,1},{1,0},{2,3},{3,2},{4,5},{5,4},{6,7},{7,6},{8,9},{9,8},{10,11... | collective-permute-start | bytes 3010568 | tf_op jit(solution)/shard_map/ppermute | solution.py:183
  82.8 29.4 %collective-permute-start.15 = (bf16[196,2560]{1,0:T(8,128)(2,1)}, bf16[196,2560]{1,0:T(8,128)(2,1)S(1)}, u32[]{:S(2)}, u32[]{:S(2)}) collective-permute-start(bf16[196,2560]{1,0:T(8,128)(2,1)} %collective-permute-done.7.refs_2_), channel_id=1, source_target_pairs={{0,2},{1,3},{2,4},{3,5},{4,6},{5,7},{6,0},{7,1},{8,10},{9,11},{10,... | collective-permute-start | bytes 3010568 | tf_op jit(solution)/shard_map/ppermute | solution.py:179
  83.6 28.6 %collective-permute-start.16 = (bf16[196,2560]{1,0:T(8,128)(2,1)}, bf16[196,2560]{1,0:T(8,128)(2,1)S(1)}, u32[]{:S(2)}, u32[]{:S(2)}) collective-permute-start(bf16[196,2560]{1,0:T(8,128)(2,1)} %collective-permute-done.8.refs_10_), channel_id=1, source_target_pairs={{0,6},{1,7},{2,0},{3,1},{4,2},{5,3},{6,4},{7,5},{8,14},{9,15},{10,... | collective-permute-start | bytes 3010568 | tf_op jit(solution)/shard_map/ppermute | solution.py:179
  112.2 3.0 %collective-permute-start.19 = (bf16[196,2560]{1,0:T(8,128)(2,1)S(1)}, bf16[196,2560]{1,0:T(8,128)(2,1)S(1)}, u32[]{:S(2)}, u32[]{:S(2)}) collective-permute-start(bf16[196,2560]{1,0:T(8,128)(2,1)S(1)} %collective-permute-done.15.refs_0_), channel_id=1, source_target_pairs={{0,1},{1,0},{2,3},{3,2},{4,5},{5,4},{6,7},{7,6},{8,9},{9,8},{10,11... | collective-permute-start | bytes 3010568 | tf_op jit(solution)/shard_map/ppermute | solution.py:183
  112.3 4.1 %collective-permute-start.20 = (bf16[196,2560]{1,0:T(8,128)(2,1)S(1)}, bf16[196,2560]{1,0:T(8,128)(2,1)S(1)}, u32[]{:S(2)}, u32[]{:S(2)}) collective-permute-start(bf16[196,2560]{1,0:T(8,128)(2,1)S(1)} %collective-permute-done.16.refs_1_), channel_id=1, source_target_pairs={{0,1},{1,0},{2,3},{3,2},{4,5},{5,4},{6,7},{7,6},{8,9},{9,8},{10,11... | collective-permute-start | bytes 3010568 | tf_op jit(solution)/shard_map/ppermute | solution.py:183
  (14 other events, 148.5 us)
Sparse Core Ops, SparseCore 0:
  30.6 59.7 all-gather.1

commit v8 on v6

--- a/solution.py
+++ b/solution.py
@@ -47,15 +47,17 @@
     for k in range(n):
         if staged:
             lefts[k].wait()
-            if k + 1 < n:
+            if 0 < k < n - 1:
                 lefts[k + 1].start()
         if staged and k == 0:
             proj = jnp.zeros((rows, cols), F32)
             for i in range(2 * parts):
                 if i == parts:
                     rights[0].wait()
+                    lefts[1].start()
+                pieces[i].wait()
+                if i == 2 * parts - 1:
                     rights[1].start()
-                pieces[i].wait()
                 a, b = edges[i], edges[i + 1]
                 left = lows[0][:, a:b] if i < parts else highs[0][:, a - half : b - half]
                 proj += jnp.dot(left, basis[a:b], preferred_element_type=F32)

time: 144 us -> 144 us (level)
  no operation moved by 1% of the time
where the time goes in v8:
time: 144 us
  waiting for transfers between devices  57.8 us (40%)
  Pallas kernels  30.5 us (21%)
  starting transfers between devices  19.4 us (13%)
  blocking collectives  18.3 us (13%)
  between operations  13.7 us (10%)
  local copies, waits for them, and re-layouts  3.11 us (2%)
    ppermute x9, waiting for transfers between devices, up(): return lax.ppermute(a, 'own', pairs)  52.4 us
    pallas_call x3, Pallas kernels, added(): pl.pallas_call(functools.partial(accumulate, n, cols // 2, mode, block),...  25.7 us
    all_to_all x1, blocking collectives, shards(): lax.all_to_all(total.astype(jnp.float16).reshape(groups, wide, gout), 'im...  18.3 us
    ppermute x9, starting transfers between devices, up(): return lax.ppermute(a, 'own', pairs)  16.4 us
    all_gather x1, waiting for transfers between devices, balanced_basis(): return (lax.all_gather(mine, 'img', axis=0, tiled=True), first)  3.37 us
    ppermute x12, starting transfers between devices, swap(): return lax.ppermute(a, 'own', [(o, o ^ 1) for o in range(CHIPS * CORES)])  2.93 us
  transfers between devices with their start and end apart: 22, of which 8 were waited for; matrix products, arithmetic and copies ran while one was open for 0% of the time, Pallas kernels for 16%

profile of v8, /device:TPU:0, one launch (start us, length us, event | category | flops | bytes accessed | tf_op | source)
XLA Modules:
  0.0 144.2 jit_solution(6259732653529722447)
XLA Ops:
  6.5 1.2 constant_dynamic-slice_fusion.slots
  7.8 0.6 copy-done.3
  8.4 2.3 %shard_map.55 = (bf16[2,144,288]{2,1,0:T(8,128)(2,1)S(1)}, bf16[2,144,288]{2,1,0:T(8,128)(2,1)S(1)}, bf16[2,144,288]{2,1,0:T(8,128)(2,1)S(1)}, bf16[2,144,288]{2,1,0:T(8,128)(2,1)S(1)}) custom-call(s32[1]{0:T(128)} %bitcast.me, s32[8]{0:T(128)S(1)} %copy-done.3, bf16[288,1152]{1,0:T(8,128)(2,1)S(1)} %constant_dynamic-slice_fusion.slots), custom_call_target="tpu_custom_call" | custom-call | flops 764411904 | bytes 1327104 | tf_op jit(solution)/shard_map/pallas_call | solution.py:146
  10.7 2.1 %collective-permute-start = (bf16[2,144,288]{2,1,0:T(8,128)(2,1)S(1)}, bf16[2,144,288]{2,1,0:T(8,128)(2,1)S(1)}, u32[]{:S(2)}, u32[]{:S(2)}) collective-permute-start(bf16[2,144,288]{2,1,0:T(8,128)(2,1)S(1)} %get-tuple-element.37), channel_id=1, source_target_pairs={{0,2},{1,3},{2,4},{3,5},{4,6},{5,7},{6,0},{7,1},{8,10},{9,11},{10,... | collective-permute-start | bytes 497672 | tf_op jit(solution)/shard_map/ppermute | solution.py:200
  12.8 3.6 %collective-permute-start.1 = (bf16[2,144,288]{2,1,0:T(8,128)(2,1)S(1)}, bf16[2,144,288]{2,1,0:T(8,128)(2,1)S(1)}, u32[]{:S(2)}, u32[]{:S(2)}) collective-permute-start(bf16[2,144,288]{2,1,0:T(8,128)(2,1)S(1)} %get-tuple-element.38), channel_id=1, source_target_pairs={{0,4},{1,5},{2,6},{3,7},{4,0},{5,1},{6,2},{7,3},{8,12},{9,13},{10,... | collective-permute-start | bytes 497672 | tf_op jit(solution)/shard_map/ppermute | solution.py:200
  16.4 1.0 collective-permute-start.2
  17.8 2.5 %collective-permute-done.refs_1_ = bf16[2,144,288]{2,1,0:T(8,128)(2,1)S(1)} collective-permute-done((bf16[2,144,288]{2,1,0:T(8,128)(2,1)S(1)}, bf16[2,144,288]{2,1,0:T(8,128)(2,1)S(1)}, u32[]{:S(2)}, u32[]{:S(2)}) %collective-permute-start) | collective-permute-done | bytes 165920 | tf_op jit(solution)/shard_map/ppermute | solution.py:200
  20.4 5.8 %collective-permute-done.1.refs_2_ = bf16[2,144,288]{2,1,0:T(8,128)(2,1)S(1)} collective-permute-done((bf16[2,144,288]{2,1,0:T(8,128)(2,1)S(1)}, bf16[2,144,288]{2,1,0:T(8,128)(2,1)S(1)}, u32[]{:S(2)}, u32[]{:S(2)}) %collective-permute-start.1) | collective-permute-done | bytes 165920 | tf_op jit(solution)/shard_map/ppermute | solution.py:200
  27.9 2.6 %shard_map.56 = bf16[288,640]{1,0:T(8,128)(2,1)} custom-call(s32[1]{0:T(128)} %bitcast.me, s32[8]{0:T(128)S(1)} %copy-done.3, bf16[2,144,288]{2,1,0:T(8,128)(2,1)S(1)} %get-tuple-element.56.refs_0_, bf16[2,144,288]{2,1,0:T(8,128)(2,1)S(1)} %collective-permute-done.refs_1_, bf16[2,144,288]{2,1,0:T(8,128)(2,1)S(1)} %collective-permute-done.1.refs_2_, ...), custom_call_target="tpu_custom_call" | custom-call | flops 424673280 | bytes 737280 | tf_op jit(solution)/shard_map/pallas_call | solution.py:186
  31.0 0.8 collective-permute-start.7
  31.8 2.4 %collective-permute-start.8 = (bf16[196,2560]{1,0:T(8,128)(2,1)S(1)}, bf16[196,2560]{1,0:T(8,128)(2,1)}, u32[]{:S(2)}, u32[]{:S(2)}) collective-permute-start(bf16[196,2560]{1,0:T(8,128)(2,1)S(1)} %pad_maximum_fusion.refs_6_), channel_id=1, source_target_pairs={{0,6},{1,7},{2,0},{3,1},{4,2},{5,3},{6,4},{7,5},{8,14},{9,15},{10,... | collective-permute-start | bytes 3010568 | tf_op jit(solution)/shard_map/ppermute | solution.py:200
  34.2 22.8 %collective-permute-done.7.refs_2_ = bf16[196,2560]{1,0:T(8,128)(2,1)} collective-permute-done((bf16[196,2560]{1,0:T(8,128)(2,1)S(1)}, bf16[196,2560]{1,0:T(8,128)(2,1)}, u32[]{:S(2)}, u32[]{:S(2)}) %collective-permute-start.7) | collective-permute-done | bytes 1003552 | tf_op jit(solution)/shard_map/ppermute | solution.py:200
  57.5 2.8 %collective-permute-start.12 = (bf16[196,2560]{1,0:T(8,128)(2,1)S(1)}, bf16[196,2560]{1,0:T(8,128)(2,1)S(1)}, u32[]{:S(2)}, u32[]{:S(2)}) collective-permute-start(bf16[196,2560]{1,0:T(8,128)(2,1)S(1)} %slice.28.refs_0_), channel_id=1, source_target_pairs={{0,6},{1,7},{2,0},{3,1},{4,2},{5,3},{6,4},{7,5},{8,14},{9,15},{10,... | collective-permute-start | bytes 3010568 | tf_op jit(solution)/shard_map/ppermute | solution.py:200
  60.8 21.3 %collective-permute-done.11.refs_8_ = bf16[196,2560]{1,0:T(8,128)(2,1)S(1)} collective-permute-done((bf16[196,2560]{1,0:T(8,128)(2,1)S(1)}, bf16[196,2560]{1,0:T(8,128)(2,1)S(1)}, u32[]{:S(2)}, u32[]{:S(2)}) %collective-permute-start.11) | collective-permute-done | bytes 1003552 | tf_op jit(solution)/shard_map/ppermute | solution.py:200
  82.8 0.8 collective-permute-start.15
  83.6 2.4 %collective-permute-start.16 = (bf16[196,2560]{1,0:T(8,128)(2,1)}, bf16[196,2560]{1,0:T(8,128)(2,1)S(1)}, u32[]{:S(2)}, u32[]{:S(2)}) collective-permute-start(bf16[196,2560]{1,0:T(8,128)(2,1)} %collective-permute-done.8.refs_10_), channel_id=1, source_target_pairs={{0,6},{1,7},{2,0},{3,1},{4,2},{5,3},{6,4},{7,5},{8,14},{9,15},{10,... | collective-permute-start | bytes 3010568 | tf_op jit(solution)/shard_map/ppermute | solution.py:200
  86.1 1.0 copy-done.14
  87.0 3.4 %all-gather.2.cloned.1.call-done.refs_12_.refs_2_ = bf16[4608,640]{1,0:T(8,128)(2,1)} async-done(((bf16[288,640]{1,0:T(8,128)(2,1)}), bf16[4608,640]{1,0:T(8,128)(2,1)}) %all-gather.2.cloned.1.call-update) | async-done | bytes 5898256 | tf_op jit(solution)/shard_map/all_gather | solution.py:217
  90.4 20.5 %shard_map.57.refs_4_ = f32[640,512]{1,0:T(8,128)} custom-call(bf16[196,2560]{1,0:T(8,128)(2,1)} %copy-done.6, bf16[196,2560]{1,0:T(8,128)(2,1)} %copy-done.9, bf16[196,2560]{1,0:T(8,128)(2,1)} %collective-permute-done.7.refs_2_, bf16[196,2560]{1,0:T(8,128)(2,1)} %copy-done.12, bf16[196,2560]{1,0:T(8,128)(2,1)} %copy-done.11, bf16[196,2560]{1,0:T(8,128)(2,1)} %copy-done.14, ...), custom_call_target="tpu_custom_call" | custom-call | flops 6936330240 | bytes 17940480 | tf_op jit(solution)/shard_map/pallas_call | solution.py:104
  111.6 2.4 %shard_map.58.refs_3_ = f32[640,512]{1,0:T(8,128)S(1)} custom-call(bf16[196,2560]{1,0:T(8,128)(2,1)S(1)} %collective-permute-done.15.refs_0_, bf16[196,2560]{1,0:T(8,128)(2,1)S(1)} %collective-permute-done.16.refs_1_, bf16[4608,640]{1,0:T(8,128)(2,1)S(1)} %copy-done.1), custom_call_target="tpu_custom_call" | custom-call | flops 1156055040 | bytes 7905280 | tf_op jit(solution)/shard_map/pallas_call | solution.py:104
  113.9 1.2 collective-permute-done.20.refs_1_
  115.1 2.8 %shard_map.59 = f32[640,512]{1,0:T(8,128)S(1)} custom-call(bf16[196,2560]{1,0:T(8,128)(2,1)S(1)} %collective-permute-done.19.refs_0_, bf16[196,2560]{1,0:T(8,128)(2,1)S(1)} %collective-permute-done.20.refs_1_, bf16[4608,640]{1,0:T(8,128)(2,1)S(1)} %copy-done.1, f32[640,512]{1,0:T(8,128)S(1)} %shard_map.58.refs_3_, f32[640,512]{1,0:T(8,128)S(1)} %copy-done.2), custom_call_target="tpu_custom_call" | custom-call | flops 1156055040 | bytes 7905280 | tf_op jit(solution)/shard_map/pallas_call | solution.py:104
  118.1 18.3 %all_to_all.5 = f16[16,40,512]{2,1,0:T(8,128)(2,1)S(1)} all-to-all(f16[16,40,512]{2,1,0:T(8,128)(2,1)S(1)} %bitcast.14), channel_id=1, replica_groups=mesh['img'=16,'own'=8] {'img'}, dimensions={0} | all-to-all | bytes 1310720 | tf_op jit(solution)/shard_map/all_to_all | solution.py:252
  136.7 0.6 broadcast_multiply_fusion
  (73 shorter events, 5.2 us)
Async XLA Ops:
  6.5 83.9 %all-gather.2.cloned.1.call-start = ((), (), s32[]{:S(2)}) async-start(), calls=%async_computation.1 | async-start | bytes 6266880 | tf_op jit(solution)/shard_map/all_gather | solution.py:217
  10.7 9.6 %collective-permute-start = (bf16[2,144,288]{2,1,0:T(8,128)(2,1)S(1)}, bf16[2,144,288]{2,1,0:T(8,128)(2,1)S(1)}, u32[]{:S(2)}, u32[]{:S(2)}) collective-permute-start(bf16[2,144,288]{2,1,0:T(8,128)(2,1)S(1)} %get-tuple-element.37), channel_id=1, source_target_pairs={{0,2},{1,3},{2,4},{3,5},{4,6},{5,7},{6,0},{7,1},{8,10},{9,11},{10,... | collective-permute-start | bytes 497672 | tf_op jit(solution)/shard_map/ppermute | solution.py:200
  12.8 13.5 %collective-permute-start.1 = (bf16[2,144,288]{2,1,0:T(8,128)(2,1)S(1)}, bf16[2,144,288]{2,1,0:T(8,128)(2,1)S(1)}, u32[]{:S(2)}, u32[]{:S(2)}) collective-permute-start(bf16[2,144,288]{2,1,0:T(8,128)(2,1)S(1)} %get-tuple-element.38), channel_id=1, source_target_pairs={{0,4},{1,5},{2,6},{3,7},{4,0},{5,1},{6,2},{7,3},{8,12},{9,13},{10,... | collective-permute-start | bytes 497672 | tf_op jit(solution)/shard_map/ppermute | solution.py:200
  16.4 10.0 %collective-permute-start.2 = (bf16[2,144,288]{2,1,0:T(8,128)(2,1)S(1)}, bf16[2,144,288]{2,1,0:T(8,128)(2,1)S(1)}, u32[]{:S(2)}, u32[]{:S(2)}) collective-permute-start(bf16[2,144,288]{2,1,0:T(8,128)(2,1)S(1)} %get-tuple-element.39), channel_id=1, source_target_pairs={{0,6},{1,7},{2,0},{3,1},{4,2},{5,3},{6,4},{7,5},{8,14},{9,15},{10,... | collective-permute-start | bytes 497672 | tf_op jit(solution)/shard_map/ppermute | solution.py:200
  17.4 9.8 %collective-permute-start.3 = (bf16[144,288]{1,0:T(8,128)(2,1)S(1)}, bf16[144,288]{1,0:T(8,128)(2,1)S(1)}, u32[]{:S(2)}, u32[]{:S(2)}) collective-permute-start(bf16[144,288]{1,0:T(8,128)(2,1)S(1)} %slice_bitcast_fusion.3), channel_id=1, source_target_pairs={{0,1},{1,0},{2,3},{3,2},{4,5},{5,4},{6,7},{7,6},{8,9},{9,8},{10,11... | collective-permute-start | bytes 248840 | tf_op jit(solution)/shard_map/ppermute | solution.py:204
  20.3 6.8 %collective-permute-start.4 = (bf16[144,288]{1,0:T(8,128)(2,1)S(1)}, bf16[144,288]{1,0:T(8,128)(2,1)S(1)}, u32[]{:S(2)}, u32[]{:S(2)}) collective-permute-start(bf16[144,288]{1,0:T(8,128)(2,1)S(1)} %slice_bitcast_fusion.2), channel_id=1, source_target_pairs={{0,1},{1,0},{2,3},{3,2},{4,5},{5,4},{6,7},{7,6},{8,9},{9,8},{10,11... | collective-permute-start | bytes 248840 | tf_op jit(solution)/shard_map/ppermute | solution.py:204
  26.3 1.4 collective-permute-start.5
  26.4 1.5 %collective-permute-start.6 = (bf16[144,288]{1,0:T(8,128)(2,1)S(1)}, bf16[144,288]{1,0:T(8,128)(2,1)S(1)}, u32[]{:S(2)}, u32[]{:S(2)}) collective-permute-start(bf16[144,288]{1,0:T(8,128)(2,1)S(1)} %slice_bitcast_fusion), channel_id=1, source_target_pairs={{0,1},{1,0},{2,3},{3,2},{4,5},{5,4},{6,7},{7,6},{8,9},{9,8},{10,11... | collective-permute-start | bytes 248840 | tf_op jit(solution)/shard_map/ppermute | solution.py:204
  27.1 55.6 %copy-start.6 = (bf16[196,2560]{1,0:T(8,128)(2,1)}, bf16[196,2560]{1,0:T(8,128)(2,1)S(1)}, u32[]{:S(2)}) copy-start(bf16[196,2560]{1,0:T(8,128)(2,1)S(1)} %slice.28.refs_0_) | copy-start | bytes 3010564
  30.5 3.7 %collective-permute-start.10 = (bf16[196,2560]{1,0:T(8,128)(2,1)S(1)}, bf16[196,2560]{1,0:T(8,128)(2,1)S(1)}, u32[]{:S(2)}, u32[]{:S(2)}) collective-permute-start(bf16[196,2560]{1,0:T(8,128)(2,1)S(1)} %pad_maximum_fusion.refs_6_), channel_id=1, source_target_pairs={{0,1},{1,0},{2,3},{3,2},{4,5},{5,4},{6,7},{7,6},{8,9},{9,8},{10,11... | collective-permute-start | bytes 3010568 | tf_op jit(solution)/shard_map/ppermute | solution.py:204
  31.0 26.0 %collective-permute-start.7 = (bf16[196,2560]{1,0:T(8,128)(2,1)S(1)}, bf16[196,2560]{1,0:T(8,128)(2,1)}, u32[]{:S(2)}, u32[]{:S(2)}) collective-permute-start(bf16[196,2560]{1,0:T(8,128)(2,1)S(1)} %slice.28.refs_0_), channel_id=1, source_target_pairs={{0,2},{1,3},{2,4},{3,5},{4,6},{5,7},{6,0},{7,1},{8,10},{9,11},{10,... | collective-permute-start | bytes 3010568 | tf_op jit(solution)/shard_map/ppermute | solution.py:200
  31.8 25.2 %collective-permute-start.8 = (bf16[196,2560]{1,0:T(8,128)(2,1)S(1)}, bf16[196,2560]{1,0:T(8,128)(2,1)}, u32[]{:S(2)}, u32[]{:S(2)}) collective-permute-start(bf16[196,2560]{1,0:T(8,128)(2,1)S(1)} %pad_maximum_fusion.refs_6_), channel_id=1, source_target_pairs={{0,6},{1,7},{2,0},{3,1},{4,2},{5,3},{6,4},{7,5},{8,14},{9,15},{10,... | collective-permute-start | bytes 3010568 | tf_op jit(solution)/shard_map/ppermute | solution.py:200
  34.2 22.8 %collective-permute-start.9 = (bf16[196,2560]{1,0:T(8,128)(2,1)S(1)}, bf16[196,2560]{1,0:T(8,128)(2,1)S(1)}, u32[]{:S(2)}, u32[]{:S(2)}) collective-permute-start(bf16[196,2560]{1,0:T(8,128)(2,1)S(1)} %slice.28.refs_0_), channel_id=1, source_target_pairs={{0,1},{1,0},{2,3},{3,2},{4,5},{5,4},{6,7},{7,6},{8,9},{9,8},{10,11... | collective-permute-start | bytes 3010568 | tf_op jit(solution)/shard_map/ppermute | solution.py:204
  34.2 49.4 %copy-start.8 = (bf16[196,2560]{1,0:T(8,128)(2,1)}, bf16[196,2560]{1,0:T(8,128)(2,1)S(1)}, u32[]{:S(2)}) copy-start(bf16[196,2560]{1,0:T(8,128)(2,1)S(1)} %collective-permute-done.10.refs_7_) | copy-start | bytes 3010564
  57.0 25.1 %collective-permute-start.11 = (bf16[196,2560]{1,0:T(8,128)(2,1)S(1)}, bf16[196,2560]{1,0:T(8,128)(2,1)S(1)}, u32[]{:S(2)}, u32[]{:S(2)}) collective-permute-start(bf16[196,2560]{1,0:T(8,128)(2,1)S(1)} %pad_maximum_fusion.refs_6_), channel_id=1, source_target_pairs={{0,2},{1,3},{2,4},{3,5},{4,6},{5,7},{6,0},{7,1},{8,10},{9,11},{10,... | collective-permute-start | bytes 3010568 | tf_op jit(solution)/shard_map/ppermute | solution.py:200
  57.5 24.6 %collective-permute-start.12 = (bf16[196,2560]{1,0:T(8,128)(2,1)S(1)}, bf16[196,2560]{1,0:T(8,128)(2,1)S(1)}, u32[]{:S(2)}, u32[]{:S(2)}) collective-permute-start(bf16[196,2560]{1,0:T(8,128)(2,1)S(1)} %slice.28.refs_0_), channel_id=1, source_target_pairs={{0,6},{1,7},{2,0},{3,1},{4,2},{5,3},{6,4},{7,5},{8,14},{9,15},{10,... | collective-permute-start | bytes 3010568 | tf_op jit(solution)/shard_map/ppermute | solution.py:200
  60.3 21.8 %collective-permute-start.13 = (bf16[196,2560]{1,0:T(8,128)(2,1)}, bf16[196,2560]{1,0:T(8,128)(2,1)S(1)}, u32[]{:S(2)}, u32[]{:S(2)}) collective-permute-start(bf16[196,2560]{1,0:T(8,128)(2,1)} %collective-permute-done.7.refs_2_), channel_id=1, source_target_pairs={{0,1},{1,0},{2,3},{3,2},{4,5},{5,4},{6,7},{7,6},{8,9},{9,8},{10,11... | collective-permute-start | bytes 3010568 | tf_op jit(solution)/shard_map/ppermute | solution.py:204
  60.3 21.9 %collective-permute-start.14 = (bf16[196,2560]{1,0:T(8,128)(2,1)}, bf16[196,2560]{1,0:T(8,128)(2,1)S(1)}, u32[]{:S(2)}, u32[]{:S(2)}) collective-permute-start(bf16[196,2560]{1,0:T(8,128)(2,1)} %collective-permute-done.8.refs_10_), channel_id=1, source_target_pairs={{0,1},{1,0},{2,3},{3,2},{4,5},{5,4},{6,7},{7,6},{8,9},{9,8},{10,11... | collective-permute-start | bytes 3010568 | tf_op jit(solution)/shard_map/ppermute | solution.py:204
  82.2 3.8 %collective-permute-start.17 = (bf16[196,2560]{1,0:T(8,128)(2,1)S(1)}, bf16[196,2560]{1,0:T(8,128)(2,1)S(1)}, u32[]{:S(2)}, u32[]{:S(2)}) collective-permute-start(bf16[196,2560]{1,0:T(8,128)(2,1)S(1)} %collective-permute-done.12.refs_4_), channel_id=1, source_target_pairs={{0,1},{1,0},{2,3},{3,2},{4,5},{5,4},{6,7},{7,6},{8,9},{9,8},{10,11... | collective-permute-start | bytes 3010568 | tf_op jit(solution)/shard_map/ppermute | solution.py:204
  82.3 4.8 %collective-permute-start.18 = (bf16[196,2560]{1,0:T(8,128)(2,1)S(1)}, bf16[196,2560]{1,0:T(8,128)(2,1)}, u32[]{:S(2)}, u32[]{:S(2)}) collective-permute-start(bf16[196,2560]{1,0:T(8,128)(2,1)S(1)} %collective-permute-done.11.refs_8_), channel_id=1, source_target_pairs={{0,1},{1,0},{2,3},{3,2},{4,5},{5,4},{6,7},{7,6},{8,9},{9,8},{10,11... | collective-permute-start | bytes 3010568 | tf_op jit(solution)/shard_map/ppermute | solution.py:204
  82.8 28.2 %collective-permute-start.15 = (bf16[196,2560]{1,0:T(8,128)(2,1)}, bf16[196,2560]{1,0:T(8,128)(2,1)S(1)}, u32[]{:S(2)}, u32[]{:S(2)}) collective-permute-start(bf16[196,2560]{1,0:T(8,128)(2,1)} %collective-permute-done.7.refs_2_), channel_id=1, source_target_pairs={{0,2},{1,3},{2,4},{3,5},{4,6},{5,7},{6,0},{7,1},{8,10},{9,11},{10,... | collective-permute-start | bytes 3010568 | tf_op jit(solution)/shard_map/ppermute | solution.py:200
  83.6 27.4 %collective-permute-start.16 = (bf16[196,2560]{1,0:T(8,128)(2,1)}, bf16[196,2560]{1,0:T(8,128)(2,1)S(1)}, u32[]{:S(2)}, u32[]{:S(2)}) collective-permute-start(bf16[196,2560]{1,0:T(8,128)(2,1)} %collective-permute-done.8.refs_10_), channel_id=1, source_target_pairs={{0,6},{1,7},{2,0},{3,1},{4,2},{5,3},{6,4},{7,5},{8,14},{9,15},{10,... | collective-permute-start | bytes 3010568 | tf_op jit(solution)/shard_map/ppermute | solution.py:200
  111.0 3.0 %collective-permute-start.19 = (bf16[196,2560]{1,0:T(8,128)(2,1)S(1)}, bf16[196,2560]{1,0:T(8,128)(2,1)S(1)}, u32[]{:S(2)}, u32[]{:S(2)}) collective-permute-start(bf16[196,2560]{1,0:T(8,128)(2,1)S(1)} %collective-permute-done.15.refs_0_), channel_id=1, source_target_pairs={{0,1},{1,0},{2,3},{3,2},{4,5},{5,4},{6,7},{7,6},{8,9},{9,8},{10,11... | collective-permute-start | bytes 3010568 | tf_op jit(solution)/shard_map/ppermute | solution.py:204
  111.1 4.1 %collective-permute-start.20 = (bf16[196,2560]{1,0:T(8,128)(2,1)S(1)}, bf16[196,2560]{1,0:T(8,128)(2,1)S(1)}, u32[]{:S(2)}, u32[]{:S(2)}) collective-permute-start(bf16[196,2560]{1,0:T(8,128)(2,1)S(1)} %collective-permute-done.16.refs_1_), channel_id=1, source_target_pairs={{0,1},{1,0},{2,3},{3,2},{4,5},{5,4},{6,7},{7,6},{8,9},{9,8},{10,11... | collective-permute-start | bytes 3010568 | tf_op jit(solution)/shard_map/ppermute | solution.py:204
  (14 other events, 147.3 us)
Sparse Core Ops, SparseCore 0:
  30.6 59.7 all-gather.1
